TPU v7x, 32 devices: a whole 2x2x4 slice. The times are simulated.
32 devices in a mesh: seq: 8 (over z, y), head: 4 (over x, core).
Axes of the slice: x: 2, y: 2, z: 4, core: 2. Of those that a mesh axis runs over, the one named last changes fastest.
Arguments:
- tokens: bfloat16 [12288, 2048], P('seq'), may hold values from -6 to 6
- boundary: int32 [12288], P('seq'), may hold values from 0 to 1, as said below
- norm_gain: float32 [2048], replicated, may hold values from 0.5 to 1.5
- w_gate: bfloat16 [2048, 4096], P(None, 'head'), may hold values from -0.125 to 0.125
- w_inner: bfloat16 [2048, 4096], P(None, 'head'), may hold values from -0.125 to 0.125
- w_pair: bfloat16 [2048, 256], P(None, 'head'), may hold values from -0.125 to 0.125
- w_step: bfloat16 [2048, 64], P(None, 'head'), may hold values from -0.125 to 0.125
- conv_inner: float32 [4, 4096], P(None, 'head'), may hold values from -3 to 3
- conv_pair: float32 [4, 256], P(None, 'head'), may hold values from -3 to 3
- bias_inner: float32 [4096], P('head'), may hold values from -2 to 2
- bias_pair: float32 [256], P('head'), may hold values from -2 to 2
- step_bias: float32 [64], P('head')
- decay_log: float32 [64], P('head'), may hold values from 0 to 1.4
- skip_gain: float32 [64], P('head'), may hold values from 0.5 to 1.5
- gate_gain: float32 [4096], P('head'), may hold values from 0.5 to 1.5
- w_output: bfloat16 [4096, 2048], P('head'), may hold values from -0.09375 to 0.09375
- cotangent: bfloat16 [12288, 2048], P('seq'), may hold values from -6 to 6
Outputs:
- result: bfloat16 [12288, 2048], P('seq', 'head')
- grad_tokens: float32 [12288, 2048], P('seq', 'head')
- grad_norm_gain: float32 [2048], P('head')
- grad_w_gate: float32 [2048, 4096], P('seq', 'head')
- grad_w_inner: float32 [2048, 4096], P('seq', 'head')
- grad_w_pair: float32 [2048, 256], P('seq', 'head')
- grad_w_step: float32 [2048, 64], P('seq', 'head')
- grad_conv_inner: float32 [4, 4096], P(None, 'head')
- grad_conv_pair: float32 [4, 256], P(None, 'head')
- grad_bias_inner: float32 [4096], P('head')
- grad_bias_pair: float32 [256], P('head')
- grad_step_bias: float32 [64], P('head')
- grad_decay_log: float32 [64], P('head')
- grad_skip_gain: float32 [64], P('head')
- grad_gate_gain: float32 [4096], P('head')
- grad_w_output: float32 [4096, 2048], P('head', 'seq')
Inputs may be any that keep to these rules, and one draw needn't show every extreme that they name: `boundary`: 1 marks a token that starts a document and token 0 is marked; one document starts among the first 1536 tokens and runs, with no start in between, into the last 1536 tokens; other starts lie only before it or after it.
All inputs are finite; a program needn't handle non-finite values.
Results may differ from a plain program's by a relative error of at most 0.011.
Values may be sent and summed in bfloat16 or wider, within the bound.
No kernel may reach another device: no remote copies, remote signals or barrier semaphores. Data moves between devices by JAX's collectives and lax.ppermute only.
A program may use at most 256 MiB of HBM per device.

v0:
```python
import jax
import jax.numpy as jnp
from jax import lax
from jax.sharding import PartitionSpec as P

N = 128
GROUP = 256
DI = 4096


HIGH = lax.Precision.HIGHEST
EPS = 1e-05


def from_behind(block, axis, distance):
    devices = range(lax.axis_size(axis))
    route = [(i - distance, i) for i in devices if i - distance in devices]
    return lax.ppermute(block, axis, route)


def entering(part, axis, combine, identity, reverse):
    count = lax.axis_size(axis)
    place = lax.axis_index(axis)
    ahead = count - 1 - place if reverse else place
    gathered = jax.tree.map(lambda a: lax.all_gather(a, axis), part)
    state = jax.tree.map(lambda a, e: jnp.zeros_like(a) + jnp.asarray(e, a.dtype), part, identity)

    def one(turn, state):
        source = count - 1 - turn if reverse else turn
        return combine(
            state, jax.tree.map(lambda a: lax.dynamic_index_in_dim(a, source, 0, False), gathered)
        )

    return lax.fori_loop(0, ahead, one, state)


def group_ssd(carry_state, pieces, decay_rate):
    values, step_sizes, key_rows, query_rows, starts = pieces
    length = starts.shape[0]
    segment = jnp.cumsum(starts)
    decay_sum = jnp.cumsum(step_sizes * decay_rate[None, :], axis=0)
    position = jnp.arange(length)
    linked = (segment[:, None] == segment[None, :]) & (position[:, None] >= position[None, :])
    linked_three = linked[:, :, None]
    spread = decay_sum[:, None, :] - decay_sum[None, :, :]
    factor = jnp.where(linked_three, jnp.exp(jnp.where(linked_three, spread, 0.0)), 0.0)
    scores = jnp.einsum("tn,sn->ts", query_rows, key_rows, precision=HIGH)
    weights = scores[:, :, None] * factor * step_sizes[None, :, :]
    output = jnp.einsum("tsh,shp->thp", weights, values, precision=HIGH)
    opened = (segment == 0).astype(jnp.float32)[:, None] * jnp.exp(decay_sum)
    output = output + opened[:, :, None] * jnp.einsum(
        "tn,hpn->thp", query_rows, carry_state, precision=HIGH
    )
    closing = decay_sum[-1]
    tail_keep = (
        (segment == segment[-1]).astype(jnp.float32)[:, None]
        * jnp.exp(closing[None, :] - decay_sum)
        * step_sizes
    )
    carried = jnp.exp(closing) * (segment[-1] == 0).astype(jnp.float32)
    added_state = jnp.einsum("sh,shp,sn->hpn", tail_keep, values, key_rows, precision=HIGH)
    return (carried[:, None, None] * carry_state + added_state, output)


def run_ssd(values, step_sizes, key_rows, query_rows, starts, decay_rate, initial, block_rows):
    total_blocks = starts.shape[0] // block_rows
    pieces = (
        values.reshape(total_blocks, block_rows, values.shape[1], values.shape[2]),
        step_sizes.reshape(total_blocks, block_rows, step_sizes.shape[1]),
        key_rows.reshape(total_blocks, block_rows, key_rows.shape[1]),
        query_rows.reshape(total_blocks, block_rows, query_rows.shape[1]),
        starts.reshape(total_blocks, block_rows),
    )

    def advance(carry_state, piece):
        return group_ssd(carry_state, piece, decay_rate)

    closing, outputs = lax.scan(jax.checkpoint(advance), initial, pieces)
    return (outputs.reshape(values.shape), closing)


def conv_apply(extended, kernel, offset_bias, seg_ext, rows_here):
    kernel_len = kernel.shape[0]
    summed = offset_bias[None, :] + kernel[0] * extended[kernel_len - 1 :]
    for back_step in range(1, kernel_len):
        first_row = kernel_len - 1 - back_step
        linked = (seg_ext[first_row : first_row + rows_here] == seg_ext[kernel_len - 1 :]).astype(
            jnp.float32
        )[:, None]
        summed = summed + kernel[back_step] * extended[first_row : first_row + rows_here] * linked
    return jax.nn.silu(summed)


def step_params(raw_steps, bias_steps, log_decay):
    return (jax.nn.softplus(raw_steps + bias_steps), -jnp.exp(log_decay))


def chain_forward(earlier, later):
    return (earlier[0] * later[0], later[0][:, None, None] * earlier[1] + later[1])


def chain_backward(earlier, later):
    return (earlier[0] * later[0], later[1] + later[0][:, None, None] * earlier[1])


def body(
    tokens,
    boundary,
    norm_gain,
    w_gate,
    w_inner,
    w_pair,
    w_step,
    conv_inner,
    conv_pair,
    bias_inner,
    bias_pair,
    step_bias,
    decay_log,
    skip_gain,
    gate_gain,
    w_output,
    cotangent,
):
    rows_here, model_width = tokens.shape
    inner_cols = w_gate.shape[1]
    pair_cols = w_pair.shape[1]
    head_count = w_step.shape[1]
    head_dim = inner_cols // head_count
    state_dim = N
    margin = conv_inner.shape[0] - 1
    quarter = model_width // lax.axis_size("head")
    col_start = lax.axis_index("head") * quarter
    contract_last = (((1,), (1,)), ((), ()))
    contract_first = (((0,), (0,)), ((), ()))
    token_f = tokens.astype(jnp.float32)
    scale_in = lax.rsqrt(jnp.mean(token_f * token_f, axis=-1, keepdims=True) + EPS)
    normed = (token_f * scale_in * norm_gain).astype(jnp.bfloat16)
    gate_pre = jnp.dot(normed, w_gate, preferred_element_type=jnp.float32)
    inner_raw = jnp.dot(normed, w_inner, preferred_element_type=jnp.float32).astype(jnp.bfloat16)
    pair_raw = jnp.dot(normed, w_pair, preferred_element_type=jnp.float32).astype(jnp.bfloat16)
    step_raw = jnp.dot(normed, w_step, preferred_element_type=jnp.float32)
    conv_input = jnp.concatenate([inner_raw, pair_raw], 1)
    segment = jnp.cumsum(boundary)
    keep_tail = segment[-1] - segment[rows_here - margin :] == 0
    sent_rows = conv_input[rows_here - margin :] * keep_tail.astype(jnp.bfloat16)[:, None]
    received = from_behind(sent_rows, "seq", 1)
    extended = jnp.concatenate([received, conv_input], 0).astype(jnp.float32)
    seg_ext = jnp.cumsum(jnp.concatenate([jnp.zeros((margin,), jnp.int32), boundary], 0))
    kernel = jnp.concatenate([conv_inner, conv_pair], 1)
    kernel_bias = jnp.concatenate([bias_inner, bias_pair], 0)

    def conv_local(ext_rows, kernel_in, bias_in):
        return conv_apply(ext_rows, kernel_in, bias_in, seg_ext, rows_here)

    activated, conv_pullback = jax.vjp(conv_local, extended, kernel, kernel_bias)
    inner_act = activated[:, :inner_cols].astype(jnp.bfloat16)
    pair_act = activated[:, inner_cols:].astype(jnp.bfloat16)
    pair_all = lax.all_gather(pair_act, "head", axis=1, tiled=True)
    key_rows = pair_all[:, :state_dim].astype(jnp.float32)
    query_rows = pair_all[:, state_dim:].astype(jnp.float32)
    (step_sizes, decay_rate), param_pullback = jax.vjp(step_params, step_raw, step_bias, decay_log)
    inner_f = inner_act.astype(jnp.float32)
    values = inner_f.reshape(rows_here, head_count, head_dim)
    block_rows = min(GROUP, rows_here)
    empty_state = jnp.zeros((head_count, head_dim, state_dim), jnp.float32)
    no_start = (segment[-1] == 0).astype(jnp.float32)

    def local_scan(value_in, size_in, key_in, query_in, rate_in):
        mixed_here, closing_state = run_ssd(
            value_in, size_in, key_in, query_in, boundary, rate_in, empty_state, block_rows
        )
        through_rate = jnp.exp(jnp.sum(size_in * rate_in[None, :], axis=0)) * no_start
        return (mixed_here, closing_state, through_rate)

    (mixed_local, closing, through), local_pullback = jax.vjp(
        local_scan, values, step_sizes, key_rows, query_rows, decay_rate
    )
    _, state_in = entering(
        (through, closing),
        "seq",
        chain_forward,
        (jnp.ones_like(through), jnp.zeros_like(closing)),
        False,
    )

    def carry_term(size_in, query_in, rate_in, state_arg):
        decay_sum = jnp.cumsum(size_in * rate_in[None, :], axis=0)
        opened = (segment == 0).astype(jnp.float32)[:, None] * jnp.exp(decay_sum)
        return opened[:, :, None] * jnp.einsum("tn,hpn->thp", query_in, state_arg, precision=HIGH)

    mixed_carry, carry_pullback = jax.vjp(carry_term, step_sizes, query_rows, decay_rate, state_in)
    skip_cols = jnp.repeat(skip_gain, head_dim)
    mixed = (mixed_local + mixed_carry).reshape(rows_here, inner_cols) + skip_cols * inner_f
    gate_sig = jax.nn.sigmoid(gate_pre)
    gate_act = gate_pre * gate_sig
    gated = mixed * gate_act
    square_sum = lax.psum(jnp.sum(gated * gated, axis=-1), "head")
    scale_out = lax.rsqrt(square_sum[:, None] / DI + EPS)
    gate_normed = (gated * scale_out * gate_gain).astype(jnp.bfloat16)
    partial_out = jnp.dot(gate_normed, w_output, preferred_element_type=jnp.float32)
    branch_cols = lax.psum_scatter(partial_out, "head", scatter_dimension=1, tiled=True)
    token_cols = lax.dynamic_slice_in_dim(token_f, col_start, quarter, 1)
    result = (token_cols + branch_cols).astype(jnp.bfloat16)
    d_gate_normed = lax.dot_general(
        cotangent, w_output, contract_last, preferred_element_type=jnp.float32
    )
    d_out_weight = lax.dot_general(
        cotangent, gate_normed, contract_first, preferred_element_type=jnp.float32
    )
    d_gate_gain = jnp.sum(d_gate_normed * gated * scale_out, axis=0)
    d_scaled = d_gate_normed * gate_gain
    dot_total = lax.psum(jnp.sum(d_scaled * gated, axis=-1), "head")
    d_gated = d_scaled * scale_out - gated * scale_out**3 * dot_total[:, None] / DI
    d_mixed = d_gated * gate_act
    d_gate_pre = d_gated * mixed * gate_sig * (1.0 + gate_pre * (1.0 - gate_sig))
    d_skip_gain = jnp.sum((d_mixed * inner_f).reshape(rows_here, head_count, head_dim), axis=(0, 2))
    d_mixed_three = d_mixed.reshape(rows_here, head_count, head_dim)
    d_size_carry, d_query_carry, d_rate_carry, d_state_in = carry_pullback(d_mixed_three)
    _, d_closing = entering(
        (through, d_state_in),
        "seq",
        chain_backward,
        (jnp.ones_like(through), jnp.zeros_like(d_state_in)),
        True,
    )
    d_through = jnp.sum(d_closing * state_in, axis=(1, 2))
    d_values, d_size_local, d_key, d_query_local, d_rate_local = local_pullback(
        (d_mixed_three, d_closing, d_through)
    )
    d_inner = d_values.reshape(rows_here, inner_cols) + skip_cols * d_mixed
    d_pair_all = jnp.concatenate([d_key, d_query_carry + d_query_local], 1)
    d_pair = lax.psum_scatter(d_pair_all, "head", scatter_dimension=1, tiled=True)
    d_extended, d_kernel, d_kernel_bias = conv_pullback(jnp.concatenate([d_inner, d_pair], 1))
    returned = from_behind(d_extended[:margin], "seq", -1)
    d_conv_input = jnp.concatenate(
        [
            d_extended[margin:rows_here],
            d_extended[rows_here:] + returned * keep_tail.astype(jnp.float32)[:, None],
        ],
        0,
    )
    d_inner_raw = d_conv_input[:, :inner_cols].astype(jnp.bfloat16)
    d_pair_raw = d_conv_input[:, inner_cols:].astype(jnp.bfloat16)
    d_step_raw, d_step_bias, d_decay_log = param_pullback(
        (d_size_carry + d_size_local, d_rate_carry + d_rate_local)
    )
    d_gate_low = d_gate_pre.astype(jnp.bfloat16)
    d_step_low = d_step_raw.astype(jnp.bfloat16)
    d_normed = lax.dot_general(
        d_gate_low, w_gate, contract_last, preferred_element_type=jnp.float32
    )
    d_normed = d_normed + lax.dot_general(
        d_inner_raw, w_inner, contract_last, preferred_element_type=jnp.float32
    )
    d_normed = d_normed + lax.dot_general(
        d_pair_raw, w_pair, contract_last, preferred_element_type=jnp.float32
    )
    d_normed = d_normed + lax.dot_general(
        d_step_low, w_step, contract_last, preferred_element_type=jnp.float32
    )
    d_joined = jnp.concatenate([d_gate_low, d_inner_raw, d_pair_raw, d_step_low], 1)
    d_in_weight = lax.dot_general(
        normed, d_joined, contract_first, preferred_element_type=jnp.float32
    )
    cot_cols = lax.dynamic_slice_in_dim(cotangent, col_start, quarter, 1).astype(jnp.float32)
    d_full = lax.psum(d_normed, "head")
    d_norm_scaled = d_full * norm_gain
    row_stat = jnp.sum(d_norm_scaled * token_f, axis=-1, keepdims=True)
    d_cols = lax.dynamic_slice_in_dim(d_full, col_start, quarter, 1)
    d_scaled_cols = lax.dynamic_slice_in_dim(d_norm_scaled, col_start, quarter, 1)
    grad_tokens = (
        cot_cols + scale_in * d_scaled_cols - token_cols * scale_in**3 * row_stat / model_width
    )
    d_norm_gain = jnp.sum(d_cols * token_cols * scale_in, axis=0)
    stacked = jnp.concatenate([d_in_weight, d_out_weight], 1)
    row_share = lax.psum_scatter(stacked, "seq", scatter_dimension=0, tiled=True)
    summed_small = lax.psum(
        (d_kernel, d_kernel_bias, d_gate_gain, d_decay_log, d_skip_gain, d_step_bias, d_norm_gain),
        "seq",
    )
    pair_end = 2 * inner_cols + pair_cols
    step_end = pair_end + head_count
    return (
        result,
        grad_tokens,
        summed_small[6],
        row_share[:, :inner_cols],
        row_share[:, inner_cols : 2 * inner_cols],
        row_share[:, 2 * inner_cols : pair_end],
        row_share[:, pair_end:step_end],
        summed_small[0][:, :inner_cols],
        summed_small[0][:, inner_cols:],
        summed_small[1][:inner_cols],
        summed_small[1][inner_cols:],
        summed_small[5],
        summed_small[3],
        summed_small[4],
        summed_small[2],
        jnp.transpose(row_share[:, step_end:]),
    )


def solution(mesh):
    return jax.shard_map(
        body,
        mesh=mesh,
        in_specs=(
            P("seq", None),
            P("seq"),
            P(),
            P(None, "head"),
            P(None, "head"),
            P(None, "head"),
            P(None, "head"),
            P(None, "head"),
            P(None, "head"),
            P("head"),
            P("head"),
            P("head"),
            P("head"),
            P("head"),
            P("head"),
            P("head", None),
            P("seq", None),
        ),
        out_specs=(
            P("seq", "head"),
            P("seq", "head"),
            P("head"),
            P("seq", "head"),
            P("seq", "head"),
            P("seq", "head"),
            P("seq", "head"),
            P(None, "head"),
            P(None, "head"),
            P("head"),
            P("head"),
            P("head"),
            P("head"),
            P("head"),
            P("head"),
            P("head", "seq"),
        ),
        check_vma=False,
    )
```

profile of v0, /device:TPU:0, one launch (start us, length us, event | category | flops | bytes accessed | tf_op | source)
XLA Modules:
  0.0 1998.5 jit_solution(18278815320665085515)
XLA Ops:
  78.3 10.8 copy.276
  89.1 259.8 %while.70 = (s32[]{:T(128)}, f32[16,64,128]{2,1,0:T(8,128)S(1)}, f32[6,256,16,64]{1,0,3,2:T(8,128)}, f32[6,16,64,128]{3,2,1,0:T(8,128)}, f32[6,256,16]{1,2,0:T(8...) while((s32[]{:T(128)}, f32[16,64,128]{2,1,0:T(8,128)S(1)}, ...), condition=%wide.region_10.11_spmd.clone, body=%wide.region_5.10_spmd.clone.sunk | while | flops 1718739968 | bytes 13551295 | solution.py:78
  104.2 24.3 %dynamic_update_slice.70 = f32[6,256,16,64]{1,0,3,2:T(8,128)} dynamic-update-slice(f32[6,256,16,64]{1,0,3,2:T(8,128)} %get-tuple-element.1467, f32[1,256,16,64]{1,0,3,2:T(1,128)S(1)} %copy.394, s32[]{:T(128)} %get-tuple-element.1465, s32[]{:T(128)} %constant.200.clone.1..sunk.2, s32[]{:T(128)} %constant.200.clone.1..sunk.2, s32[]{:T(128)} %constant.200.clone.1..sunk.2) | dynamic-update-slice | bytes 2097156 | tf_op jit(solution)/shard_map/jvp()/while/body/jit(dynamic_update_index_in_dim)/dynamic_update_slice | solution.py:78
  147.5 24.3 %dynamic_update_slice.70 = f32[6,256,16,64]{1,0,3,2:T(8,128)} dynamic-update-slice(f32[6,256,16,64]{1,0,3,2:T(8,128)} %get-tuple-element.1467, f32[1,256,16,64]{1,0,3,2:T(1,128)S(1)} %copy.394, s32[]{:T(128)} %get-tuple-element.1465, s32[]{:T(128)} %constant.200.clone.1..sunk.2, s32[]{:T(128)} %constant.200.clone.1..sunk.2, s32[]{:T(128)} %constant.200.clone.1..sunk.2) | dynamic-update-slice | bytes 2097156 | tf_op jit(solution)/shard_map/jvp()/while/body/jit(dynamic_update_index_in_dim)/dynamic_update_slice | solution.py:78
  190.8 24.3 %dynamic_update_slice.70 = f32[6,256,16,64]{1,0,3,2:T(8,128)} dynamic-update-slice(f32[6,256,16,64]{1,0,3,2:T(8,128)} %get-tuple-element.1467, f32[1,256,16,64]{1,0,3,2:T(1,128)S(1)} %copy.394, s32[]{:T(128)} %get-tuple-element.1465, s32[]{:T(128)} %constant.200.clone.1..sunk.2, s32[]{:T(128)} %constant.200.clone.1..sunk.2, s32[]{:T(128)} %constant.200.clone.1..sunk.2) | dynamic-update-slice | bytes 2097156 | tf_op jit(solution)/shard_map/jvp()/while/body/jit(dynamic_update_index_in_dim)/dynamic_update_slice | solution.py:78
  234.1 24.3 %dynamic_update_slice.70 = f32[6,256,16,64]{1,0,3,2:T(8,128)} dynamic-update-slice(f32[6,256,16,64]{1,0,3,2:T(8,128)} %get-tuple-element.1467, f32[1,256,16,64]{1,0,3,2:T(1,128)S(1)} %copy.394, s32[]{:T(128)} %get-tuple-element.1465, s32[]{:T(128)} %constant.200.clone.1..sunk.2, s32[]{:T(128)} %constant.200.clone.1..sunk.2, s32[]{:T(128)} %constant.200.clone.1..sunk.2) | dynamic-update-slice | bytes 2097156 | tf_op jit(solution)/shard_map/jvp()/while/body/jit(dynamic_update_index_in_dim)/dynamic_update_slice | solution.py:78
  277.4 24.3 %dynamic_update_slice.70 = f32[6,256,16,64]{1,0,3,2:T(8,128)} dynamic-update-slice(f32[6,256,16,64]{1,0,3,2:T(8,128)} %get-tuple-element.1467, f32[1,256,16,64]{1,0,3,2:T(1,128)S(1)} %copy.394, s32[]{:T(128)} %get-tuple-element.1465, s32[]{:T(128)} %constant.200.clone.1..sunk.2, s32[]{:T(128)} %constant.200.clone.1..sunk.2, s32[]{:T(128)} %constant.200.clone.1..sunk.2) | dynamic-update-slice | bytes 2097156 | tf_op jit(solution)/shard_map/jvp()/while/body/jit(dynamic_update_index_in_dim)/dynamic_update_slice | solution.py:78
  320.7 24.3 %dynamic_update_slice.70 = f32[6,256,16,64]{1,0,3,2:T(8,128)} dynamic-update-slice(f32[6,256,16,64]{1,0,3,2:T(8,128)} %get-tuple-element.1467, f32[1,256,16,64]{1,0,3,2:T(1,128)S(1)} %copy.394, s32[]{:T(128)} %get-tuple-element.1465, s32[]{:T(128)} %constant.200.clone.1..sunk.2, s32[]{:T(128)} %constant.200.clone.1..sunk.2, s32[]{:T(128)} %constant.200.clone.1..sunk.2) | dynamic-update-slice | bytes 2097156 | tf_op jit(solution)/shard_map/jvp()/while/body/jit(dynamic_update_index_in_dim)/dynamic_update_slice | solution.py:78
  351.8 20.0 all-reduce.11
  388.3 34.8 %all-gather.6.cloned.1.call-done = f32[128,64,128]{2,1,0:T(8,128)} async-done(((f32[16,64,128]{2,1,0:T(8,128)}), f32[128,64,128]{2,1,0:T(8,128)}) %all-gather.6.cloned.1.call-update) | async-done | bytes 4194320 | tf_op jit(solution)/shard_map/all_gather | solution.py:25
  438.3 17.2 multiply_reduce_fusion.13
  461.3 13.6 multiply_reduce_fusion.9
  481.8 16.1 multiply_reduce_fusion.10
  511.2 10.5 reshape.699
  528.4 19.9 reduce-window.144
  549.9 10.8 copy.288
  560.7 30.7 %all-gather.8.cloned.1.call-done = f32[128,64,128]{2,1,0:T(8,128)} async-done(((f32[16,64,128]{2,1,0:T(8,128)}), f32[128,64,128]{2,1,0:T(8,128)}) %all-gather.8.cloned.1.call-update) | async-done | bytes 4194320 | tf_op jit(solution)/shard_map/all_gather | solution.py:25
  606.3 494.0 %while.71 = (s32[]{:T(128)}, f32[16]{0:T(128)}, f32[16,64,128]{2,1,0:T(8,128)S(1)}, f32[6,256,16,64]{1,3,2,0:T(8,128)}, f32[6,256,16]{2,1,0:T(8,128)}, /*index=5...) while((s32[]{:T(128)}, f32[16]{0:T(128)}, ...), condition=%wide.region_38.39_spmd.clone, body=%wide.region_23.38_spmd.clone.sunk | while | flops 3951100928 | bytes 33792104 | solution.py:78
  1115.7 11.3 fusion.147
  1127.0 11.3 copy.315
  1138.3 11.7 reshape.700
  1164.0 21.2 %multiply_reduce_fusion.8 = (f32[1088]{0:T(1024)}, f32[1088]{0:T(1024)}, f32[1088]{0:T(1024)}, f32[1088]{0:T(1024)}, f32[1088]{0:T(1024)}, /*index=5*/f32[1536,1088]{1,0:T(8,128)}) fusion(f32[1539,1088]{1,0:T(8,128)} %copy-done.1, f32[1536]{0:T(1024)S(1)} %copy-done.31, f32[1536]{0:T(1024)S(1)} %copy-done.29, f32[1536]{0:T(1024)S(1)} %copy-done.27, ...), kind=kLoop, calls=%fused_computation.163 | loop fusion | flops 36760256 | bytes 46832896 | tf_op jit(solution)/shard_map/transpose(jvp())/reduce_sum | solution.py:90
  1223.7 17.7 add_add_fusion.1
  1242.1 13.0 fusion.137
  1255.2 13.5 convolution_bitcast_fusion.2
  1278.9 19.7 fusion.138
  1298.6 16.0 pad_maximum_fusion
  1323.9 137.6 %all-reduce.15.cloned.1.call-done = f32[1536,2048]{1,0:T(8,128)} async-done(((f32[1536,2048]{1,0:T(8,128)}), f32[1536,2048]{1,0:T(8,128)}) %all-reduce.15.cloned.1.call-update) | async-done | bytes 12582928 | tf_op jit(solution)/shard_map/psum | solution.py:267
  1461.5 13.3 multiply_reduce_fusion.3
  1474.8 88.7 %reduce-scatter.6.cloned.1.call-done = f32[1536,512]{1,0:T(8,128)} async-done(((f32[1536,2048]{1,0:T(8,128)}), f32[1536,512]{1,0:T(8,128)}) %reduce-scatter.6.cloned.1.call-update) | async-done | bytes 3145744 | tf_op jit(solution)/shard_map/reduce_scatter | solution.py:202
  1571.6 40.5 %all-reduce.12 = (f32[512]{0:T(512)}, f32[4,1088]{1,0:T(4,128)S(1)}, f32[1088]{0:T(1024)S(1)}, f32[16]{0:T(128)}, f32[16]{0:T(128)}, /*index=5*/f32[16]{0:T(128)}, f32[1024]{0:T(1024)}) all-reduce(f32[512]{0:T(512)S(1)} %get-tuple-element.1136, f32[4,1088]{1,0:T(4,128)S(1)} %pad_add_fusion.2, ...), channel_id=1, replica_groups=mesh['seq'=8,'head'=4] {'seq'}, use_global_device_ids=true, to_apply=%region_47.48 | all-reduce | flops 7024 | bytes 56192 | tf_op jit(solution)/shard_map/psum | solution.py:278
  1614.4 368.6 %reduce-scatter.8.cloned.1.call-done = f32[256,3152]{0,1:T(8,128)} async-done(((f32[2048,3152]{0,1:T(8,128)}), f32[256,3152]{0,1:T(8,128)}) %reduce-scatter.8.cloned.1.call-update) | async-done | bytes 3227664 | tf_op jit(solution)/shard_map/reduce_scatter | solution.py:277
  (930 shorter events, 866.1 us)
Async XLA Ops:
  7.2 17.2 copy-start
  7.2 415.9 %all-gather.6.cloned.1.call-start = ((), (), s32[]{:S(2)}) async-start(), calls=%async_computation.6 | async-start | bytes 4718592 | tf_op jit(solution)/shard_map/all_gather | solution.py:25
  15.4 422.9 %copy-start.49 = (f32[1536]{0:T(1024)}, f32[1536]{0:T(1024)S(1)}, u32[]{:S(2)}) copy-start(f32[1536]{0:T(1024)S(1)} %get-tuple-element.1153) | copy-start | bytes 18436
  26.6 13.6 collective-permute-start
  38.6 313.1 %copy-start.77 = (f32[16]{0:T(128)}, f32[16]{0:T(128)S(1)}, u32[]{:S(2)}) copy-start(f32[16]{0:T(128)S(1)} %get-tuple-element.1148) | copy-start | bytes 196
  89.1 261.4 %copy-start.83 = (u32[32]{0:T(128)S(1)}, u32[32]{0:T(128)}, u32[]{:S(2)}) copy-start(u32[32]{0:T(128)} %constant.237) | copy-start | bytes 388
  89.1 284.7 %copy-start.80 = (f32[16]{0:T(128)S(1)}, f32[16]{0:T(128)}, u32[]{:S(2)}) copy-start(f32[16]{0:T(128)} %param.38) | copy-start | bytes 196
  349.8 241.6 %all-gather.8.cloned.1.call-start = ((), (), s32[]{:S(2)}) async-start(), calls=%async_computation.7 | async-start | bytes 4718592 | tf_op jit(solution)/shard_map/all_gather | solution.py:25
  373.9 107.8 %copy-start.46 = (f32[1024]{0:T(1024)}, f32[1024]{0:T(1024)S(1)}, u32[]{:S(2)}) copy-start(f32[1024]{0:T(1024)S(1)} %mul.1002) | copy-start | bytes 12292
  379.0 125.5 %copy-start.23 = (f32[1536,16]{0,1:T(8,128)}, f32[1536,16]{0,1:T(8,128)S(1)}, u32[]{:S(2)}) copy-start(f32[1536,16]{0,1:T(8,128)S(1)} %fusion.127) | copy-start | bytes 294916
  438.3 23.0 %copy-start.65 = (f32[1024]{0:T(1024)S(1)}, f32[1024]{0:T(1024)}, u32[]{:S(2)}) copy-start(f32[1024]{0:T(1024)} %param.39) | copy-start | bytes 12292
  461.3 20.5 %copy-start.56 = (f32[1536]{0:T(1024)}, f32[1536]{0:T(1024)S(1)}, u32[]{:S(2)}) copy-start(f32[1536]{0:T(1024)S(1)} %get-tuple-element.1157) | copy-start | bytes 18436
  511.2 651.5 %reduce-scatter.10.cloned.1.call-start = ((), (), s32[]{:S(2)}) async-start(), calls=%async_computation.8 | async-start | bytes 1966080
  672.6 14.5 copy-start.4
  754.8 13.2 copy-start.13
  754.9 14.6 copy-start.4
  837.1 14.5 copy-start.4
  919.4 14.5 copy-start.4
  1001.6 14.5 copy-start.4
  1083.8 14.5 copy-start.4
  1115.6 345.9 %all-reduce.15.cloned.1.call-start = ((), (), s32[]{:S(2)}) async-start(), calls=%async_computation.4 | async-start | bytes 25165824 | tf_op jit(solution)/shard_map/psum | solution.py:267
  1138.3 14.7 copy-start.47
  1153.0 70.7 %copy-start.19 = (bf16[1536,16]{1,0:T(8,128)(2,1)}, bf16[1536,16]{1,0:T(8,128)(2,1)S(1)}, u32[]{:S(2)}) copy-start(bf16[1536,16]{1,0:T(8,128)(2,1)S(1)} %get-tuple-element.1147) | copy-start | bytes 147460
  1163.9 21.3 %copy-start.37 = (f32[1088]{0:T(1024)S(1)}, f32[1088]{0:T(1024)}, u32[]{:S(2)}) copy-start(f32[1088]{0:T(1024)} %copy-done.36) | copy-start | bytes 13060
  1164.0 21.2 %copy-start.39 = (f32[1088]{0:T(1024)S(1)}, f32[1088]{0:T(1024)}, u32[]{:S(2)}) copy-start(f32[1088]{0:T(1024)} %copy-done.38) | copy-start | bytes 13060
  1164.0 21.2 %copy-start.41 = (f32[1088]{0:T(1024)S(1)}, f32[1088]{0:T(1024)}, u32[]{:S(2)}) copy-start(f32[1088]{0:T(1024)} %copy-done.40) | copy-start | bytes 13060
  1164.0 21.2 %copy-start.43 = (f32[1088]{0:T(1024)S(1)}, f32[1088]{0:T(1024)}, u32[]{:S(2)}) copy-start(f32[1088]{0:T(1024)} %copy-done.42) | copy-start | bytes 13060
  1194.1 9.1 collective-permute-start.1
  1241.5 322.0 %reduce-scatter.6.cloned.1.call-start = ((), (), s32[]{:S(2)}) async-start(), calls=%async_computation.3 | async-start | bytes 15728640 | tf_op jit(solution)/shard_map/reduce_scatter | solution.py:202
  1255.1 13.6 copy-start.15
  1255.1 727.9 %reduce-scatter.8.cloned.1.call-start = ((), (), s32[]{:S(2)}) async-start(), calls=%async_computation.5 | async-start | bytes 29048832 | tf_op jit(solution)/shard_map/reduce_scatter | solution.py:277
  1323.9 239.5 %copy-start.48 = (f32[1536]{0:T(1024)S(1)}, f32[1536]{0:T(1024)}, u32[]{:S(2)}) copy-start(f32[1536]{0:T(1024)} %get-tuple-element.1152) | copy-start | bytes 18436
  (120 other events, 849.1 us)
Sparse Core Ops, SparseCore 0:
  349.9 73.2 all-gather.5
  511.3 80.0 all-gather.7
  1115.7 25.3 reduce-scatter.9
  1241.6 219.9 all-reduce.14
  1464.2 99.2 reduce-scatter.5
  1567.7 415.2 reduce-scatter.7
where the time goes:
time: 2020 us; the launch traced here: 2000 us
  waiting for transfers between devices  660 us (33%)
  local copies, waits for them, and re-layouts  473 us (23%)
  matrix products  409 us (20%)
  other arithmetic  340 us (17%)
  blocking collectives  81.9 us (4%)
    reduce_scatter x1, waiting for transfers between devices, body(): lax.psum_scatter(stacked, 'seq', scatter_dimension=0, tiled=True)  369 us
    dynamic_update_slice x18, local copies, waits for them, and re-layouts, run_ssd(): closing, outputs = lax.scan(jax.checkpoint(advance), initial, pieces)  156 us
    psum x1, waiting for transfers between devices, body(): d_full = lax.psum(d_normed, 'head')  138 us
    dot_general x18, matrix products, group_ssd(): output = jnp.einsum('tsh,shp->thp', weights, values, precision=HIGH)  123 us
    another operation x92, other arithmetic  96.4 us
    reduce_scatter x1, waiting for transfers between devices, body(): lax.psum_scatter(partial_out, 'head', scatter_dimension=1, tiled=True)  88.7 us
    another operation x112, local copies, waits for them, and re-layouts  69.7 us
    all_gather x2, waiting for transfers between devices, entering(): gathered = jax.tree.map(lambda a: lax.all_gather(a, axis), part)  65.5 us
  transfers between devices with their start and end apart: 8, of which 5 were waited for; matrix products, arithmetic and copies ran while one was open for 12% of the time, Pallas kernels for 0%

commit v1 on v0

v1 whole, which is shorter than its diff:
```python
import jax
import jax.numpy as jnp
from jax import lax
from jax.experimental import pallas as pl
from jax.experimental.pallas import tpu as pltpu
from jax.sharding import PartitionSpec as P

N = 128
HP = 64
DI = 4096
EPS = 1e-05
L = 128
LANES = 128
HALO = 16
F32 = jnp.float32
BF = jnp.bfloat16
VMEM_LIMIT = 56 * 1024 * 1024
FIRST = (((0,), (0,)), ((), ()))
LAST = (((1,), (1,)), ((), ()))


def dot(a, b):
    return jnp.dot(a, b, preferred_element_type=F32)


def dotg(a, b, dims):
    return lax.dot_general(a, b, dims, preferred_element_type=F32)


def split2(v):
    hi = v.astype(BF)
    return hi, (v - hi.astype(F32)).astype(BF)


def split3(v):
    hi = v.astype(BF)
    rest = v - hi.astype(F32)
    mid = rest.astype(BF)
    return hi, mid, (rest - mid.astype(F32)).astype(BF)


def exact_sum(tri, v):
    hi, mid, lo = split3(v)
    return dot(tri, hi) + dot(tri, mid) + dot(tri, lo)


def expand(v, spread2):
    hi, lo = split2(v)
    return dot(jnp.concatenate([hi, lo], 1), spread2)


def fold8(v):
    return jnp.sum(v.reshape(v.shape[0] // 8, 8, v.shape[1]), axis=0)


def stacked_pair(v, left):
    zero = jnp.zeros_like(v)
    return jnp.concatenate([jnp.where(left, v, zero), jnp.where(left, zero, v)], 0)


def lane_is_left(shape):
    return lax.broadcasted_iota(jnp.int32, shape, 1) < HP


def mask_of(info, seg_row):
    rows = lax.broadcasted_iota(jnp.int32, (L, L), 0)
    cols = lax.broadcasted_iota(jnp.int32, (L, L), 1)
    linked = (info[:, 0:1] == seg_row) & (rows >= cols)
    return jnp.where(linked, 0.0, -1e30).astype(F32)


def sigmoid(v):
    return 1.0 / (1.0 + jnp.exp(-v))


def chunk_spec(width, place):
    return pl.BlockSpec((L, width), lambda c: (place(c), 0))


def slab_spec(rows, width, place):
    return pl.BlockSpec((1, rows, width), lambda c: (place(c), 0, 0))


def whole_spec(shape):
    return pl.BlockSpec(shape, lambda c: (0,) * len(shape))


def ahead(c):
    return c


def call(kernel, steps, in_specs, out_specs, out_shape, scratch, args, flops, traffic):
    return pl.pallas_call(
        kernel,
        grid=(steps,),
        in_specs=in_specs,
        out_specs=out_specs,
        out_shape=out_shape,
        scratch_shapes=scratch,
        compiler_params=pltpu.CompilerParams(
            dimension_semantics=("arbitrary",), vmem_limit_bytes=VMEM_LIMIT
        ),
        cost_estimate=pl.CostEstimate(flops=flops, bytes_accessed=traffic, transcendentals=0),
    )(*args)


def conv_kernel(
    raw_ref, pair_ref, step_ref, info_ref, halo_ref, taps_ref, head_ref, tri_ref, spread_ref,
    act_ref, pact_ref, dt_ref, cs_ref, state_ref, total_ref, buf,
):
    c = pl.program_id(0)
    inner = raw_ref.shape[1]
    groups = inner // LANES
    pair_groups = pair_ref.shape[1] // LANES

    @pl.when(c == 0)
    def _():
        buf[0:8, :] = halo_ref[HALO - 8 :, :].astype(F32)
        state_ref[...] = jnp.zeros_like(state_ref)
        total_ref[...] = jnp.zeros_like(total_ref)

    info = info_ref[...]
    masks = [None] + [jnp.broadcast_to(info[:, 2 + k : 3 + k], (L, LANES)) for k in (1, 2, 3)]
    dt = jax.nn.softplus(step_ref[...] + head_ref[0:1, :])
    dt_ref[...] = dt
    cs = exact_sum(tri_ref[...], dt * head_ref[1:2, :])
    cs_ref[...] = cs
    closing = cs[L - 1 :, :]
    total_ref[...] += jnp.broadcast_to(closing, total_ref.shape)
    tail = jnp.exp(closing - cs) * info[:, 2:3] * dt
    tail_wide = expand(tail, spread_ref[...])
    keep = jnp.exp(closing) * info[0:1, 9:10]
    keep_wide = expand(jnp.broadcast_to(keep, (8, LANES)), spread_ref[...])[0:1, :]
    acts = []
    for j in range(groups + pair_groups):
        cols = slice(j * LANES, (j + 1) * LANES)
        if j < groups:
            raw = raw_ref[:, cols].astype(F32)
        else:
            raw = pair_ref[:, (j - groups) * LANES : (j - groups + 1) * LANES].astype(F32)
        buf[8 : 8 + L, cols] = raw
        pre = taps_ref[4:5, cols] + taps_ref[0:1, cols] * raw
        for k in (1, 2, 3):
            pre = pre + taps_ref[k : k + 1, cols] * buf[8 - k : 8 - k + L, cols] * masks[k]
        act = (pre * sigmoid(pre)).astype(BF)
        buf[0:8, cols] = raw[L - 8 :, :]
        if j < groups:
            act_ref[:, cols] = act
        else:
            pact_ref[:, (j - groups) * LANES : (j - groups + 1) * LANES] = act
    key = pact_ref[:, :N]
    for j in range(groups):
        cols = slice(j * LANES, (j + 1) * LANES)
        weighted = (act_ref[:, cols].astype(F32) * tail_wide[:, cols]).astype(BF)
        state_ref[:, cols] = keep_wide[:, cols] * state_ref[:, cols] + dotg(key, weighted, FIRST)


def out_kernel(
    act_ref, pact_ref, dt_ref, cs_ref, info_ref, seg_ref, gate_ref, dgn_ref, state_in_ref,
    gains_ref, spread_ref,
    mixed_ref, gg_ref, sums_ref, entry_ref, state,
):
    c = pl.program_id(0)
    inner = act_ref.shape[1]
    groups = inner // LANES

    @pl.when(c == 0)
    def _():
        state[...] = state_in_ref[...]

    info = info_ref[...]
    mask = mask_of(info, seg_ref[0])
    key = pact_ref[:, :N]
    query = pact_ref[:, N:]
    scores = dotg(query, key, LAST)
    dt = dt_ref[...]
    cs = cs_ref[...]
    cs_rows = cs.T
    closing = cs[L - 1 :, :]
    spread = spread_ref[...]
    dt_wide = expand(dt, spread)
    open_wide = expand(jnp.exp(cs) * info[:, 1:2], spread)
    tail_wide = expand(jnp.exp(closing - cs) * info[:, 2:3], spread)
    keep = jnp.exp(closing) * info[0:1, 9:10]
    keep_wide = expand(jnp.broadcast_to(keep, (8, LANES)), spread)[0:1, :]
    left = lane_is_left((L, LANES))
    square = jnp.zeros((L, LANES), F32)
    cross = jnp.zeros((L, LANES), F32)
    for j in range(groups):
        cols = slice(j * LANES, (j + 1) * LANES)
        x = act_ref[:, cols].astype(F32)
        xd = x * dt_wide[:, cols]
        xd_low = xd.astype(BF)
        weights = []
        for h in (2 * j, 2 * j + 1):
            factor = jnp.exp(cs[:, h : h + 1] - cs_rows[h : h + 1, :] + mask)
            weights.append((scores * factor).astype(BF))
        entry = state[:, cols].astype(BF)
        entry_ref[0, :, cols] = entry
        y = dot(jnp.concatenate(weights, 1), stacked_pair(xd_low, left))
        y = y + open_wide[:, cols] * dot(query, entry)
        mixed = y + gains_ref[0:1, cols] * x
        mixed_ref[:, cols] = mixed.astype(BF)
        gate = gate_ref[:, cols].astype(F32)
        gated = mixed * (gate * sigmoid(gate))
        gg = gated * gains_ref[1:2, cols]
        gg_ref[:, cols] = gg.astype(BF)
        square = square + gated * gated
        cross = cross + gg * dgn_ref[:, cols].astype(F32)
        weighted = (xd * tail_wide[:, cols]).astype(BF)
        state[:, cols] = keep_wide[:, cols] * state[:, cols] + dotg(key, weighted, FIRST)
    lane = lax.broadcasted_iota(jnp.int32, (L, LANES), 1)
    both = jnp.where(
        lane == 0,
        jnp.sum(square, axis=1, keepdims=True),
        jnp.sum(cross, axis=1, keepdims=True),
    )
    sums_ref[0] = both.T[0:8, :]


def gate_kernel(
    mixed_ref, gate_ref, dgn_ref, act_ref, pact_ref, cs_ref, info_ref, stats_ref, gains_ref, spread_ref,
    dmix_ref, dgate_ref, stat_ref, dstate_ref, dgain_ref, dskip_ref,
):
    c = pl.program_id(0)
    inner = act_ref.shape[1]
    groups = inner // LANES

    @pl.when(c == 0)
    def _():
        dstate_ref[...] = jnp.zeros_like(dstate_ref)
        dgain_ref[...] = jnp.zeros_like(dgain_ref)
        dskip_ref[...] = jnp.zeros_like(dskip_ref)

    info = info_ref[...]
    stats = jnp.concatenate([stats_ref[0]] * (LANES // 8), 0).T
    scale = jnp.broadcast_to(stats[:, 0:1], (L, LANES))
    coef = jnp.broadcast_to(stats[:, 1:2], (L, LANES))
    cs = cs_ref[...]
    spread = spread_ref[...]
    open_wide = expand(jnp.exp(cs) * info[:, 1:2], spread)
    keep = jnp.exp(cs[L - 1 :, :]) * info[0:1, 9:10]
    keep_wide = expand(jnp.broadcast_to(keep, (8, LANES)), spread)[0:1, :]
    query = pact_ref[:, N:]
    row = jnp.zeros((L, LANES), F32)
    for j in range(groups):
        cols = slice(j * LANES, (j + 1) * LANES)
        mixed = mixed_ref[:, cols].astype(F32)
        gate = gate_ref[:, cols].astype(F32)
        dgn = dgn_ref[:, cols].astype(F32)
        x = act_ref[:, cols].astype(F32)
        sig = sigmoid(gate)
        act = gate * sig
        gated = mixed * act
        scaled = dgn * scale
        dgain_ref[:, cols] += fold8(scaled * gated)
        dgated = scaled * gains_ref[1:2, cols] - gated * coef
        dmix = dgated * act
        dgate = dgated * mixed * (sig + act * (1.0 - sig))
        dskip_ref[:, cols] += fold8(dmix * x)
        row = row + dgate * gate
        dgate_ref[:, cols] = dgate.astype(BF)
        low = dmix.astype(BF)
        dmix_ref[:, cols] = low
        opened = (low.astype(F32) * open_wide[:, cols]).astype(BF)
        dstate_ref[:, cols] = keep_wide[:, cols] * dstate_ref[:, cols] + dotg(query, opened, FIRST)
    stat_ref[0] = jnp.broadcast_to(jnp.sum(row, axis=1, keepdims=True), (L, LANES)).T[0:8, :]


def back_kernel(
    act_ref, pact_ref, dt_ref, cs_ref, info_ref, seg_ref, dmix_ref, entry_ref, dstate_in_ref,
    raw_ref, pair_ref, raw_prev_ref, pair_prev_ref, step_ref, halo_ref, near_ref,
    taps_ref, head_ref, gains_ref, tri_ref, spread_ref, gather_ref,
    d_ref, stat_ref, dtaps_ref, dhead_ref, dhalo_ref,
    dstate, buf, dbuf,
):
    c = pl.program_id(0)
    last = pl.num_programs(0) - 1
    inner = act_ref.shape[1]
    groups = inner // LANES
    wide = inner + 2 * N

    @pl.when(c == 0)
    def _():
        dstate[...] = dstate_in_ref[...]
        dbuf[L:, :] = jnp.zeros((8, wide), F32)
        dtaps_ref[...] = jnp.zeros_like(dtaps_ref)
        dhead_ref[...] = jnp.zeros_like(dhead_ref)

    @pl.when(c == last)
    def _():
        buf[0:8, :] = halo_ref[HALO - 8 :, :].astype(F32)

    @pl.when(c < last)
    def _():
        buf[0:8, :inner] = raw_prev_ref[HALO - 8 :, :].astype(F32)
        buf[0:8, inner:] = pair_prev_ref[HALO - 8 :, :].astype(F32)

    info = info_ref[...]
    masks = [None] + [jnp.broadcast_to(info[:, 2 + k : 3 + k], (L, LANES)) for k in (1, 2, 3)]
    afters = [None] + [jnp.broadcast_to(info[:, 5 + k : 6 + k], (L, LANES)) for k in (1, 2, 3)]
    mask = mask_of(info, seg_ref[0])
    key = pact_ref[:, :N]
    query = pact_ref[:, N:]
    scores = dotg(query, key, LAST)
    dt = dt_ref[...]
    cs = cs_ref[...]
    cs_rows = cs.T
    closing = cs[L - 1 :, :]
    spread = spread_ref[...]
    dt_wide = expand(dt, spread)
    open_wide = expand(jnp.exp(cs) * info[:, 1:2], spread)
    tail_wide = expand(jnp.exp(closing - cs) * info[:, 2:3], spread)
    keep = jnp.exp(closing) * info[0:1, 9:10]
    keep_wide = expand(jnp.broadcast_to(keep, (8, LANES)), spread)[0:1, :]
    left = lane_is_left((L, LANES))

    def conv_back(j, raw, dact):
        cols = slice(j * LANES, (j + 1) * LANES)
        buf[8 : 8 + L, cols] = raw
        pre = taps_ref[4:5, cols] + taps_ref[0:1, cols] * raw
        moved = [raw]
        for k in (1, 2, 3):
            moved.append(buf[8 - k : 8 - k + L, cols] * masks[k])
            pre = pre + taps_ref[k : k + 1, cols] * moved[k]
        sig = sigmoid(pre)
        dpre = dact * (sig * (1.0 + pre * (1.0 - sig)))
        for k in range(4):
            dtaps_ref[8 * k : 8 * k + 8, cols] += fold8(dpre * moved[k])
        dtaps_ref[32:40, cols] += fold8(dpre)
        dbuf[0:L, cols] = dpre
        draw = taps_ref[0:1, cols] * dpre
        for k in (1, 2, 3):
            draw = draw + taps_ref[k : k + 1, cols] * dbuf[k : k + L, cols] * afters[k]
        dbuf[L : L + 8, cols] = dpre[0:8, :]
        d_ref[:, cols] = draw.astype(BF)
        return draw * raw

    row = jnp.zeros((L, LANES), F32)
    dscores = jnp.zeros((L, L), F32)
    dkey = jnp.zeros((L, N), F32)
    dquery = jnp.zeros((L, N), F32)
    dcs = jnp.zeros((L, LANES), F32)
    ddt = jnp.zeros((L, LANES), F32)
    dclose = jnp.zeros((8, LANES), F32)
    for j in range(groups):
        cols = slice(j * LANES, (j + 1) * LANES)
        x = act_ref[:, cols].astype(F32)
        xd = (x * dt_wide[:, cols]).astype(BF)
        dm = dmix_ref[:, cols]
        dmf = dm.astype(F32)
        xdf = xd.astype(F32)
        factors = []
        weights = []
        for h in (2 * j, 2 * j + 1):
            factor = jnp.exp(cs[:, h : h + 1] - cs_rows[h : h + 1, :] + mask)
            factors.append(factor)
            weights.append((scores * factor).astype(BF))
        pair_x = stacked_pair(xd, left)
        pair_d = stacked_pair(dm, left)
        dweights = dotg(dm, pair_x, LAST)
        dscores = dscores + dweights[:, :L] * factors[0] + dweights[:, L:] * factors[1]
        y = dot(jnp.concatenate(weights, 1), pair_x)
        dxd = dotg(jnp.concatenate(weights, 0), pair_d, FIRST)
        entry = entry_ref[0, :, cols]
        dst = dstate[:, cols]
        dst_low = dst.astype(BF)
        opened = (dmf * open_wide[:, cols]).astype(BF)
        tailed = (xdf * tail_wide[:, cols]).astype(BF)
        from_state = dot(query, entry)
        to_state = dot(key, dst_low)
        out_part = tailed.astype(F32) * to_state
        diff = dmf * y + opened.astype(F32) * from_state - xdf * dxd - out_part
        dxd = dxd + to_state * tail_wide[:, cols]
        hi, lo = split2(diff)
        gather = gather_ref[cols, :]
        dcs = dcs + dot(hi, gather) + dot(lo, gather)
        ddt = ddt + dot((dxd * x).astype(BF), gather)
        close = fold8(out_part) + keep_wide[:, cols] * fold8(dst * entry.astype(F32))
        hi, lo = split2(close)
        dclose = dclose + dot(hi, gather) + dot(lo, gather)
        dquery = dquery + dotg(opened, entry, LAST)
        dkey = dkey + dotg(tailed, dst_low, LAST)
        dstate[:, cols] = keep_wide[:, cols] * dst + dotg(query, opened, FIRST)
        dx = dxd * dt_wide[:, cols] + gains_ref[0:1, cols] * dmf
        row = row + conv_back(j, raw_ref[:, cols].astype(F32), dx)
    dscores = dscores.astype(BF)
    dquery = dquery + dot(dscores, key)
    dkey = dkey + dotg(dscores, query, FIRST)
    row = row + conv_back(groups, pair_ref[:, :N].astype(F32), dkey)
    row = row + conv_back(groups + 1, pair_ref[:, N:].astype(F32), dquery)
    later = dcs
    hi, mid, lo = split3(later)
    tri = tri_ref[...]
    da = dotg(tri, hi, FIRST) + dotg(tri, mid, FIRST) + dotg(tri, lo, FIRST)
    da = da + jnp.sum(dclose, axis=0, keepdims=True)
    ddt = ddt + head_ref[1:2, :] * da
    step = step_ref[...]
    dstep = ddt * sigmoid(step + head_ref[0:1, :])
    dhead_ref[0:8, :] += fold8(dstep)
    dhead_ref[8:16, :] += fold8(dt * da)
    d_ref[:, wide:] = dstep.astype(BF)
    row = row + dstep * step
    stat_ref[0] = jnp.broadcast_to(jnp.sum(row, axis=1, keepdims=True), (L, LANES)).T[0:8, :]

    @pl.when(c == last)
    def _():
        near = near_ref[...]
        for j in range(groups + 2):
            cols = slice(j * LANES, (j + 1) * LANES)
            head_rows = jnp.concatenate([jnp.zeros((8, LANES), F32), dbuf[0:8, cols]], 0)
            dbuf[0:16, cols] = head_rows
            total = jnp.zeros((8, LANES), F32)
            for k in (1, 2, 3):
                total = total + taps_ref[k : k + 1, cols] * dbuf[k : k + 8, cols] * near[:, 5 + k : 6 + k]
            dhalo_ref[:, cols] = total


def flip(block, axis, bit):
    count = lax.axis_size(axis)
    route = [(i, i ^ bit) for i in range(count)]
    return jax.tree.map(lambda a: lax.ppermute(a, axis, route), block)


def sum_over(block, axis):
    bit = 1
    while bit < lax.axis_size(axis):
        block = jax.tree.map(jnp.add, block, flip(block, axis, bit))
        bit *= 2
    return block


def gather_over(block, axis, dim):
    count = lax.axis_size(axis)
    place = lax.axis_index(axis)
    pieces = jnp.stack([block] + [flip(block, axis, d) for d in range(1, count)], 0)
    return jnp.concatenate(
        [lax.dynamic_index_in_dim(pieces, place ^ q, 0, False) for q in range(count)], dim
    )


def shift_over(block, axis, distance):
    devices = range(lax.axis_size(axis))
    route = [(i, i + distance) for i in devices if i + distance in devices]
    return lax.ppermute(block, axis, route)


def entering(through, state, axis, reverse):
    count = lax.axis_size(axis)
    place = lax.axis_index(axis)
    before_decay = jnp.ones_like(through)
    before = jnp.zeros_like(state)
    bit = 1
    while bit < count:
        other_decay = flip(through, axis, bit)
        other = flip(state.astype(BF), axis, bit).astype(F32)
        upper = (place & bit) != 0
        follows = jnp.logical_not(upper) if reverse else upper
        before = jnp.where(follows, before + before_decay * other, before)
        before_decay = jnp.where(follows, before_decay * other_decay, before_decay)
        state = jnp.where(follows, state + through * other, other + other_decay * state)
        through = through * other_decay
        bit *= 2
    return before


def body(
    tokens, boundary, norm_gain, w_gate, w_inner, w_pair, w_step, conv_inner, conv_pair,
    bias_inner, bias_pair, step_bias, decay_log, skip_gain, gate_gain, w_output, cotangent,
):
    rows, width = tokens.shape
    inner = w_gate.shape[1]
    heads = w_step.shape[1]
    head_count = lax.axis_size("head")
    place = lax.axis_index("head")
    quarter = width // head_count
    pair_cols = w_pair.shape[1]
    pair = pair_cols * head_count
    wide = inner + pair
    steps = rows // L
    margin = conv_inner.shape[0] - 1
    sds = jax.ShapeDtypeStruct

    def behind(c):
        return steps - 1 - c

    starts = boundary.reshape(steps, L).astype(F32)
    upper = jnp.triu(jnp.ones((L, L), BF))
    seg = dot(starts.astype(BF), upper)
    seg_last = seg[:, L - 1 :]
    m1 = 1.0 - boundary.astype(F32)
    m2 = m1 * jnp.concatenate([jnp.ones((1,), F32), m1[:-1]])
    m3 = m2 * jnp.concatenate([jnp.ones((2,), F32), m1[:-2]])
    afters = []
    for k, m in ((1, m1), (2, m2), (3, m3)):
        ext = jnp.concatenate([jnp.zeros((8,), F32), m, jnp.zeros((3,), F32)])
        afters.append(ext[k : k + 8 + rows])
    zero = jnp.zeros((rows,), F32)
    opened = (seg == 0).astype(F32).reshape(rows)
    tail = (seg == seg_last).astype(F32).reshape(rows)
    keep = jnp.broadcast_to((seg_last == 0).astype(F32), (steps, L)).reshape(rows)
    info = jnp.stack(
        [seg.reshape(rows), opened, tail, m1, m2, m3]
        + [a[8:] for a in afters]
        + [keep]
        + [zero] * 6,
        1,
    )
    near = jnp.stack([jnp.zeros((8,), F32)] * 6 + [a[:8] for a in afters] + [jnp.zeros((8,), F32)] * 7, 1)
    seg_rows = seg.reshape(steps, 1, L)
    no_start = (jnp.max(boundary) == 0).astype(F32)
    tail_starts = boundary[rows - HALO :].astype(F32)
    after_it = jnp.sum(jnp.triu(jnp.ones((HALO, HALO), F32), 1) * tail_starts[None, :], axis=1)
    is_margin = jnp.arange(HALO) >= HALO - margin
    keep_tail = jnp.where(is_margin & (after_it == 0), 1.0, 0.0)[:, None]

    head_of = jnp.arange(inner)[None, :] // HP
    spread = (head_of == jnp.arange(LANES)[:, None]).astype(BF)
    spread2 = jnp.concatenate([spread, spread], 0)
    gather = (head_of.T == jnp.arange(LANES)[None, :]).astype(BF)
    lower = jnp.tril(jnp.ones((L, L), BF))

    pair_small = jnp.concatenate([conv_pair, bias_pair[None, :], jnp.zeros((3, pair_cols), F32)], 0)
    pair_small = gather_over(pair_small, "head", 1)
    w_pair_all = gather_over(w_pair, "head", 1)
    taps = jnp.concatenate(
        [jnp.concatenate([conv_inner, bias_inner[None, :], jnp.zeros((3, inner), F32)], 0), pair_small], 1
    )
    pad = LANES - heads
    rate = -jnp.exp(decay_log)
    head_rows = jnp.pad(jnp.stack([step_bias, rate] + [jnp.zeros_like(rate)] * 6, 0), ((0, 0), (0, pad)))
    skip_cols = jnp.repeat(skip_gain, HP)
    gains = jnp.stack([skip_cols, gate_gain] + [jnp.zeros_like(gate_gain)] * 6, 0)
    w_step_pad = jnp.pad(w_step, ((0, 0), (0, pad)))

    def norm(t):
        t = t.astype(F32)
        s = lax.rsqrt(jnp.mean(t * t, axis=-1, keepdims=True) + EPS)
        return s, (t * s * norm_gain).astype(BF)

    sent = (tokens[rows - HALO :].astype(F32) * keep_tail).astype(BF)
    token_halo = shift_over(sent, "seq", 1)
    scale_in, normed = norm(tokens)
    _, normed_halo = norm(token_halo)
    inner_raw = dot(normed, w_inner).astype(BF)
    pair_raw = dot(normed, w_pair_all).astype(BF)
    step_raw = dot(normed, w_step_pad)
    halo = jnp.concatenate([dot(normed_halo, w_inner), dot(normed_halo, w_pair_all)], 1).astype(BF)

    wide_flops = 2 * rows * N * inner
    act, pact, dt, cs, closing, total = call(
        conv_kernel,
        steps,
        [
            chunk_spec(inner, ahead), chunk_spec(pair, ahead), chunk_spec(LANES, ahead), chunk_spec(16, ahead),
            whole_spec((HALO, wide)), whole_spec((8, wide)), whole_spec((8, LANES)), whole_spec((L, L)),
            whole_spec((2 * LANES, inner)),
        ],
        [
            chunk_spec(inner, ahead), chunk_spec(pair, ahead), chunk_spec(LANES, ahead), chunk_spec(LANES, ahead),
            whole_spec((N, inner)), whole_spec((8, LANES)),
        ],
        [
            sds((rows, inner), BF), sds((rows, pair), BF), sds((rows, LANES), F32), sds((rows, LANES), F32),
            sds((N, inner), F32), sds((8, LANES), F32),
        ],
        [pltpu.VMEM((8 + L, wide), F32)],
        (inner_raw, pair_raw, step_raw, info, halo, taps, head_rows, lower, spread2),
        2 * wide_flops,
        rows * inner * 5,
    )
    through = jnp.repeat(jnp.exp(total[0, :heads]) * no_start, HP)[None, :]
    state_in = entering(through, closing, "seq", False)

    gate_pre = dot(normed, w_gate).astype(BF)
    dgn = dotg(cotangent, w_output, LAST).astype(BF)

    mixed, gg, sums, entries = call(
        out_kernel,
        steps,
        [
            chunk_spec(inner, ahead), chunk_spec(pair, ahead), chunk_spec(LANES, ahead), chunk_spec(LANES, ahead),
            chunk_spec(16, ahead), slab_spec(1, L, ahead), chunk_spec(inner, ahead), chunk_spec(inner, ahead),
            whole_spec((N, inner)), whole_spec((8, inner)), whole_spec((2 * LANES, inner)),
        ],
        [chunk_spec(inner, ahead), chunk_spec(inner, ahead), slab_spec(8, L, ahead), slab_spec(N, inner, ahead)],
        [
            sds((rows, inner), BF), sds((rows, inner), BF), sds((steps, 8, L), F32), sds((steps, N, inner), BF),
        ],
        [pltpu.VMEM((N, inner), F32)],
        (act, pact, dt, cs, info, seg_rows, gate_pre, dgn, state_in, gains, spread2),
        6 * wide_flops,
        rows * inner * 14,
    )
    sums = sum_over(sums[:, 0:2, :], "head")
    scale_rows = lax.rsqrt(sums[:, 0:1, :] / DI + EPS)
    coef_rows = scale_rows * scale_rows * scale_rows * sums[:, 1:2, :] / DI
    stats = jnp.concatenate([scale_rows, coef_rows, jnp.zeros((steps, 6, L), F32)], 1)
    scale_out = scale_rows.reshape(rows, 1)

    partial_out = dot(gg, w_output).astype(BF)
    branch = lax.psum_scatter(partial_out, "head", scatter_dimension=1, tiled=True).astype(F32)
    token_cols = lax.dynamic_slice_in_dim(tokens, place * quarter, quarter, 1).astype(F32)
    result = (token_cols + scale_out * branch).astype(BF)

    cot_scaled = (cotangent.astype(F32) * scale_out).astype(BF)
    dw_out = dotg(cot_scaled, gg, FIRST).astype(BF)
    dw_out = lax.psum_scatter(dw_out, "seq", scatter_dimension=0, tiled=True).astype(F32)

    dmix, dgate, stat_gate, dstate_local, dgain, dskip = call(
        gate_kernel,
        steps,
        [
            chunk_spec(inner, behind), chunk_spec(inner, behind), chunk_spec(inner, behind), chunk_spec(inner, behind),
            chunk_spec(pair, behind), chunk_spec(LANES, behind), chunk_spec(16, behind), slab_spec(8, L, behind),
            whole_spec((8, inner)), whole_spec((2 * LANES, inner)),
        ],
        [
            chunk_spec(inner, behind), chunk_spec(inner, behind), slab_spec(8, L, behind), whole_spec((N, inner)),
            whole_spec((8, inner)), whole_spec((8, inner)),
        ],
        [
            sds((rows, inner), BF), sds((rows, inner), BF), sds((steps, 8, L), F32), sds((N, inner), F32),
            sds((8, inner), F32), sds((8, inner), F32),
        ],
        [],
        (mixed, gate_pre, dgn, act, pact, cs, info, stats, gains, spread2),
        2 * wide_flops,
        rows * inner * 14,
    )
    dclosing = entering(through, dstate_local, "seq", True)

    dw_gate = dotg(normed, dgate, FIRST).astype(BF)
    dw_gate = lax.psum_scatter(dw_gate, "seq", scatter_dimension=0, tiled=True).astype(F32)
    dn_gate = dotg(dgate, w_gate, LAST)

    def before_spec(width):
        return pl.BlockSpec((HALO, width), lambda c: (jnp.maximum(behind(c) * (L // HALO) - 1, 0), 0))

    d_all, stat_back, dtaps, dhead, dhalo = call(
        back_kernel,
        steps,
        [
            chunk_spec(inner, behind), chunk_spec(pair, behind), chunk_spec(LANES, behind), chunk_spec(LANES, behind),
            chunk_spec(16, behind), slab_spec(1, L, behind), chunk_spec(inner, behind), slab_spec(N, inner, behind),
            whole_spec((N, inner)),
            chunk_spec(inner, behind), chunk_spec(pair, behind), before_spec(inner), before_spec(pair),
            chunk_spec(LANES, behind), whole_spec((HALO, wide)), whole_spec((8, 16)),
            whole_spec((8, wide)), whole_spec((8, LANES)), whole_spec((8, inner)), whole_spec((L, L)),
            whole_spec((2 * LANES, inner)), whole_spec((inner, LANES)),
        ],
        [
            chunk_spec(wide + LANES, behind), slab_spec(8, L, behind), whole_spec((40, wide)),
            whole_spec((16, LANES)), whole_spec((8, wide)),
        ],
        [
            sds((rows, wide + LANES), BF), sds((steps, 8, L), F32), sds((40, wide), F32),
            sds((16, LANES), F32), sds((8, wide), F32),
        ],
        [pltpu.VMEM((N, inner), F32), pltpu.VMEM((8 + L, wide), F32), pltpu.VMEM((L + 8, wide), F32)],
        (
            act, pact, dt, cs, info, seg_rows, dmix, entries, dclosing, inner_raw, pair_raw, inner_raw, pair_raw,
            step_raw, halo, near, taps, head_rows, gains, lower, spread2, gather,
        ),
        14 * wide_flops,
        rows * inner * 14,
    )
    returned = shift_over(dhalo, "seq", -1)
    returned = jnp.concatenate([jnp.zeros((HALO - 8, wide), F32), returned], 0) * keep_tail
    tail_rows = slice(rows - HALO, rows)
    d_all = d_all.at[tail_rows, :wide].set((d_all[tail_rows, :wide].astype(F32) + returned).astype(BF))
    raw_tail = jnp.concatenate([inner_raw[tail_rows], pair_raw[tail_rows]], 1).astype(F32)
    stat_tail = jnp.sum(raw_tail * returned, axis=1)

    w_rest = jnp.concatenate([w_inner, w_pair_all, w_step_pad], 1)
    dw_rest = dotg(normed, d_all, FIRST).astype(BF)
    dw_rest = lax.psum_scatter(dw_rest, "seq", scatter_dimension=0, tiled=True).astype(F32)
    d_normed = (dn_gate + dotg(d_all, w_rest, LAST)).astype(BF)
    d_cols = lax.psum_scatter(d_normed, "head", scatter_dimension=1, tiled=True).astype(F32)
    row_stat = (stat_gate[:, 0, :] + stat_back[:, 0, :]).reshape(rows)
    row_stat = row_stat.at[tail_rows].add(stat_tail)
    row_stat = sum_over(row_stat.reshape(steps, L), "head").reshape(rows, 1)
    gain_cols = lax.dynamic_slice_in_dim(norm_gain, place * quarter, quarter, 0)
    cot_cols = lax.dynamic_slice_in_dim(cotangent, place * quarter, quarter, 1).astype(F32)
    grad_tokens = (
        cot_cols + scale_in * d_cols * gain_cols - token_cols * scale_in * scale_in * row_stat / width
    )
    d_norm_gain = jnp.sum(d_cols * token_cols * scale_in, axis=0)

    dtaps = jnp.sum(dtaps.reshape(5, 8, wide), axis=1)
    dhead = jnp.sum(dhead.reshape(2, 8, LANES), axis=1)
    dgain = jnp.sum(dgain, axis=0)
    dskip = jnp.sum(jnp.sum(dskip, axis=0).reshape(heads, HP), axis=1)
    pair_taps = sum_over(dtaps[:, inner:], "head")
    small = sum_over((dtaps[:, :inner], pair_taps, dhead, dgain, dskip, d_norm_gain), "seq")
    taps_sum, pair_sum, head_sum, gain_sum, skip_sum, norm_sum = small
    pair_sum = lax.dynamic_slice_in_dim(pair_sum, place * pair_cols, pair_cols, 1)
    dw_pair = lax.psum_scatter(dw_rest[:, inner:wide], "head", scatter_dimension=1, tiled=True)
    return (
        result,
        grad_tokens,
        norm_sum,
        dw_gate,
        dw_rest[:, :inner],
        dw_pair,
        dw_rest[:, wide : wide + heads],
        taps_sum[:4],
        pair_sum[:4],
        taps_sum[4],
        pair_sum[4],
        head_sum[0, :heads],
        head_sum[1, :heads] * rate,
        skip_sum,
        gain_sum,
        jnp.transpose(dw_out),
    )


def solution(mesh):
    return jax.shard_map(
        body,
        mesh=mesh,
        in_specs=(
            P("seq", None),
            P("seq"),
            P(),
            P(None, "head"),
            P(None, "head"),
            P(None, "head"),
            P(None, "head"),
            P(None, "head"),
            P(None, "head"),
            P("head"),
            P("head"),
            P("head"),
            P("head"),
            P("head"),
            P("head"),
            P("head", None),
            P("seq", None),
        ),
        out_specs=(
            P("seq", "head"),
            P("seq", "head"),
            P("head"),
            P("seq", "head"),
            P("seq", "head"),
            P("seq", "head"),
            P("seq", "head"),
            P(None, "head"),
            P(None, "head"),
            P("head"),
            P("head"),
            P("head"),
            P("head"),
            P("head"),
            P("head"),
            P("head", "seq"),
        ),
        check_vma=False,
    )
```

time: 2020 us -> 721 us (0.36)
  local copies, waits for them, and re-layouts: 473 us -> 27.5 us
  waiting for transfers between devices: 660 us -> 353 us
  other arithmetic: 340 us -> 37.3 us
  matrix products: 409 us -> 121 us
  Pallas kernels: 0 us -> 107 us
  blocking collectives: 81.9 us -> 0 us
  starting transfers between devices: 6.57 us -> 50.4 us
    dot_general x99 -> x14, matrix products: 409 us -> 121 us  [the longest x6 77.9 us: dotg(): return lax.dot_general(a, b, dims, preferred_element_type=F32)]
    dynamic_update_slice x18 -> x0, local copies, waits for them, and re-layouts: 156 us -> none  [run_ssd(): closing, outputs = lax.scan(jax.checkpoint(advance), initial, pieces)]
    reduce_scatter x1 -> x4, waiting for transfers between devices: 369 us -> 226 us  [the longest x1 89.1 us: body(): lax.psum_scatter(dw_gate, 'seq', scatter_dimension=0, tiled=True)]
    psum x1 -> x0, waiting for transfers between devices: 138 us -> none  [body(): d_full = lax.psum(d_normed, 'head')]
    pallas_call x0 -> x4, Pallas kernels: none -> 107 us  [call(): pl.pallas_call(kernel, grid=(steps,), in_specs=in_specs, out_specs=out_sp...]
    another operation x92 -> x6, other arithmetic: 96.4 us -> 1.66 us  [the longest x3 0.91 us: gather_over(): jnp.stack([block] + [flip(block, axis, d) for d in range(1, count)], 0)]
    another operation x120 -> x27, local copies, waits for them, and re-layouts: 94.8 us -> 2.74 us  [the longest x12 1.36 us: body(): jnp.stack([seg.reshape(rows), opened, tail, m1, m2, m3] + [a[8:] for a in...]
    all_gather x2 -> x0, waiting for transfers between devices: 65.5 us -> none  [entering(): gathered = jax.tree.map(lambda a: lax.all_gather(a, axis), part)]
  transfers between devices with their start and end apart: 8 -> 46, of which waited for: 5 -> 23; matrix products, arithmetic and copies ran while one was open for 12% -> 21% of each run, Pallas kernels for 0% -> 0%
where the time goes in v1:
time: 721 us; the launch traced here: 712 us
  waiting for transfers between devices  353 us (49%)
  matrix products  121 us (17%)
  Pallas kernels  107 us (15%)
  starting transfers between devices  50.4 us (7%)
  other arithmetic  37.3 us (5%)
  local copies, waits for them, and re-layouts  27.5 us (4%)
  between operations  15.9 us (2%)
    pallas_call x4, Pallas kernels, call(): pl.pallas_call(kernel, grid=(steps,), in_specs=in_specs, out_specs=out_sp...  107 us
    reduce_scatter x1, waiting for transfers between devices, body(): lax.psum_scatter(dw_gate, 'seq', scatter_dimension=0, tiled=True)  89.1 us
    dot_general x6, matrix products, dotg(): return lax.dot_general(a, b, dims, preferred_element_type=F32)  77.9 us
    reduce_scatter x1, waiting for transfers between devices, body(): lax.psum_scatter(dw_out, 'seq', scatter_dimension=0, tiled=True).astype(F32)  75.8 us
    reduce_scatter x1, waiting for transfers between devices, body(): lax.psum_scatter(d_normed, 'head', scatter_dimension=1, tiled=True)  61.1 us
    ppermute x38, waiting for transfers between devices, flip(): return jax.tree.map(lambda a: lax.ppermute(a, axis, route), block)  54.9 us
    reduce_scatter x1, waiting for transfers between devices, body(): lax.psum_scatter(partial_out, 'head', scatter_dimension=1, tiled=True)  47.3 us
    ppermute x38, starting transfers between devices, flip(): return jax.tree.map(lambda a: lax.ppermute(a, axis, route), block)  45.1 us
  transfers between devices with their start and end apart: 46, of which 23 were waited for; matrix products, arithmetic and copies ran while one was open for 21% of the time, Pallas kernels for 0%

profile of v1, /device:TPU:0, one launch (start us, length us, event | category | flops | bytes accessed | tf_op | source)
XLA Modules:
  0.0 712.0 jit_solution(11654892626170666969)
XLA Ops:
  15.3 4.2 fusion
  21.1 10.4 %convolution_convert_fusion.5.raw_ref.raw_prev_ref = bf16[1536,1024]{1,0:T(8,128)(2,1)} fusion(bf16[2048,1024]{1,0:T(8,128)(2,1)S(1)} %copy-done, bf16[1536,2048]{1,0:T(8,128)(2,1)} %param.21, f32[2048]{0:T(1024)S(1)} %copy-done.13, f32[1536]{0:T(1024)S(1)} %add_rsqrt_fusion), kind=kOutput, calls=%fused_computation.18 | convolution fusion | flops 6456606720 | bytes 13645824 | tf_op jit(solution)/shard_map/dot_general | solution.py:23
  39.5 3.7 collective-permute-start.3
  45.3 3.4 convolution_convert_fusion.7
  49.0 3.1 convolution_convert_fusion.6.pair_ref.pair_prev_ref
  53.1 16.7 %shard_map.288 = (bf16[1536,1024]{1,0:T(8,128)(2,1)}, bf16[1536,256]{1,0:T(8,128)(2,1)}, f32[1536,128]{1,0:T(8,128)}, f32[1536,128]{1,0:T(8,128)}, f32[128,1024]{1,0:T(8,128)}, /*index=5*/f32[8,128]{1,0:T(8,128)}) custom-call(bf16[1536,1024]{1,0:T(8,128)(2,1)} %convolution_convert_fusion.5.raw_ref.raw_prev_ref, ...), custom_call_target="tpu_custom_call" | custom-call | flops 805306368 | bytes 7864320 | tf_op jit(solution)/shard_map/pallas_call | solution.py:93
  73.8 11.6 %convolution_convert_fusion.4.gate_ref = bf16[1536,1024]{1,0:T(8,128)(2,1)} fusion(bf16[2048,1024]{1,0:T(8,128)(2,1)} %param.24, bf16[1536,2048]{1,0:T(8,128)(2,1)} %param.21, f32[2048]{0:T(1024)S(1)} %copy-done.13, f32[1536]{0:T(1024)S(1)} %add_rsqrt_fusion), kind=kOutput, calls=%fused_computation.17 | convolution fusion | flops 6456606720 | bytes 13645824 | tf_op jit(solution)/shard_map/dot_general | solution.py:23
  88.6 11.2 %convolution_convert_fusion.3.dgn_ref = bf16[1536,1024]{1,0:T(8,128)(2,1)} fusion(bf16[1536,2048]{1,0:T(8,128)(2,1)} %param.37, bf16[1024,2048]{1,0:T(8,128)(2,1)} %param.36), kind=kOutput, calls=%fused_computation.16 | convolution fusion | flops 6444023808 | bytes 13631488 | tf_op jit(solution)/shard_map/dot_general | solution.py:27
  100.2 3.1 collective-permute-start.11
  104.6 8.6 %collective-permute-done.11 = bf16[128,1024]{1,0:T(8,128)(2,1)S(1)} collective-permute-done((bf16[128,1024]{1,0:T(8,128)(2,1)S(1)}, bf16[128,1024]{1,0:T(8,128)(2,1)S(1)}, u32[]{:S(2)}, u32[]{:S(2)}) %collective-permute-start.11) | collective-permute-done | bytes 262176 | tf_op jit(solution)/shard_map/ppermute | solution.py:422
  114.1 17.7 %shard_map.289 = (bf16[1536,1024]{1,0:T(8,128)(2,1)}, bf16[1536,1024]{1,0:T(8,128)(2,1)}, f32[12,8,128]{2,1,0:T(8,128)}, bf16[12,128,1024]{2,1,0:T(8,128)(2,1)}) custom-call(bf16[1536,1024]{1,0:T(8,128)(2,1)} %get-tuple-element.61.act_ref, bf16[1536,256]{1,0:T(8,128)(2,1)} %get-tuple-element.62.pact_ref, f32[1536,128]{1,0:T(8,128)} %get-tuple-element.63.dt_ref, ...), custom_call_target="tpu_custom_call" | custom-call | flops 2415919104 | bytes 22020096 | tf_op jit(solution)/shard_map/pallas_call | solution.py:93
  139.0 15.3 %shard_map.290 = (bf16[1536,1024]{1,0:T(8,128)(2,1)}, bf16[1536,1024]{1,0:T(8,128)(2,1)}, f32[12,8,128]{2,1,0:T(8,128)}, f32[128,1024]{1,0:T(8,128)}, f32[8,1024]{1,0:T(8,128)}, /*index=5*/f32[8,1024]{1,0:T(8,128)}) custom-call(bf16[1536,1024]{1,0:T(8,128)(2,1)} %get-tuple-element.69.mixed_ref, bf16[1536,1024]{1,0:T(8,128)(2,1)} %convolution_convert_fusion.4.gate_ref, ...), custom_call_target="tpu_custom_call" | custom-call | flops 805306368 | bytes 22020096 | tf_op jit(solution)/shard_map/pallas_call | solution.py:93
  156.7 6.0 collective-permute-done.14
  164.8 5.6 collective-permute-done.15
  176.6 8.0 %collective-permute-done.16 = bf16[128,1024]{1,0:T(8,128)(2,1)} collective-permute-done((bf16[128,1024]{1,0:T(8,128)(2,1)}, bf16[128,1024]{1,0:T(8,128)(2,1)}, u32[]{:S(2)}, u32[]{:S(2)}) %collective-permute-start.16) | collective-permute-done | bytes 262176 | tf_op jit(solution)/shard_map/ppermute | solution.py:422
  186.5 57.5 %shard_map.291 = (bf16[1536,1408]{1,0:T(8,128)(2,1)}, f32[12,8,128]{2,1,0:T(8,128)}, f32[40,1280]{1,0:T(8,128)}, f32[16,128]{1,0:T(8,128)}, f32[8,1280]{1,0:T(8,128)}) custom-call(bf16[1536,1024]{1,0:T(8,128)(2,1)} %get-tuple-element.61.act_ref, bf16[1536,256]{1,0:T(8,128)(2,1)} %get-tuple-element.62.pact_ref, f32[1536,128]{1,0:T(8,128)} %get-tuple-element.63.dt_ref, ...), custom_call_target="tpu_custom_call" | custom-call | flops 5637144576 | bytes 22020096 | tf_op jit(solution)/shard_map/pallas_call | solution.py:93
  245.3 4.8 collective-permute-done.17
  251.6 14.8 %convolution_convert_fusion = bf16[2048,1408]{1,0:T(8,128)(2,1)} fusion(bf16[1536,1408]{1,0:T(8,128)(2,1)} %fusion.35, bf16[1536,2048]{1,0:T(8,128)(2,1)S(1)} %bitcast.117, f32[2048]{0:T(1024)S(1)} %copy-done.14, f32[1536]{0:T(1024)S(1)} %add_rsqrt_fusion), kind=kOutput, calls=%fused_computation.7 | convolution fusion | flops 8873836544 | bytes 16398336 | tf_op jit(solution)/shard_map/dot_general | solution.py:27
  266.5 11.4 %convolution_convert_fusion.1 = bf16[1536,2048]{1,0:T(8,128)(2,1)} fusion(bf16[1536,1024]{1,0:T(8,128)(2,1)} %get-tuple-element.68, bf16[1024,2048]{1,0:T(8,128)(2,1)} %param.36), kind=kOutput, calls=%fused_computation.8 | convolution fusion | flops 6445596672 | bytes 13631488 | tf_op jit(solution)/shard_map/dot_general | solution.py:23
  280.0 9.6 %concatenate.82 = bf16[2048,1408]{1,0:T(8,128)(2,1)} concatenate(bf16[2048,1024]{1,0:T(8,128)(2,1)} %param.25, bf16[2048,64]{1,0:T(8,128)(2,1)S(1)} %copy.86, bf16[2048,64]{1,0:T(8,128)(2,1)S(1)} %copy.87, bf16[2048,64]{1,0:T(8,128)(2,1)S(1)} %copy.88, bf16[2048,64]{1,0:T(8,128)(2,1)S(1)} %copy.89, bf16[2048,128]{1,0:T(8,128)(2,1)S(1)} %pad.22.clone), dimensions={1} | concatenate | bytes 11534336 | tf_op jit(solution)/shard_map/concatenate | solution.py:675
  289.6 16.2 %fusion.69 = f32[1536,2048]{1,0:T(8,128)} fusion(bf16[1536,1408]{1,0:T(8,128)(2,1)} %fusion.35, bf16[2048,1408]{1,0:T(8,128)(2,1)} %concatenate.82), kind=kOutput, calls=%fused_computation.172 | convolution fusion | flops 8858370048 | bytes 22675456 | tf_op jit(solution)/shard_map/dot_general | solution.py:27
  305.7 11.5 %add_convert_fusion = bf16[1536,2048]{1,0:T(8,128)(2,1)} fusion(f32[1536,2048]{1,0:T(8,128)} %fusion.69, bf16[1536,1024]{1,0:T(8,128)(2,1)S(1)} %copy-done.22, bf16[2048,1024]{1,0:T(8,128)(2,1)S(1)} %copy-done.20), kind=kOutput, calls=%fused_computation.6 | convolution fusion | flops 6448742400 | bytes 26214400 | tf_op jit(solution)/shard_map/dot_general | solution.py:27
  319.2 12.2 %fusion.5 = bf16[2048,1024]{1,0:T(8,128)(2,1)} fusion(bf16[1536,1024]{1,0:T(8,128)(2,1)S(1)} %copy-done.21, bf16[1536,2048]{1,0:T(8,128)(2,1)} %param.37, f32[1536]{0:T(1024)S(1)} %bitcast.138), kind=kOutput, calls=%fused_computation.19 | convolution fusion | flops 6453985280 | bytes 13637632 | tf_op jit(solution)/shard_map/dot_general | solution.py:27
  331.4 12.0 %convolution_convert_fusion.2 = bf16[2048,1024]{1,0:T(8,128)(2,1)} fusion(bf16[1536,1024]{1,0:T(8,128)(2,1)} %get-tuple-element.70, bf16[1536,2048]{1,0:T(8,128)(2,1)} %param.21, f32[2048]{0:T(1024)S(1)} %copy-done.14, f32[1536]{0:T(1024)S(1)} %add_rsqrt_fusion), kind=kOutput, calls=%fused_computation.15 | convolution fusion | flops 6457131008 | bytes 13645824 | tf_op jit(solution)/shard_map/dot_general | solution.py:27
  358.6 3.6 collective-permute-done.35
  363.3 3.7 collective-permute-done.36
  390.3 47.3 %reduce-scatter.9.cloned.1.call-done = bf16[1536,512]{1,0:T(8,128)(2,1)} async-done(((bf16[1536,2048]{1,0:T(8,128)(2,1)}), bf16[1536,512]{1,0:T(8,128)(2,1)}) %reduce-scatter.9.cloned.1.call-update) | async-done | bytes 1572880 | tf_op jit(solution)/shard_map/reduce_scatter | solution.py:602
  437.5 61.1 %reduce-scatter.11.cloned.1.call-done = bf16[1536,512]{1,0:T(8,128)(2,1)} async-done(((bf16[1536,2048]{1,0:T(8,128)(2,1)}), bf16[1536,512]{1,0:T(8,128)(2,1)}) %reduce-scatter.11.cloned.1.call-update) | async-done | bytes 1572880 | tf_op jit(solution)/shard_map/reduce_scatter | solution.py:679
  498.7 5.2 fusion.14
  514.6 75.8 %reduce-scatter.17.cloned.1.call-done = bf16[256,1024]{1,0:T(8,128)(2,1)} async-done(((bf16[2048,1024]{1,0:T(8,128)(2,1)}), bf16[256,1024]{1,0:T(8,128)(2,1)}) %reduce-scatter.17.cloned.1.call-update) | async-done | bytes 524304 | tf_op jit(solution)/shard_map/reduce_scatter | solution.py:608
  592.8 89.1 %reduce-scatter.13.cloned.1.call-done = bf16[256,1024]{1,0:T(8,128)(2,1)} async-done(((bf16[2048,1024]{1,0:T(8,128)(2,1)}), bf16[256,1024]{1,0:T(8,128)(2,1)}) %reduce-scatter.13.cloned.1.call-update) | async-done | bytes 524304 | tf_op jit(solution)/shard_map/reduce_scatter | solution.py:634
  686.5 18.2 %reduce-scatter.19.cloned.1.call-done = f32[64,256]{1,0:T(8,128)} async-done(((f32[256,256]{1,0:T(8,128)}), f32[64,256]{1,0:T(8,128)}) %reduce-scatter.19.cloned.1.call-update) | async-done | bytes 65552
  (291 shorter events, 113.6 us)
Async XLA Ops:
  7.2 381.2 %reduce-scatter.15.cloned.1.call-start = ((), (), s32[]{:S(2)}) async-start(), calls=%async_computation.9 | async-start | bytes 6488064 | tf_op jit(solution)/shard_map/reduce_scatter | solution.py:677
  7.2 41.4 %collective-permute-start = (bf16[2048,64]{0,1:T(8,128)(2,1)}, bf16[2048,64]{0,1:T(8,128)(2,1)S(1)}, u32[]{:S(2)}, u32[]{:S(2)}) collective-permute-start(bf16[2048,64]{0,1:T(8,128)(2,1)} %param.26), channel_id=1, source_target_pairs={{0,1},{1,0},{2,3},{3,2},{4,5},{5,4},{6,7},{7,6},{8,9},{9,8},{10,11... | collective-permute-start | bytes 786440 | tf_op jit(solution)/shard_map/ppermute | solution.py:422
  7.8 40.9 %collective-permute-start.1 = (bf16[2048,64]{0,1:T(8,128)(2,1)}, bf16[2048,64]{0,1:T(8,128)(2,1)S(1)}, u32[]{:S(2)}, u32[]{:S(2)}) collective-permute-start(bf16[2048,64]{0,1:T(8,128)(2,1)} %param.26), channel_id=1, source_target_pairs={{0,2},{1,3},{2,0},{3,1},{4,6},{5,7},{6,4},{7,5},{8,10},{9,11},{10,... | collective-permute-start | bytes 786440 | tf_op jit(solution)/shard_map/ppermute | solution.py:422
  11.2 28.0 %collective-permute-start.4 = (f32[8,64]{1,0:T(8,128)S(1)}, f32[8,64]{1,0:T(8,128)S(1)}, u32[]{:S(2)}, u32[]{:S(2)}) collective-permute-start(f32[8,64]{1,0:T(8,128)S(1)} %get-tuple-element.172), channel_id=1, source_target_pairs={{0,1},{1,0},{2,3},{3,2},{4,5},{5,4},{6,7},{7,6},{8,9},{9,8},{10,11... | collective-permute-start | bytes 6152 | tf_op jit(solution)/shard_map/ppermute | solution.py:422
  11.3 28.2 %collective-permute-start.5 = (f32[8,64]{1,0:T(8,128)S(1)}, f32[8,64]{1,0:T(8,128)S(1)}, u32[]{:S(2)}, u32[]{:S(2)}) collective-permute-start(f32[8,64]{1,0:T(8,128)S(1)} %get-tuple-element.172), channel_id=1, source_target_pairs={{0,2},{1,3},{2,0},{3,1},{4,6},{5,7},{6,4},{7,5},{8,10},{9,11},{10,... | collective-permute-start | bytes 6152 | tf_op jit(solution)/shard_map/ppermute | solution.py:422
  11.6 31.6 %collective-permute-start.6 = (f32[8,64]{1,0:T(8,128)S(1)}, f32[8,64]{1,0:T(8,128)S(1)}, u32[]{:S(2)}, u32[]{:S(2)}) collective-permute-start(f32[8,64]{1,0:T(8,128)S(1)} %get-tuple-element.172), channel_id=1, source_target_pairs={{0,3},{1,2},{2,1},{3,0},{4,7},{5,6},{6,5},{7,4},{8,11},{9,10},{10,... | collective-permute-start | bytes 6152 | tf_op jit(solution)/shard_map/ppermute | solution.py:422
  39.2 9.5 %collective-permute-start.2 = (bf16[2048,64]{0,1:T(8,128)(2,1)S(1)}, bf16[2048,64]{0,1:T(8,128)(2,1)S(1)}, u32[]{:S(2)}, u32[]{:S(2)}) collective-permute-start(bf16[2048,64]{0,1:T(8,128)(2,1)S(1)} %copy-done.6), channel_id=1, source_target_pairs={{0,3},{1,2},{2,1},{3,0},{4,7},{5,6},{6,5},{7,4},{8,11},{9,10},{10,... | collective-permute-start | bytes 786440 | tf_op jit(solution)/shard_map/ppermute | solution.py:422
  39.5 5.6 collective-permute-start.3
  70.6 14.8 %collective-permute-start.8 = (f32[1,1024]{1,0:T(1,128)S(1)}, f32[1,1024]{1,0:T(1,128)S(1)}, u32[]{:S(2)}, u32[]{:S(2)}) collective-permute-start(f32[1,1024]{1,0:T(1,128)S(1)} %broadcast_in_dim_reshape.3), channel_id=1, source_target_pairs={{0,4},{4,0},{8,12},{12,8},{16,20},{20,16},{24,28},{28,24},{1,5},{5... | collective-permute-start | bytes 12296 | tf_op jit(solution)/shard_map/ppermute | solution.py:422
  73.5 14.8 %collective-permute-start.7 = (bf16[128,1024]{1,0:T(8,128)(2,1)S(1)}, bf16[128,1024]{1,0:T(8,128)(2,1)S(1)}, u32[]{:S(2)}, u32[]{:S(2)}) collective-permute-start(bf16[128,1024]{1,0:T(8,128)(2,1)S(1)} %convert_element_type.162), channel_id=1, source_target_pairs={{0,4},{4,0},{8,12},{12,8},{16,20},{20,16},{24,28},{28,24},{1,5},{5... | collective-permute-start | bytes 786440 | tf_op jit(solution)/shard_map/ppermute | solution.py:422
  85.5 14.5 %collective-permute-start.10 = (f32[1,1024]{1,0:T(1,128)S(1)}, f32[1,1024]{1,0:T(1,128)S(1)}, u32[]{:S(2)}, u32[]{:S(2)}) collective-permute-start(f32[1,1024]{1,0:T(1,128)S(1)} %mul.308), channel_id=1, source_target_pairs={{0,8},{4,12},{8,0},{12,4},{16,24},{20,28},{24,16},{28,20},{1,9},{5... | collective-permute-start | bytes 12296 | tf_op jit(solution)/shard_map/ppermute | solution.py:422
  88.5 11.5 %collective-permute-start.9 = (bf16[128,1024]{1,0:T(8,128)(2,1)S(1)}, bf16[128,1024]{1,0:T(8,128)(2,1)S(1)}, u32[]{:S(2)}, u32[]{:S(2)}) collective-permute-start(bf16[128,1024]{1,0:T(8,128)(2,1)S(1)} %fusion.27), channel_id=1, source_target_pairs={{0,8},{4,12},{8,0},{12,4},{16,24},{20,28},{24,16},{28,20},{1,9},{5... | collective-permute-start | bytes 786440 | tf_op jit(solution)/shard_map/ppermute | solution.py:422
  100.2 12.9 %collective-permute-start.11 = (bf16[128,1024]{1,0:T(8,128)(2,1)S(1)}, bf16[128,1024]{1,0:T(8,128)(2,1)S(1)}, u32[]{:S(2)}, u32[]{:S(2)}) collective-permute-start(bf16[128,1024]{1,0:T(8,128)(2,1)S(1)} %fusion.19), channel_id=1, source_target_pairs={{0,16},{4,20},{8,24},{12,28},{16,0},{20,4},{24,8},{28,12},{1,17},{... | collective-permute-start | bytes 786440 | tf_op jit(solution)/shard_map/ppermute | solution.py:422
  155.4 7.3 %collective-permute-start.14 = (bf16[128,1024]{1,0:T(8,128)(2,1)S(1)}, bf16[128,1024]{1,0:T(8,128)(2,1)S(1)}, u32[]{:S(2)}, u32[]{:S(2)}) collective-permute-start(bf16[128,1024]{1,0:T(8,128)(2,1)S(1)} %convert_element_type.173), channel_id=1, source_target_pairs={{0,4},{4,0},{8,12},{12,8},{16,20},{20,16},{24,28},{28,24},{1,5},{5... | collective-permute-start | bytes 786440 | tf_op jit(solution)/shard_map/ppermute | solution.py:422
  163.9 6.4 collective-permute-start.15
  172.4 12.1 %collective-permute-start.16 = (bf16[128,1024]{1,0:T(8,128)(2,1)}, bf16[128,1024]{1,0:T(8,128)(2,1)}, u32[]{:S(2)}, u32[]{:S(2)}) collective-permute-start(bf16[128,1024]{1,0:T(8,128)(2,1)} %fusion.24), channel_id=1, source_target_pairs={{0,16},{4,20},{8,24},{12,28},{16,0},{20,4},{24,8},{28,12},{1,17},{... | collective-permute-start | bytes 786440 | tf_op jit(solution)/shard_map/ppermute | solution.py:422
  244.0 6.1 collective-permute-start.17
  266.5 171.1 %reduce-scatter.9.cloned.1.call-start = ((), (), s32[]{:S(2)}) async-start(), calls=%async_computation.6 | async-start | bytes 7864320 | tf_op jit(solution)/shard_map/reduce_scatter | solution.py:602
  277.9 220.7 %reduce-scatter.11.cloned.1.call-start = ((), (), s32[]{:S(2)}) async-start(), calls=%async_computation.7 | async-start | bytes 7864320 | tf_op jit(solution)/shard_map/reduce_scatter | solution.py:679
  317.3 273.1 %reduce-scatter.17.cloned.1.call-start = ((), (), s32[]{:S(2)}) async-start(), calls=%async_computation.10 | async-start | bytes 4718592 | tf_op jit(solution)/shard_map/reduce_scatter | solution.py:608
  331.4 350.6 %reduce-scatter.13.cloned.1.call-start = ((), (), s32[]{:S(2)}) async-start(), calls=%async_computation.8 | async-start | bytes 4718592 | tf_op jit(solution)/shard_map/reduce_scatter | solution.py:634
  343.5 361.2 %reduce-scatter.19.cloned.1.call-start = ((), (), s32[]{:S(2)}) async-start(), calls=%async_computation.11 | async-start | bytes 327680
  350.8 16.7 %collective-permute-start.39 = (f32[1024]{0:T(1024)S(1)}, f32[1024]{0:T(1024)S(1)}, u32[]{:S(2)}, u32[]{:S(2)}) collective-permute-start(f32[1024]{0:T(1024)S(1)} %add.292), channel_id=1, source_target_pairs={{0,16},{4,20},{8,24},{12,28},{16,0},{20,4},{24,8},{28,12},{1,17},{... | collective-permute-start | bytes 12296 | tf_op jit(solution)/shard_map/ppermute | solution.py:422
  352.6 15.4 %collective-permute-start.31 = (f32[2,128]{1,0:T(2,128)S(1)}, f32[2,128]{1,0:T(2,128)S(1)}, u32[]{:S(2)}, u32[]{:S(2)}) collective-permute-start(f32[2,128]{1,0:T(2,128)S(1)} %bitcast_reduce_fusion.1), channel_id=1, source_target_pairs={{0,4},{4,0},{8,12},{12,8},{16,20},{20,16},{24,28},{28,24},{1,5},{5... | collective-permute-start | bytes 3080 | tf_op jit(solution)/shard_map/ppermute | solution.py:422
  362.1 4.8 collective-permute-start.36
  368.2 8.2 %collective-permute-start.26 = (f32[5,256]{1,0:T(8,128)S(1)}, f32[5,256]{1,0:T(8,128)S(1)}, u32[]{:S(2)}, u32[]{:S(2)}) collective-permute-start(f32[5,256]{1,0:T(8,128)S(1)} %slice.190), channel_id=1, source_target_pairs={{0,1},{1,0},{2,3},{3,2},{4,5},{5,4},{6,7},{7,6},{8,9},{9,8},{10,11... | collective-permute-start | bytes 15368 | tf_op jit(solution)/shard_map/ppermute | solution.py:422
  368.3 17.2 %collective-permute-start.23 = (f32[5,1024]{1,0:T(8,128)S(1)}, f32[5,1024]{1,0:T(8,128)S(1)}, u32[]{:S(2)}, u32[]{:S(2)}) collective-permute-start(f32[5,1024]{1,0:T(8,128)S(1)} %slice.188), channel_id=1, source_target_pairs={{0,4},{4,0},{8,12},{12,8},{16,20},{20,16},{24,28},{28,24},{1,5},{5... | collective-permute-start | bytes 61448 | tf_op jit(solution)/shard_map/ppermute | solution.py:422
  372.0 4.5 collective-permute-start.33
  385.5 119.9 %collective-permute-start.24 = (f32[5,1024]{1,0:T(8,128)S(1)}, f32[5,1024]{1,0:T(8,128)S(1)}, u32[]{:S(2)}, u32[]{:S(2)}) collective-permute-start(f32[5,1024]{1,0:T(8,128)S(1)} %slice_add_fusion.2), channel_id=1, source_target_pairs={{0,8},{4,12},{8,0},{12,4},{16,24},{20,28},{24,16},{28,20},{1,9},{5... | collective-permute-start | bytes 61448 | tf_op jit(solution)/shard_map/ppermute | solution.py:422
  387.6 117.8 %collective-permute-start.30 = (f32[5,256]{1,0:T(8,128)S(1)}, f32[5,256]{1,0:T(8,128)S(1)}, u32[]{:S(2)}, u32[]{:S(2)}) collective-permute-start(f32[5,256]{1,0:T(8,128)S(1)} %add.282), channel_id=1, source_target_pairs={{0,16},{4,20},{8,24},{12,28},{16,0},{20,4},{24,8},{28,12},{1,17},{... | collective-permute-start | bytes 15368 | tf_op jit(solution)/shard_map/ppermute | solution.py:422
  505.5 5.1 collective-permute-start.25
  511.8 174.1 %collective-permute-start.22 = (f32[512]{0:T(512)S(1)}, f32[512]{0:T(512)S(1)}, u32[]{:S(2)}, u32[]{:S(2)}) collective-permute-start(f32[512]{0:T(512)S(1)} %add.274), channel_id=1, source_target_pairs={{0,16},{4,20},{8,24},{12,28},{16,0},{20,4},{24,8},{28,12},{1,17},{... | collective-permute-start | bytes 6152 | tf_op jit(solution)/shard_map/ppermute | solution.py:422
  (45 other events, 785.9 us)
Sparse Core Ops, SparseCore 0:
  266.6 110.1 reduce-scatter.14
  379.3 58.1 reduce-scatter.8
  440.2 58.3 reduce-scatter.10
  502.1 88.1 reduce-scatter.16
  594.3 87.6 reduce-scatter.12
  684.8 19.8 reduce-scatter.18

commit v2 on v1

v2 whole, which is shorter than its diff:
```python
import functools

import jax
import jax.numpy as jnp
import numpy as np
from jax import lax
from jax.experimental import pallas as pl
from jax.experimental.pallas import tpu as pltpu
from jax.sharding import PartitionSpec as P

N = 128
HP = 64
DI = 4096
EPS = 1e-05
L = 128
LANES = 128
HALO = 16
F32 = jnp.float32
BF = jnp.bfloat16
VMEM_LIMIT = 56 * 1024 * 1024
FIRST = (((0,), (0,)), ((), ()))
LAST = (((1,), (1,)), ((), ()))


def dot(a, b):
    return jnp.dot(a, b, preferred_element_type=F32)


def dotg(a, b, dims):
    return lax.dot_general(a, b, dims, preferred_element_type=F32)


def split2(v):
    hi = v.astype(BF)
    return hi, (v - hi.astype(F32)).astype(BF)


def split3(v):
    hi = v.astype(BF)
    rest = v - hi.astype(F32)
    mid = rest.astype(BF)
    return hi, mid, (rest - mid.astype(F32)).astype(BF)


def exact_sum(tri, v):
    hi, mid, lo = split3(v)
    return dot(tri, hi) + dot(tri, mid) + dot(tri, lo)


def expand(v, spread2):
    hi, lo = split2(v)
    return dot(jnp.concatenate([hi, lo], 1), spread2)


def fold8(v):
    return jnp.sum(v.reshape(v.shape[0] // 8, 8, v.shape[1]), axis=0)


def stacked_pair(v, left):
    zero = jnp.zeros_like(v)
    return jnp.concatenate([jnp.where(left, v, zero), jnp.where(left, zero, v)], 0)


def lane_is_left(shape):
    return lax.broadcasted_iota(jnp.int32, shape, 1) < HP


def columns(slab):
    pad = LANES - slab.shape[0]
    return jnp.concatenate([slab, jnp.zeros((pad, L), F32)], 0).T


def mask_of(info, seg_row):
    rows = lax.broadcasted_iota(jnp.int32, (L, L), 0)
    cols = lax.broadcasted_iota(jnp.int32, (L, L), 1)
    linked = (info[:, 0:1] == seg_row) & (rows >= cols)
    return jnp.where(linked, 0.0, -1e30).astype(F32)


def sigmoid(v):
    return 0.5 * jnp.tanh(0.5 * v) + 0.5


def chunk_spec(width, place):
    return pl.BlockSpec((L, width), lambda c: (place(c), 0))


def slab_spec(rows, width, place):
    return pl.BlockSpec((1, rows, width), lambda c: (place(c), 0, 0))


def whole_spec(shape):
    return pl.BlockSpec(shape, lambda c: (0,) * len(shape))


def ahead(c):
    return c


ANY = pl.BlockSpec(memory_space=pl.ANY)


class Chain:
    def __init__(self):
        self.last = None

    def run(self, kernel, grid, ins, outs, after=(), scratch=(), ids=None, aliases=None, us=5.0):
        given = [array for array, _ in ins]
        after = [a for a in list(after) + [self.last] if a is not None and not any(a is g for g in given)]
        lead = 0 if ids is None else 1
        keep_in = lead + len(ins)

        def inner(*refs):
            kernel(*refs[:keep_in], *refs[keep_in + len(after) :])

        result = pl.pallas_call(
            inner,
            grid_spec=pltpu.PrefetchScalarGridSpec(
                num_scalar_prefetch=lead,
                grid=grid,
                in_specs=[spec for _, spec in ins] + [ANY] * len(after),
                out_specs=[spec for spec, _, _ in outs],
                scratch_shapes=list(scratch),
            ),
            out_shape=[jax.ShapeDtypeStruct(shape, dtype) for _, shape, dtype in outs],
            input_output_aliases={lead + i: o for i, o in (aliases or {}).items()},
            compiler_params=pltpu.CompilerParams(
                dimension_semantics=("arbitrary",) * len(grid), vmem_limit_bytes=VMEM_LIMIT
            ),
            cost_estimate=pl.CostEstimate(flops=int(us * 1.15e9), bytes_accessed=10**4, transcendentals=0),
        )(*(() if ids is None else (ids,)), *given, *after)
        self.last = min(result, key=lambda r: r.size)
        return result


def whole(array):
    zeros = (0,) * array.ndim
    return array, pl.BlockSpec(array.shape, lambda *_: zeros)


def norm_rows(block, gain):
    t = block.astype(F32)
    scale = lax.rsqrt(jnp.mean(t * t, axis=-1, keepdims=True) + EPS)
    return scale, (t * scale * gain).astype(BF)


def proj_kernel(tokens_ref, gain_ref, w_ref, normed_ref, scale_ref, inner_ref):
    scale, normed = norm_rows(tokens_ref[...], gain_ref[...])
    scale_ref[...] = scale
    normed_ref[...] = normed
    inner_ref[...] = dot(normed, w_ref[...]).astype(BF)


def along(v, k):
    zero = jnp.zeros((1, v.shape[1]), v.dtype)
    if k > 0:
        other = jnp.concatenate([zero, v[:-1]], 0)
        return jnp.concatenate([other[:, L - k :], v[:, : L - k]], 1)
    other = jnp.concatenate([v[1:], zero], 0)
    return jnp.concatenate([v[:, -k:], other[:, :-k]], 1)


def prep_kernel(
    starts_ref, upper_ref, tokens_ref, step_bias_ref, decay_ref, skip_ref, gate_gain_ref, spread_ref,
    info_ref, sent_ref, keep_ref, head_ref, gains_ref,
):
    starts = starts_ref[...].astype(F32)
    seg = dot(starts.astype(BF), upper_ref[...])
    m1 = 1.0 - starts
    m2 = m1 * (1.0 - along(starts, 1))
    m3 = m2 * (1.0 - along(starts, 2))
    seg_last = jnp.broadcast_to(seg[:, L - 1 :], seg.shape)
    one = jnp.ones_like(seg)
    zero = jnp.zeros_like(seg)
    fields = [
        seg, jnp.where(seg == 0, one, zero), jnp.where(seg == seg_last, one, zero), m1, m2, m3,
        along(m1, -1), along(m2, -2), along(m3, -3), jnp.where(seg_last == 0, one, zero),
    ]
    for i in range(16):
        info_ref[:, i, :] = fields[i] if i < len(fields) else zero
    rows = lax.broadcasted_iota(jnp.int32, (HALO, L), 0)
    lanes = lax.broadcasted_iota(jnp.int32, (HALO, L), 1)
    last = jnp.broadcast_to(starts[starts.shape[0] - 1 :, :], (HALO, L))
    later = jnp.sum(jnp.where(lanes > rows + L - HALO, last, 0.0), axis=1, keepdims=True)
    place = lax.broadcasted_iota(jnp.int32, (HALO, 1), 0)
    keep = jnp.where((later == 0) & (place >= HALO - 3), 1.0, 0.0)
    keep_ref[...] = keep
    sent_ref[...] = (tokens_ref[...].astype(F32) * keep).astype(BF)
    heads = step_bias_ref.shape[1]
    head_ref[...] = jnp.zeros_like(head_ref)
    head_ref[0:1, 0:heads] = step_bias_ref[...]
    head_ref[1:2, 0:heads] = -jnp.exp(decay_ref[...])
    head_ref[2:3, 0:heads] = skip_ref[...]
    gains_ref[...] = expand(jnp.broadcast_to(head_ref[2:3, :], (8, LANES)), spread_ref[...])
    gains_ref[1:2, :] = gate_gain_ref[...]


def side_kernel(
    swap_ref, normed_ref, own_ref, one_ref, two_ref, three_ref, w_step_ref, halo_ref, gain_ref, w_ref,
    conv_ref, bias_ref,
    side_ref, halo_out_ref, w_side_ref, taps_ref,
):
    @pl.when(pl.program_id(0) == 0)
    def _():
        width = w_ref.shape[0]
        near = jnp.concatenate([own_ref[...], one_ref[...]], 1)
        far = jnp.concatenate([two_ref[...], three_ref[...]], 1)
        swap = swap_ref[0] != 0
        first = jnp.where(swap, far, near)
        second = jnp.where(swap, near, far)
        w_side_ref[:, 0:N] = first[:width]
        w_side_ref[:, N : 2 * N] = second[:width]
        w_side_ref[:, 2 * N :] = jnp.zeros((width, LANES), BF)
        w_side_ref[:, 2 * N : 2 * N + w_step_ref.shape[1]] = w_step_ref[...]
        inner = w_ref.shape[1]
        taps_ref[0:4, :inner] = conv_ref[...]
        taps_ref[4:5, :inner] = bias_ref[...]
        taps_ref[5:8, :inner] = jnp.zeros((3, inner), F32)
        for i, part in enumerate((first, second)):
            extra = part[width:].astype(F32)
            taps_ref[:, inner + i * N : inner + (i + 1) * N] = extra[0:8] + extra[8:16] + extra[16:24]
        _, halo = norm_rows(halo_ref[...], gain_ref[...])
        halo_out_ref[:, :inner] = dot(halo, w_ref[...])
        halo_out_ref[:, inner:] = dot(halo, w_side_ref[...])

    side_ref[...] = dot(normed_ref[...], w_side_ref[...])


def combine_kernel(
    reverse, first, known, final,
    follows_ref, arrived_ref, state_ref, rows_ref, *rest,
):
    rest = list(rest)
    before_ref = None if first else rest.pop(0)
    factor_ref = rest.pop(0) if known else None
    follows = follows_ref[0] != 0
    n = state_ref.shape[0]
    other = arrived_ref[0:n, :].astype(F32)
    if known:
        factor = factor_ref[2:3, :]
    else:
        extra = arrived_ref[n : n + 3, :].astype(F32)
        factor = extra[0:1] + extra[1:2] + extra[2:3]
    through = rows_ref[0:1, :]
    past = jnp.ones_like(through) if first else rows_ref[1:2, :]
    before = jnp.zeros_like(other) if first else before_ref[...]
    rest.pop(0)[...] = jnp.where(follows, before + past * other, before)
    new_rows = rest.pop(0)
    if first:
        new_rows[...] = jnp.zeros_like(new_rows)
    else:
        new_rows[...] = rows_ref[...]
    product = through * factor
    new_rows[0:1, :] = product
    new_rows[1:2, :] = jnp.where(follows, past * factor, past)
    new_rows[2:3, :] = factor
    if not final:
        state = state_ref[...]
        state = jnp.where(follows, state + through * other, other + factor * state)
        rest.pop(0)[...] = state
        low_ref = rest.pop(0)
        low_ref[0:n, :] = state.astype(BF)
        if not known:
            low_ref[n:, :] = factor_rows(product)


def factor_rows(row):
    hi, mid, lo = split3(row)
    return jnp.concatenate([hi, mid, lo, jnp.zeros((HALO - 3, row.shape[1]), BF)], 0)


def meet_kernel(_, *refs):
    for i in range(4):
        total = refs[2 * i][...].astype(F32) + refs[2 * i + 1][...].astype(F32)
        refs[8 + i][...] = total.astype(refs[8 + i].dtype)


def settle_kernel(mine, one, two, three, *rest):
    out_ref = rest[-1]
    total = mine[...] + one[...].astype(F32) + two[...].astype(F32) + three[...].astype(F32)
    out_ref[...] = total.T if out_ref.shape != total.shape else total


def add_kernel(count, *refs):
    for i in range(count):
        refs[2 * count + i][...] = refs[2 * i][...] + refs[2 * i + 1][...]


def share_kernel(swap_ref, kept_ref, got_ref, mine_ref, sent_ref):
    total = kept_ref[...].astype(F32) + got_ref[...].astype(F32)
    half = total.shape[1] // 2
    left, right = total[:, :half], total[:, half:]
    swap = swap_ref[0] != 0
    mine_ref[...] = jnp.where(swap, right, left)
    sent_ref[...] = jnp.where(swap, left, right).astype(BF)


def join_kernel(mine_ref, got_ref, step_ref, out_ref):
    half = mine_ref.shape[1]
    out_ref[:, :half] = (mine_ref[...] + got_ref[...].astype(F32)).astype(BF)
    out_ref[:, half:] = step_ref[:, :half]


def fix_kernel(
    raw_ref, side_ref, keep_ref, back_ref, small_ref, small_got_ref, d_in, dside_in, stat_in,
    d_ref, dside_ref, stat_ref, small_out_ref,
):
    small_out_ref[...] = small_ref[...] + small_got_ref[...]
    inner = raw_ref.shape[1]
    pair = 2 * N
    back = jnp.concatenate([jnp.zeros((HALO - 8, inner + pair), F32), back_ref[...]], 0) * keep_ref[...]
    d_ref[...] = (d_in[...].astype(F32) + back[:, :inner]).astype(BF)
    dside_ref[...] = dside_in[...]
    dside_ref[:, :pair] = (dside_in[:, :pair].astype(F32) + back[:, inner:]).astype(BF)
    row = jnp.sum(back[:, :inner] * raw_ref[...].astype(F32), axis=1, keepdims=True)
    row = row + jnp.sum(back[:, inner:] * side_ref[:, :pair].astype(BF).astype(F32), axis=1, keepdims=True)
    tall = jnp.concatenate([jnp.zeros((L - HALO, LANES), F32), jnp.broadcast_to(row, (HALO, LANES))], 0)
    stat_ref[...] = stat_in[...]
    stat_ref[0] += tall.T[0:8, :]


def nn_kernel(x_ref, w_ref, *rest):
    rest[-1][...] = dot(x_ref[...], w_ref[...]).astype(BF)


def nt_kernel(x_ref, w_ref, *rest):
    rest[-1][...] = dotg(x_ref[...], w_ref[...], LAST).astype(BF)


def cols_kernel(_, x_ref, w_ref, out_ref):
    out_ref[...] = dot(x_ref[...], w_ref[...]).astype(out_ref.dtype)


def cols_add_kernel(_, x_ref, w_ref, got_ref, out_ref):
    out_ref[...] = (dot(x_ref[...], w_ref[...]) + got_ref[...].astype(F32)).astype(out_ref.dtype)


def gate_back_kernel(_, x_ref, w_ref, out_ref):
    out_ref[0] = dotg(x_ref[...], w_ref[...], LAST).astype(BF)


def normed_back_kernel(_, x_ref, w_ref, y_ref, v_ref, base_ref, *rest):
    total = dotg(x_ref[...], w_ref[...], LAST) + dotg(y_ref[...], v_ref[...], LAST) + base_ref[0].astype(F32)
    if len(rest) == 2:
        total = total + rest[0][...].astype(F32)
    rest[-1][...] = total.astype(rest[-1].dtype)


def weight_kernel(scaled, count, grown, _, x_ref, *rest):
    x = x_ref[...]
    if scaled:
        x = (x.astype(F32) * rest[0][...]).astype(BF)
        rest = rest[1:]
    outs = rest[count + grown :]
    for y_ref, out_ref in zip(rest[:count], outs):
        total = dotg(x, y_ref[...], FIRST)
        if len(outs) > count and y_ref is rest[count - 1]:
            half = N // 2
            out_ref[...] = jnp.concatenate([total[:, half:N], total[:, N + half : 2 * N]], 1).astype(BF)
            outs[-2][...] = jnp.concatenate([total[:, :half], total[:, N : N + half]], 1).astype(BF)
            outs[-1][...] = total[:, 2 * N :].astype(BF)
        else:
            out_ref[...] = total.astype(BF)


def conv_kernel(
    raw_ref, side_ref, info_ref, halo_ref, taps_ref, head_ref, tri_ref, spread_ref,
    act_ref, pact_ref, dt_ref, cs_ref, state_ref, low_ref, rows_ref, buf, total_ref,
):
    c = pl.program_id(0)
    inner = raw_ref.shape[1]
    groups = inner // LANES
    pair = pact_ref.shape[1]
    pair_groups = pair // LANES

    @pl.when(c == 0)
    def _():
        buf[0:8, :] = halo_ref[HALO - 8 :, : inner + pair].astype(BF).astype(F32)
        state_ref[...] = jnp.zeros_like(state_ref)
        total_ref[...] = jnp.zeros_like(total_ref)

    info = columns(info_ref[0])
    masks = [None] + [jnp.broadcast_to(info[:, 2 + k : 3 + k], (L, LANES)) for k in (1, 2, 3)]
    dt = jax.nn.softplus(side_ref[:, pair:] + head_ref[0:1, :])
    dt_ref[...] = dt
    cs = exact_sum(tri_ref[...], dt * head_ref[1:2, :])
    cs_ref[...] = cs
    closing = cs[L - 1 :, :]
    total_ref[0:1, :] += closing
    total_ref[1:2, :] = jnp.where(c == 0, 1.0, total_ref[1:2, :]) * info[0:1, 9:10]
    tail = jnp.exp(closing - cs) * info[:, 2:3] * dt
    tail_wide = expand(tail, spread_ref[...])
    keep = jnp.exp(closing) * info[0:1, 9:10]
    keep_wide = expand(jnp.broadcast_to(keep, (8, LANES)), spread_ref[...])[0:1, :]
    acts = []
    for j in range(groups + pair_groups):
        cols = slice(j * LANES, (j + 1) * LANES)
        if j < groups:
            raw = raw_ref[:, cols].astype(F32)
        else:
            raw = side_ref[:, (j - groups) * LANES : (j - groups + 1) * LANES].astype(BF).astype(F32)
        buf[8 : 8 + L, cols] = raw
        pre = taps_ref[4:5, cols] + taps_ref[0:1, cols] * raw
        for k in (1, 2, 3):
            pre = pre + taps_ref[k : k + 1, cols] * buf[8 - k : 8 - k + L, cols] * masks[k]
        act = (pre * sigmoid(pre)).astype(BF)
        buf[0:8, cols] = raw[L - 8 :, :]
        if j < groups:
            act_ref[:, cols] = act
        else:
            pact_ref[:, (j - groups) * LANES : (j - groups + 1) * LANES] = act
    key = pact_ref[:, :N]
    for j in range(groups):
        cols = slice(j * LANES, (j + 1) * LANES)
        weighted = (act_ref[:, cols].astype(F32) * tail_wide[:, cols]).astype(BF)
        state_ref[:, cols] = keep_wide[:, cols] * state_ref[:, cols] + dotg(key, weighted, FIRST)

    @pl.when(c == pl.num_programs(0) - 1)
    def _():
        through = jnp.exp(total_ref[0:1, :]) * total_ref[1:2, :]
        rows_ref[...] = expand(jnp.broadcast_to(through, (8, LANES)), spread_ref[...])
        low_ref[0:N, :] = state_ref[...].astype(BF)
        low_ref[N:, :] = factor_rows(rows_ref[0:1, :])


def out_kernel(
    act_ref, pact_ref, dt_ref, cs_ref, info_ref, gate_ref, dgn_ref, state_in_ref,
    gains_ref, spread_ref,
    mixed_ref, gg_ref, sums_ref, entry_ref, state,
):
    c = pl.program_id(0)
    inner = act_ref.shape[1]
    groups = inner // LANES

    @pl.when(c == 0)
    def _():
        state[...] = state_in_ref[...]

    info = columns(info_ref[0])
    mask = mask_of(info, info_ref[0, 0:1, :])
    key = pact_ref[:, :N]
    query = pact_ref[:, N:]
    scores = dotg(query, key, LAST)
    dt = dt_ref[...]
    cs = cs_ref[...]
    cs_rows = cs.T
    closing = cs[L - 1 :, :]
    spread = spread_ref[...]
    dt_wide = expand(dt, spread)
    open_wide = expand(jnp.exp(cs) * info[:, 1:2], spread)
    tail_wide = expand(jnp.exp(closing - cs) * info[:, 2:3], spread)
    keep = jnp.exp(closing) * info[0:1, 9:10]
    keep_wide = expand(jnp.broadcast_to(keep, (8, LANES)), spread)[0:1, :]
    left = lane_is_left((L, LANES))
    square = jnp.zeros((L, LANES), F32)
    cross = jnp.zeros((L, LANES), F32)
    for j in range(groups):
        cols = slice(j * LANES, (j + 1) * LANES)
        x = act_ref[:, cols].astype(F32)
        xd = x * dt_wide[:, cols]
        xd_low = xd.astype(BF)
        weights = []
        for h in (2 * j, 2 * j + 1):
            factor = jnp.exp(cs[:, h : h + 1] - cs_rows[h : h + 1, :] + mask)
            weights.append((scores * factor).astype(BF))
        entry = state[:, cols].astype(BF)
        entry_ref[0, :, cols] = entry
        y = dot(jnp.concatenate(weights, 1), stacked_pair(xd_low, left))
        y = y + open_wide[:, cols] * dot(query, entry)
        mixed = y + gains_ref[0:1, cols] * x
        mixed_ref[:, cols] = mixed.astype(BF)
        gate = gate_ref[:, cols].astype(F32)
        gated = mixed * (gate * sigmoid(gate))
        gg = gated * gains_ref[1:2, cols]
        gg_ref[:, cols] = gg.astype(BF)
        square = square + gated * gated
        cross = cross + gg * dgn_ref[:, cols].astype(F32)
        weighted = (xd * tail_wide[:, cols]).astype(BF)
        state[:, cols] = keep_wide[:, cols] * state[:, cols] + dotg(key, weighted, FIRST)
    lane = lax.broadcasted_iota(jnp.int32, (L, LANES), 1)
    both = jnp.where(
        lane == 0,
        jnp.sum(square, axis=1, keepdims=True),
        jnp.sum(cross, axis=1, keepdims=True),
    )
    sums_ref[0] = both.T[0:2, :]


def gate_kernel(
    mixed_ref, gate_ref, dgn_ref, act_ref, pact_ref, cs_ref, info_ref, near_ref, far_ref, gains_ref, spread_ref,
    dmix_ref, dgate_ref, stat_ref, dstate_ref, low_ref, dgain_ref, dskip_ref,
):
    c = pl.program_id(0)
    inner = act_ref.shape[1]
    groups = inner // LANES

    @pl.when(c == 0)
    def _():
        dstate_ref[...] = jnp.zeros_like(dstate_ref)
        dgain_ref[...] = jnp.zeros_like(dgain_ref)
        dskip_ref[...] = jnp.zeros_like(dskip_ref)

    info = columns(info_ref[0])
    both = near_ref[0] + far_ref[0]
    scale_row = lax.rsqrt(both[0:1, :] / DI + EPS)
    coef_row = scale_row * scale_row * scale_row * both[1:2, :] / DI
    stats = columns(jnp.concatenate([scale_row, coef_row, jnp.zeros((6, L), F32)], 0))
    scale = jnp.broadcast_to(stats[:, 0:1], (L, LANES))
    coef = jnp.broadcast_to(stats[:, 1:2], (L, LANES))
    cs = cs_ref[...]
    spread = spread_ref[...]
    open_wide = expand(jnp.exp(cs) * info[:, 1:2], spread)
    keep = jnp.exp(cs[L - 1 :, :]) * info[0:1, 9:10]
    keep_wide = expand(jnp.broadcast_to(keep, (8, LANES)), spread)[0:1, :]
    query = pact_ref[:, N:]
    row = jnp.zeros((L, LANES), F32)
    for j in range(groups):
        cols = slice(j * LANES, (j + 1) * LANES)
        mixed = mixed_ref[:, cols].astype(F32)
        gate = gate_ref[:, cols].astype(F32)
        dgn = dgn_ref[:, cols].astype(F32)
        x = act_ref[:, cols].astype(F32)
        sig = sigmoid(gate)
        act = gate * sig
        gated = mixed * act
        scaled = dgn * scale
        dgain_ref[:, cols] += fold8(scaled * gated)
        dgated = scaled * gains_ref[1:2, cols] - gated * coef
        dmix = dgated * act
        dgate = dgated * mixed * (sig + act * (1.0 - sig))
        dskip_ref[:, cols] += fold8(dmix * x)
        row = row + dgate * gate
        dgate_ref[:, cols] = dgate.astype(BF)
        low = dmix.astype(BF)
        dmix_ref[:, cols] = low
        opened = (low.astype(F32) * open_wide[:, cols]).astype(BF)
        dstate_ref[:, cols] = keep_wide[:, cols] * dstate_ref[:, cols] + dotg(query, opened, FIRST)
    stat_ref[0] = jnp.broadcast_to(jnp.sum(row, axis=1, keepdims=True), (L, LANES)).T[0:8, :]

    @pl.when(c == pl.num_programs(0) - 1)
    def _():
        low_ref[...] = dstate_ref[...].astype(BF)


def back_kernel(
    grown, final,
    act_ref, pact_ref, dt_ref, cs_ref, info_ref, dmix_ref, entry_ref,
    raw_ref, side_ref, raw_prev_ref, side_prev_ref, halo_ref,
    taps_ref, head_ref, gains_ref, tri_ref, spread_ref, gather_ref,
    dstate_in_ref, carried_in_ref, dtaps_in_ref, dhead_in_ref, dgain_ref, dskip_ref, stat_in_ref, *rest,
):
    rest = list(rest[grown:])
    d_ref, dside_ref, stat_ref, dstate, carried_ref, dtaps_ref, dhead_ref = rest[:7]
    small_ref, dhalo_ref = rest[7:9] if final else (None, None)
    buf, dbuf = rest[-2:]
    c = pl.program_id(0)
    last = pl.num_programs(0) - 1
    inner = act_ref.shape[1]
    groups = inner // LANES
    pair = 2 * N
    wide = inner + pair

    @pl.when(c == 0)
    def _():
        dstate[...] = dstate_in_ref[...]
        dbuf[L:, :] = carried_in_ref[...]
        dtaps_ref[...] = dtaps_in_ref[...]
        dhead_ref[...] = dhead_in_ref[...]

    def before():
        buf[0:8, :inner] = raw_prev_ref[HALO - 8 :, :].astype(F32)
        buf[0:8, inner:] = side_prev_ref[HALO - 8 :, :pair].astype(BF).astype(F32)

    if final:

        @pl.when(c == last)
        def _():
            buf[0:8, :] = halo_ref[HALO - 8 :, :wide].astype(BF).astype(F32)

        pl.when(c < last)(before)
    else:
        before()

    info = columns(info_ref[0])
    masks = [None] + [jnp.broadcast_to(info[:, 2 + k : 3 + k], (L, LANES)) for k in (1, 2, 3)]
    afters = [None] + [jnp.broadcast_to(info[:, 5 + k : 6 + k], (L, LANES)) for k in (1, 2, 3)]
    mask = mask_of(info, info_ref[0, 0:1, :])
    key = pact_ref[:, :N]
    query = pact_ref[:, N:]
    scores = dotg(query, key, LAST)
    dt = dt_ref[...]
    cs = cs_ref[...]
    cs_rows = cs.T
    closing = cs[L - 1 :, :]
    spread = spread_ref[...]
    dt_wide = expand(dt, spread)
    open_wide = expand(jnp.exp(cs) * info[:, 1:2], spread)
    tail_wide = expand(jnp.exp(closing - cs) * info[:, 2:3], spread)
    keep = jnp.exp(closing) * info[0:1, 9:10]
    keep_wide = expand(jnp.broadcast_to(keep, (8, LANES)), spread)[0:1, :]
    left = lane_is_left((L, LANES))

    def conv_back(j, raw, dact):
        cols = slice(j * LANES, (j + 1) * LANES)
        buf[8 : 8 + L, cols] = raw
        pre = taps_ref[4:5, cols] + taps_ref[0:1, cols] * raw
        moved = [raw]
        for k in (1, 2, 3):
            moved.append(buf[8 - k : 8 - k + L, cols] * masks[k])
            pre = pre + taps_ref[k : k + 1, cols] * moved[k]
        sig = sigmoid(pre)
        dpre = dact * (sig * (1.0 + pre * (1.0 - sig)))
        for k in range(4):
            dtaps_ref[8 * k : 8 * k + 8, cols] += fold8(dpre * moved[k])
        dtaps_ref[32:40, cols] += fold8(dpre)
        dbuf[0:L, cols] = dpre
        draw = taps_ref[0:1, cols] * dpre
        for k in (1, 2, 3):
            draw = draw + taps_ref[k : k + 1, cols] * dbuf[k : k + L, cols] * afters[k]
        dbuf[L : L + 8, cols] = dpre[0:8, :]
        if j < groups:
            d_ref[:, cols] = draw.astype(BF)
        else:
            dside_ref[:, (j - groups) * LANES : (j - groups + 1) * LANES] = draw.astype(BF)
        return draw * raw

    row = jnp.zeros((L, LANES), F32)
    dscores = jnp.zeros((L, L), F32)
    dkey = jnp.zeros((L, N), F32)
    dquery = jnp.zeros((L, N), F32)
    dcs = jnp.zeros((L, LANES), F32)
    ddt = jnp.zeros((L, LANES), F32)
    dclose = jnp.zeros((8, LANES), F32)
    for j in range(groups):
        cols = slice(j * LANES, (j + 1) * LANES)
        x = act_ref[:, cols].astype(F32)
        xd = (x * dt_wide[:, cols]).astype(BF)
        dm = dmix_ref[:, cols]
        dmf = dm.astype(F32)
        xdf = xd.astype(F32)
        factors = []
        weights = []
        for h in (2 * j, 2 * j + 1):
            factor = jnp.exp(cs[:, h : h + 1] - cs_rows[h : h + 1, :] + mask)
            factors.append(factor)
            weights.append((scores * factor).astype(BF))
        pair_x = stacked_pair(xd, left)
        pair_d = stacked_pair(dm, left)
        dweights = dotg(dm, pair_x, LAST)
        dscores = dscores + dweights[:, :L] * factors[0] + dweights[:, L:] * factors[1]
        y = dot(jnp.concatenate(weights, 1), pair_x)
        dxd = dotg(jnp.concatenate(weights, 0), pair_d, FIRST)
        entry = entry_ref[0, :, cols]
        dst = dstate[:, cols]
        dst_low = dst.astype(BF)
        opened = (dmf * open_wide[:, cols]).astype(BF)
        tailed = (xdf * tail_wide[:, cols]).astype(BF)
        from_state = dot(query, entry)
        to_state = dot(key, dst_low)
        out_part = tailed.astype(F32) * to_state
        diff = dmf * y + opened.astype(F32) * from_state - xdf * dxd - out_part
        dxd = dxd + to_state * tail_wide[:, cols]
        hi, lo = split2(diff)
        gather = gather_ref[cols, :]
        dcs = dcs + dot(hi, gather) + dot(lo, gather)
        ddt = ddt + dot((dxd * x).astype(BF), gather)
        close = fold8(out_part) + keep_wide[:, cols] * fold8(dst * entry.astype(F32))
        hi, lo = split2(close)
        dclose = dclose + dot(hi, gather) + dot(lo, gather)
        dquery = dquery + dotg(opened, entry, LAST)
        dkey = dkey + dotg(tailed, dst_low, LAST)
        dstate[:, cols] = keep_wide[:, cols] * dst + dotg(query, opened, FIRST)
        dx = dxd * dt_wide[:, cols] + gains_ref[0:1, cols] * dmf
        row = row + conv_back(j, raw_ref[:, cols].astype(F32), dx)
    dscores = dscores.astype(BF)
    dquery = dquery + dot(dscores, key)
    dkey = dkey + dotg(dscores, query, FIRST)
    row = row + conv_back(groups, side_ref[:, :N].astype(BF).astype(F32), dkey)
    row = row + conv_back(groups + 1, side_ref[:, N:pair].astype(BF).astype(F32), dquery)
    later = dcs
    hi, mid, lo = split3(later)
    tri = tri_ref[...]
    da = dotg(tri, hi, FIRST) + dotg(tri, mid, FIRST) + dotg(tri, lo, FIRST)
    da = da + jnp.sum(dclose, axis=0, keepdims=True)
    ddt = ddt + head_ref[1:2, :] * da
    step = side_ref[:, pair:]
    dstep = ddt * sigmoid(step + head_ref[0:1, :])
    dhead_ref[0:8, :] += fold8(dstep)
    dhead_ref[8:16, :] += fold8(dt * da)
    dside_ref[:, pair:] = dstep.astype(BF)
    row = row + dstep * step
    stat_ref[0] = stat_in_ref[0] + jnp.broadcast_to(jnp.sum(row, axis=1, keepdims=True), (L, LANES)).T[0:8, :]

    @pl.when(c == last)
    def _():
        carried_ref[...] = dbuf[L:, :]

    if final:

        @pl.when(c == last)
        def _():
            for k in range(5):
                small_ref[k : k + 1, :] = jnp.sum(dtaps_ref[8 * k : 8 * k + 8, :], axis=0, keepdims=True)
            small_ref[5:8, :] = jnp.zeros((3, wide), F32)
            small_ref[5:6, :inner] = jnp.sum(dgain_ref[...], axis=0, keepdims=True)
            skip = jnp.broadcast_to(jnp.sum(dskip_ref[...], axis=0, keepdims=True), (8, inner))
            hi, lo = split2(skip)
            skip = dot(hi, gather_ref[...]) + dot(lo, gather_ref[...])
            small_ref[6:7, 0:LANES] = skip[0:1, :]
            small_ref[6:7, LANES : 2 * LANES] = jnp.sum(dhead_ref[0:8, :], axis=0, keepdims=True)
            small_ref[6:7, 2 * LANES : 3 * LANES] = (
                jnp.sum(dhead_ref[8:16, :], axis=0, keepdims=True) * head_ref[1:2, :]
            )
            dhalo_ref[...] = jnp.zeros((8, wide), F32)
            for j in range(groups + 2):
                cols = slice(j * LANES, (j + 1) * LANES)
                for k in (1, 2, 3):
                    reach = dbuf[L : L + 8, cols] * masks[k][0:8, :] * taps_ref[k : k + 1, cols]
                    dhalo_ref[8 - k :, cols] += reach[0:k, :]


def flip(block, axis, bit):
    count = lax.axis_size(axis)
    route = [(i, i ^ bit) for i in range(count)]
    return jax.tree.map(lambda a: lax.ppermute(a, axis, route), block)


def sum_over(block, axis):
    bit = 1
    while bit < lax.axis_size(axis):
        block = block + flip(block, axis, bit)
        bit *= 2
    return block


def shift_over(block, axis, distance):
    devices = range(lax.axis_size(axis))
    route = [(i, i + distance) for i in devices if i + distance in devices]
    return lax.ppermute(block, axis, route)


def body(
    tokens, boundary, norm_gain, w_gate, w_inner, w_pair, w_step, conv_inner, conv_pair,
    bias_inner, bias_pair, step_bias, decay_log, skip_gain, gate_gain, w_output, cotangent,
):
    rows, width = tokens.shape
    inner = w_gate.shape[1]
    heads = w_step.shape[1]
    head_count = lax.axis_size("head")
    place = lax.axis_index("head")
    quarter = width // head_count
    pair_cols = w_pair.shape[1]
    pair = pair_cols * head_count
    wide = inner + pair
    side = pair + LANES
    steps = rows // L
    chain = Chain()
    run = chain.run

    def behind(c):
        return steps - 1 - c

    def row_of(v):
        return v.reshape(1, -1)

    head_of = np.arange(inner)[None, :] // HP == np.arange(LANES)[:, None]
    spread2 = jnp.asarray(np.concatenate([head_of, head_of], 0), BF)
    gather = jnp.asarray(head_of.T, BF)
    lower = jnp.asarray(np.tril(np.ones((L, L))), BF)
    upper = jnp.asarray(np.triu(np.ones((L, L))), BF)

    def split_low(v):
        hi, mid, lo = split3(v)
        return [hi, mid, lo]

    swap = (place & 2) != 0

    def own_columns(block):
        near = jnp.where(swap, block[:, N:], block[:, :N])
        far = jnp.where(swap, block[:, :N], block[:, N:])
        kept = jnp.concatenate([near[:, :pair_cols], far[:, :pair_cols]], 1)
        sent = jnp.concatenate([near[:, pair_cols:], far[:, pair_cols:]], 1)
        total = kept.astype(F32) + flip(sent, "head", 1).astype(F32)
        return total[:, :pair_cols] + flip(total[:, pair_cols:].astype(block.dtype), "head", 2).astype(F32)

    pair_small = jnp.concatenate([conv_pair, row_of(bias_pair), jnp.zeros((3, pair_cols), F32)], 0)
    pair_own = jnp.concatenate([w_pair, *split_low(pair_small), jnp.zeros((8, pair_cols), BF)], 0)
    pair_pieces = [pair_own] + [flip(pair_own, "head", d) for d in (1, 2, 3)]
    gain_row = row_of(norm_gain)

    info_spec = slab_spec(16, L, ahead)
    info_back = slab_spec(16, L, behind)
    one_step = (1,)
    info, sent, keep_tail, head_rows, gains = run(
        prep_kernel,
        one_step,
        [
            whole(boundary.reshape(steps, L)), whole(upper),
            (tokens, pl.BlockSpec((HALO, width), lambda c: (rows // HALO - 1, 0))),
            whole(row_of(step_bias)), whole(row_of(decay_log)), whole(row_of(skip_gain)), whole(row_of(gate_gain)),
            whole(spread2),
        ],
        [
            (whole_spec((steps, 16, L)), (steps, 16, L), F32), (whole_spec((HALO, width)), (HALO, width), BF),
            (whole_spec((HALO, 1)), (HALO, 1), F32), (whole_spec((8, LANES)), (8, LANES), F32),
            (whole_spec((8, inner)), (8, inner), F32),
        ],
        us=2,
    )
    token_halo = shift_over(sent, "seq", 1)

    big = 512
    blocks = rows // big

    def rows_spec(cols, start=0, size=big):
        return pl.BlockSpec((size, cols), lambda i, *_: (i + start, 0))

    def fixed(shape):
        return pl.BlockSpec(shape, lambda i, *_: (0,) * len(shape))

    normed, scale_in, inner_raw = run(
        proj_kernel,
        (blocks,),
        [(tokens, rows_spec(width)), whole(gain_row), whole(w_inner)],
        [
            (rows_spec(width), (rows, width), BF),
            (rows_spec(1), (rows, 1), F32),
            (rows_spec(inner), (rows, inner), BF),
        ],
        us=12,
    )
    halo_shape = (HALO, inner + side)
    side_raw, halo, w_side, taps = run(
        side_kernel,
        (blocks,),
        [(normed, rows_spec(width))]
        + [whole(p) for p in pair_pieces]
        + [whole(w_step), whole(token_halo), whole(gain_row), whole(w_inner), whole(conv_inner), whole(row_of(bias_inner))],
        [
            (rows_spec(side), (rows, side), F32),
            (fixed(halo_shape), halo_shape, F32),
            (fixed((width, side)), (width, side), BF),
            (fixed((8, wide)), (8, wide), F32),
        ],
        ids=swap.astype(jnp.int32).reshape(1),
        us=10,
    )

    low_rows = N + HALO
    act, pact, dt, cs, closing, closing_low, through = run(
        conv_kernel,
        (steps,),
        [
            (inner_raw, chunk_spec(inner, ahead)), (side_raw, chunk_spec(side, ahead)), (info, info_spec),
            whole(halo), whole(taps), whole(head_rows), whole(lower), whole(spread2),
        ],
        [
            (chunk_spec(inner, ahead), (rows, inner), BF), (chunk_spec(pair, ahead), (rows, pair), BF),
            (chunk_spec(LANES, ahead), (rows, LANES), F32), (chunk_spec(LANES, ahead), (rows, LANES), F32),
            (whole_spec((N, inner)), (N, inner), F32), (whole_spec((low_rows, inner)), (low_rows, inner), BF),
            (whole_spec((8, inner)), (8, inner), F32),
        ],
        scratch=[pltpu.VMEM((8 + L, wide), F32), pltpu.VMEM((8, LANES), F32)],
        us=17,
    )

    seq_count = lax.axis_size("seq")
    seq_place = lax.axis_index("seq")

    def exchange(state, low, rows0, known, reverse, between):
        before, row, factors = None, rows0, []
        bit = 1
        while bit < seq_count:
            arrived = flip(low, "seq", bit)
            if between:
                between.pop(0)()
            follows = (seq_place & bit) != 0
            if reverse:
                follows = jnp.logical_not(follows)
            final = bit * 2 >= seq_count
            has = known is not None
            ins = [whole(arrived), whole(state), whole(row)]
            if before is not None:
                ins.append(whole(before))
            if has:
                ins.append(whole(known[len(factors)]))
            big_out = (fixed((N, inner)), (N, inner), F32)
            outs = [big_out, (fixed((8, inner)), (8, inner), F32)]
            if not final:
                height = N if has else low_rows
                outs += [big_out, (fixed((height, inner)), (height, inner), BF)]
            got = run(
                functools.partial(combine_kernel, reverse, before is None, has, final),
                one_step,
                ins,
                outs,
                ids=follows.astype(jnp.int32).reshape(1),
                us=2,
            )
            before, row = got[0], got[1]
            factors.append(row)
            if not final:
                state, low = got[2], got[3]
            bit *= 2
        for work in between:
            work()
        return before, factors

    def product(kernel, x, w, start, size, into):
        out = [] if into is None else [(into, ANY)]
        return run(
            kernel,
            (size,),
            [(x, rows_spec(x.shape[1], start)), whole(w)] + out,
            [(rows_spec(inner, start), (rows, inner), BF)],
            aliases={2: 0} if out else None,
            us=2.9 * size,
        )[0]

    third = max(blocks // 3, 1)
    held = {}

    def gate_one():
        held["gate"] = product(nn_kernel, normed, w_gate, 0, blocks - third, None)

    def gate_two():
        held["gate"] = product(nn_kernel, normed, w_gate, blocks - third, third, held["gate"])
        held["dgn"] = product(nt_kernel, cotangent, w_output, 0, third, None)

    def gate_three():
        held["dgn"] = product(nt_kernel, cotangent, w_output, third, blocks - third, held["dgn"])

    state_in, factors = exchange(closing, closing_low, through, None, False, [gate_one, gate_two, gate_three])
    gate_pre, dgn = held["gate"], held["dgn"]

    mixed, gg, sums, entries = run(
        out_kernel,
        (steps,),
        [
            (act, chunk_spec(inner, ahead)), (pact, chunk_spec(pair, ahead)), (dt, chunk_spec(LANES, ahead)),
            (cs, chunk_spec(LANES, ahead)), (info, info_spec),
            (gate_pre, chunk_spec(inner, ahead)), (dgn, chunk_spec(inner, ahead)),
            whole(state_in), whole(gains), whole(spread2),
        ],
        [
            (chunk_spec(inner, ahead), (rows, inner), BF), (chunk_spec(inner, ahead), (rows, inner), BF),
            (slab_spec(2, L, ahead), (steps, 2, L), F32), (slab_spec(N, inner, ahead), (steps, N, inner), BF),
        ],
        scratch=[pltpu.VMEM((N, inner), F32)],
        us=18,
    )

    order = [place ^ 3, place ^ 1, place ^ 2, place]

    def quarter_spec():
        return pl.BlockSpec((big, quarter), lambda i, ids: (i, 0))

    def out_quarter(which, got, dtype, after=()):
        ins = [
            (gg, pl.BlockSpec((big, inner), lambda i, ids: (i, 0))),
            (w_output, pl.BlockSpec((inner, quarter), lambda i, ids: (0, ids[0]))),
        ]
        if got is not None:
            ins.append((got, quarter_spec()))
        return run(
            cols_kernel if got is None else cols_add_kernel,
            (blocks,),
            ins,
            [(quarter_spec(), (rows, quarter), dtype)],
            after=after,
            ids=order[which].reshape(1),
            us=5,
        )[0]

    sums_core = flip(sums, "head", 1)
    out_a = out_quarter(0, None, BF)
    sums = sums + sums_core
    got_a = flip(out_a, "head", 1)
    sums_x = flip(sums, "head", 2)
    out_b = out_quarter(1, None, BF, [sums_core])
    got_b = flip(out_b, "head", 1)
    scale_out = lax.rsqrt((sums + sums_x)[:, 0, :] / DI + EPS).reshape(rows, 1)

    share = width // seq_count
    manual = seq_count == 8
    half = seq_count // 2
    seq_core = seq_place % 2
    if manual:
        row_ids = [jnp.arange(half) * 2 + (1 - seq_core), jnp.arange(half) * 2 + seq_core]
    else:
        share = 256
        row_ids = [jnp.arange(width // share)]

    def weight_rows(which, x, ys, scale=None, into=()):
        ids = row_ids[which].astype(jnp.int32)
        count = ids.shape[0]
        ins = [(x, pl.BlockSpec((rows, share), lambda i, ids: (0, ids[i])))]
        if scale is not None:
            ins.append(whole(scale))
        outs = []
        lead = count * which
        for y, cols, at in ys:
            ins.append((y, pl.BlockSpec((rows, cols), lambda i, ids, at=at: (0, at))))
            if cols == side:
                spec = pl.BlockSpec((share, LANES), lambda i, ids: (i + lead, 0))
                outs += [(spec, (width, LANES), BF)] * 3
            else:
                outs.append((pl.BlockSpec((share, cols), lambda i, ids: (i, 0)), (count * share, cols), BF))
        aliases = {len(ins) + k: len(outs) - 3 + k for k in range(len(into))}
        return run(
            functools.partial(weight_kernel, scale is not None, len(ys), len(into)),
            (count,),
            ins + [(a, ANY) for a in into],
            outs,
            ids=ids,
            aliases=aliases,
            us=8,
        )

    class Spread:
        def __init__(self, kept, got):
            cols = kept.shape[1]
            part = share // 2
            z = seq_place // 2
            ids = jnp.stack([z ^ d for d in range(4)]).astype(jnp.int32)
            ins = []
            for d in range(4):
                spec = pl.BlockSpec((part, cols), lambda i, ids, d=d: (ids[d] * 2 + i, 0))
                ins += [(kept, spec), (got, spec)]
            out = pl.BlockSpec((part, cols), lambda i, ids: (i, 0))
            sums = run(
                meet_kernel,
                (2,),
                ins,
                [(out, (share, cols), BF if d else F32) for d in range(4)],
                ids=ids,
                us=4,
            )
            self.parts = [sums[0]] + [flip(sums[d], "seq", 2 * d) for d in (1, 2, 3)]
            self.shape = (share, cols)

        def settle(self, turned=False, into=None, place=0, total=1):
            rows_, cols = self.shape
            count = 1 if turned else 2
            step = (rows_ // count, cols)
            spec = pl.BlockSpec(step, lambda i: (i, 0))
            if turned:
                out = (pl.BlockSpec((cols, rows_), lambda i: (0, 0)), (cols, rows_), F32)
            else:
                out = (pl.BlockSpec(step, lambda i: (i, place)), (rows_, cols * total), F32)
            return run(
                settle_kernel,
                (count,),
                [(p, spec) for p in self.parts] + ([] if into is None else [(into, ANY)]),
                [out],
                aliases=None if into is None else {4: 0},
                us=2,
            )[0]

    (out_first,) = weight_rows(0, cotangent, [(gg, inner, 0)], scale_out)
    if manual:
        out_got = flip(out_first, "seq", 1)
    away = out_quarter(2, got_a, BF)
    away_got = flip(away, "head", 2)
    mine = out_quarter(3, got_b, F32)
    if manual:
        (out_second,) = weight_rows(1, cotangent, [(gg, inner, 0)], scale_out)

    dmix, dgate, stat, dstate_local, dstate_low, dgain, dskip = run(
        gate_kernel,
        (steps,),
        [
            (mixed, chunk_spec(inner, behind)), (gate_pre, chunk_spec(inner, behind)), (dgn, chunk_spec(inner, behind)),
            (act, chunk_spec(inner, behind)), (pact, chunk_spec(pair, behind)), (cs, chunk_spec(LANES, behind)),
            (info, info_back), (sums, slab_spec(2, L, behind)), (sums_x, slab_spec(2, L, behind)),
            whole(gains), whole(spread2),
        ],
        [
            (chunk_spec(inner, behind), (rows, inner), BF), (chunk_spec(inner, behind), (rows, inner), BF),
            (slab_spec(8, L, behind), (steps, 8, L), F32), (whole_spec((N, inner)), (N, inner), F32),
            (whole_spec((N, inner)), (N, inner), BF),
            (whole_spec((8, inner)), (8, inner), F32), (whole_spec((8, inner)), (8, inner), F32),
        ],
        us=17,
    )

    order_ids = jnp.stack(order).astype(jnp.int32)

    def gate_first():
        held["first"] = weight_rows(0, normed, [(dgate, inner, 0)])[0]

    def gate_second():
        if manual:
            held["got"] = flip(held["first"], "seq", 1)
            held["second"] = weight_rows(1, normed, [(dgate, inner, 0)])[0]

    def gate_third():
        held["dn"] = run(
            gate_back_kernel,
            (4, blocks),
            [
                (dgate, pl.BlockSpec((big, inner), lambda n, i, ids: (i, 0))),
                (w_gate, pl.BlockSpec((quarter, inner), lambda n, i, ids: (ids[n], 0))),
            ],
            [(pl.BlockSpec((1, big, quarter), lambda n, i, ids: (n, i, 0)), (4, rows, quarter), BF)],
            ids=order_ids,
            us=17,
        )[0]

    dstate, _ = exchange(
        dstate_local, dstate_low, through, factors, True, [gate_first, gate_second, gate_third]
    )
    dn_gate = held["dn"]

    parts = 1
    each = steps // parts
    carried = jnp.zeros((8, wide), F32)
    dtaps = jnp.zeros((40, wide), F32)
    dhead = jnp.zeros((16, LANES), F32)
    d_inner = d_side = small = dhalo = None
    if manual:
        out_sum = Spread(out_second, out_got)
        gate_sum = Spread(held["second"], held["got"])
    for part in range(parts):
        first = steps - 1 - part * each

        def at(c, first=first):
            return first - c

        def near_end(c, at=at):
            return jnp.maximum(at(c) * (L // HALO) - 1, 0)

        final = part == parts - 1
        grown = [] if d_inner is None else [(d_inner, ANY), (d_side, ANY)]
        state_specs = [
            (whole_spec((N, inner)), (N, inner), F32), (whole_spec((8, wide)), (8, wide), F32),
            (whole_spec((40, wide)), (40, wide), F32), (whole_spec((16, LANES)), (16, LANES), F32),
        ]
        if final:
            state_specs += [(whole_spec((8, wide)), (8, wide), F32)] * 2
        ins = [
            (act, chunk_spec(inner, at)), (pact, chunk_spec(pair, at)), (dt, chunk_spec(LANES, at)),
            (cs, chunk_spec(LANES, at)), (info, slab_spec(16, L, at)),
            (dmix, chunk_spec(inner, at)), (entries, slab_spec(N, inner, at)),
            (inner_raw, chunk_spec(inner, at)), (side_raw, chunk_spec(side, at)),
            (inner_raw, pl.BlockSpec((HALO, inner), lambda c, p=near_end: (p(c), 0))),
            (side_raw, pl.BlockSpec((HALO, side), lambda c, p=near_end: (p(c), 0))),
            whole(halo), whole(taps), whole(head_rows), whole(gains), whole(lower), whole(spread2), whole(gather),
            whole(dstate), whole(carried), whole(dtaps), whole(dhead), whole(dgain), whole(dskip),
            (stat, slab_spec(8, L, at)), *grown,
        ]
        aliases = {24: 2}
        if grown:
            aliases.update({25: 0, 26: 1})
        got = run(
            functools.partial(back_kernel, len(grown), final),
            (each,),
            ins,
            [
                (chunk_spec(inner, at), (rows, inner), BF), (chunk_spec(side, at), (rows, side), BF),
                (slab_spec(8, L, at), (steps, 8, L), F32), *state_specs,
            ],
            after=[away_got] if part == min(1, parts - 1) else [],
            scratch=[pltpu.VMEM((8 + L, wide), F32), pltpu.VMEM((L + 8, wide), F32)],
            aliases=aliases,
            us=64 / parts,
        )
        d_inner, d_side, stat, dstate, carried, dtaps, dhead = got[:7]
        if final:
            small, dhalo = got[7:]

    returned = shift_over(dhalo, "seq", -1)
    small_got = flip(small, "seq", 1)

    def last_rows(cols):
        return pl.BlockSpec((HALO, cols), lambda c: (rows // HALO - 1, 0))

    last_slab = slab_spec(8, L, lambda c: steps - 1)
    if manual:
        dw_out = out_sum.settle(True)
    d_inner, d_side, stat, small = run(
        fix_kernel,
        one_step,
        [
            (inner_raw, last_rows(inner)), (side_raw, last_rows(side)), whole(keep_tail), whole(returned),
            whole(small), whole(small_got),
            (d_inner, last_rows(inner)), (d_side, last_rows(side)), (stat, last_slab),
        ],
        [
            (last_rows(inner), (rows, inner), BF), (last_rows(side), (rows, side), BF), (last_slab, (steps, 8, L), F32),
            (whole_spec((8, wide)), (8, wide), F32),
        ],
        aliases={6: 0, 7: 1, 8: 2},
        us=2,
    )

    def add(pairs):
        return run(
            functools.partial(add_kernel, len(pairs)),
            one_step,
            [whole(a) for pair_ in pairs for a in pair_],
            [(pl.BlockSpec(a.shape, lambda i, n=a.ndim: (0,) * n), a.shape, a.dtype) for a, _ in pairs],
            us=1,
        )

    def normed_quarter(which, got, dtype):
        ins = [
            (d_inner, pl.BlockSpec((big, inner), lambda i, ids: (i, 0))),
            (w_inner, pl.BlockSpec((quarter, inner), lambda i, ids: (ids[0], 0))),
            (d_side, pl.BlockSpec((big, side), lambda i, ids: (i, 0))),
            (w_side, pl.BlockSpec((quarter, side), lambda i, ids: (ids[0], 0))),
            (dn_gate, pl.BlockSpec((1, big, quarter), lambda i, ids: (which, i, 0))),
        ]
        if got is not None:
            ins.append((got, quarter_spec()))
        return run(
            normed_back_kernel,
            (blocks,),
            ins,
            [(quarter_spec(), (rows, quarter), dtype)],
            ids=order[which].reshape(1),
            us=6.5,
        )[0]

    token_cols = lax.dynamic_slice_in_dim(tokens, place * quarter, quarter, 1).astype(F32)
    half_inner = inner // 2
    inner_parts = [(d_inner, half_inner, 0), (d_inner, half_inner, 1), (d_side, side, 0)]

    swap_id = swap.astype(jnp.int32).reshape(1)
    first_a, first_b, sent, kept, step = weight_rows(0, normed, inner_parts)
    stat = stat[:, 0, :]
    stat_got = flip(stat, "head", 1)
    small_got = flip(small, "seq", 2)
    if manual:
        got_first = [flip(block, "seq", 1) for block in (first_a, first_b)]
        second_a, second_b, sent, kept, step = weight_rows(1, normed, inner_parts, None, [sent, kept, step])
    side_got = flip(sent, "head", 1)
    dn_a = normed_quarter(0, None, BF)
    dn_got_a = flip(dn_a, "head", 1)
    tall = pl.BlockSpec((256, LANES), lambda i, *_: (i, 0))
    thin = pl.BlockSpec((256, pair_cols), lambda i, *_: (i, 0))
    side_mine, side_sent = run(
        share_kernel,
        (width // 256,),
        [(kept, tall), (side_got, tall)],
        [(thin, (width, pair_cols), F32), (thin, (width, pair_cols), BF)],
        ids=swap_id,
        us=3,
    )
    side_got = flip(side_sent, "head", 2)
    if manual:
        dw_gate = gate_sum.settle()
    stat, small = add([(stat, stat_got), (small, small_got)])
    stat_got = flip(stat, "head", 2)
    small_got = flip(small, "seq", 4)
    dn_b = normed_quarter(1, None, BF)
    dn_got_b = flip(dn_b, "head", 1)
    if manual:
        sum_a = Spread(second_a, got_first[0])
    rest = run(
        join_kernel,
        (width // 256,),
        [(side_mine, thin), (side_got, thin), (step, tall)],
        [(tall, (width, LANES), BF)],
        us=3,
    )[0]
    if manual:
        rest_got = flip(rest[: half * share], "seq", 1)
    dn_away = normed_quarter(2, dn_got_a, BF)
    dn_away_got = flip(dn_away, "head", 2)
    dn_mine = normed_quarter(3, dn_got_b, F32)
    stat, small = add([(stat, stat_got), (small, small_got)])
    bit = 8
    while bit < seq_count:
        small = small + flip(small, "seq", bit)
        bit *= 2
    if manual:
        sum_b = Spread(second_b, got_first[1])
        sum_rest = Spread(rest[half * share :], rest_got)
        dw_inner = sum_a.settle(total=2)
        dw_inner = sum_b.settle(into=dw_inner, place=1, total=2)
        dw_side = sum_rest.settle()
    else:
        dw_out, dw_gate, dw_inner, dw_side = [
            lax.psum_scatter(block, "seq", scatter_dimension=0, tiled=True).astype(F32)
            for block in (out_first, held["first"], jnp.concatenate([first_a, first_b], 1), rest)
        ]
        dw_out = jnp.transpose(dw_out)
    row_stat = stat.reshape(rows, 1)
    result = (token_cols + scale_out * (mine + away_got.astype(F32))).astype(BF)
    d_cols = dn_mine + dn_away_got.astype(F32)
    gain_cols = lax.dynamic_slice_in_dim(norm_gain, place * quarter, quarter, 0)
    cot_cols = lax.dynamic_slice_in_dim(cotangent, place * quarter, quarter, 1).astype(F32)
    grad_tokens = (
        cot_cols + scale_in * d_cols * gain_cols - token_cols * scale_in * scale_in * row_stat / width
    )
    d_norm_gain = jnp.sum(d_cols * token_cols * scale_in, axis=0)
    norm_sum = sum_over(d_norm_gain.reshape(-1, LANES), "seq").reshape(-1)
    pair_sum = own_columns(small[:, inner:])
    return (
        result,
        grad_tokens,
        norm_sum,
        dw_gate,
        dw_inner,
        dw_side[:, :pair_cols],
        dw_side[:, pair_cols : pair_cols + heads],
        small[:4, :inner],
        pair_sum[:4],
        small[4, :inner],
        pair_sum[4],
        small[6, LANES : LANES + heads],
        small[6, 2 * LANES : 2 * LANES + heads],
        small[6, :heads],
        small[5, :inner],
        dw_out,
    )


def solution(mesh):
    return jax.shard_map(
        body,
        mesh=mesh,
        in_specs=(
            P("seq", None),
            P("seq"),
            P(),
            P(None, "head"),
            P(None, "head"),
            P(None, "head"),
            P(None, "head"),
            P(None, "head"),
            P(None, "head"),
            P("head"),
            P("head"),
            P("head"),
            P("head"),
            P("head"),
            P("head"),
            P("head", None),
            P("seq", None),
        ),
        out_specs=(
            P("seq", "head"),
            P("seq", "head"),
            P("head"),
            P("seq", "head"),
            P("seq", "head"),
            P("seq", "head"),
            P("seq", "head"),
            P(None, "head"),
            P(None, "head"),
            P("head"),
            P("head"),
            P("head"),
            P("head"),
            P("head"),
            P("head"),
            P("head", "seq"),
        ),
        check_vma=False,
    )
```

time: 721 us -> 506 us (0.70)
  waiting for transfers between devices: 353 us -> 28.2 us
  Pallas kernels: 107 us -> 356 us
  matrix products: 121 us -> 0 us
  other arithmetic: 37.3 us -> 14.2 us
  between operations: 15.9 us -> 1.45 us
  starting transfers between devices: 50.4 us -> 63.8 us
  local copies, waits for them, and re-layouts: 27.5 us -> 34.8 us
    reduce_scatter x5 -> x0, waiting for transfers between devices: 273 us -> none  [the longest x1 89.1 us: body(): lax.psum_scatter(dw_gate, 'seq', scatter_dimension=0, tiled=True)]
    pallas_call x4 -> x47, Pallas kernels: 107 us -> 356 us  [run(): pl.pallas_call(inner, grid_spec=pltpu.PrefetchScalarGridSpec(num_scalar_p...]
    dot_general x14 -> x0, matrix products: 121 us -> none  [the longest x6 77.9 us: dotg(): return lax.dot_general(a, b, dims, preferred_element_type=F32)]
    ppermute x38 -> x49, waiting for transfers between devices: 54.9 us -> 28.2 us  [flip(): return jax.tree.map(lambda a: lax.ppermute(a, axis, route), block)]
    unnamed x7 -> x0, waiting for transfers between devices: 18.3 us -> none
    unnamed x63 -> x131, local copies, waits for them, and re-layouts: 5.57 us -> 21.1 us
    ppermute x38 -> x49, starting transfers between devices: 45.1 us -> 58.8 us  [flip(): return jax.tree.map(lambda a: lax.ppermute(a, axis, route), block)]
    convert_element_type x10 -> x0, other arithmetic: 10.5 us -> none  [the longest x6 5.76 us: entering(): other = flip(state.astype(BF), axis, bit).astype(F32)]
  transfers between devices with their start and end apart: 46 -> 51, of which waited for: 23 -> 7; matrix products, arithmetic and copies ran while one was open for 21% -> 6% of each run, Pallas kernels for 0% -> 60%
where the time goes in v2:
time: 506 us; the launch traced here: 499 us
  Pallas kernels  356 us (70%)
  starting transfers between devices  63.8 us (13%)
  local copies, waits for them, and re-layouts  34.8 us (7%)
  waiting for transfers between devices  28.2 us (6%)
  other arithmetic  14.2 us (3%)
    pallas_call x47, Pallas kernels, run(): pl.pallas_call(inner, grid_spec=pltpu.PrefetchScalarGridSpec(num_scalar_p...  356 us
    ppermute x49, starting transfers between devices, flip(): return jax.tree.map(lambda a: lax.ppermute(a, axis, route), block)  58.8 us
    ppermute x49, waiting for transfers between devices, flip(): return jax.tree.map(lambda a: lax.ppermute(a, axis, route), block)  28.2 us
    unnamed x131, local copies, waits for them, and re-layouts  21.1 us
  transfers between devices with their start and end apart: 51, of which 7 were waited for; matrix products, arithmetic and copies ran while one was open for 6% of the time, Pallas kernels for 60%

profile of v2, /device:TPU:0, one launch (start us, length us, event | category | flops | bytes accessed | tf_op | source)
XLA Modules:
  0.0 498.8 jit_solution(2345369786525996876)
XLA Ops:
  14.0 12.3 %shard_map.325 = (bf16[1536,2048]{1,0:T(8,128)(2,1)}, f32[1536,1]{1,0:T(8,128)}, bf16[1536,1024]{1,0:T(8,128)(2,1)}) custom-call(bf16[1536,2048]{1,0:T(8,128)(2,1)} %refs_0_.3, f32[1,2048]{1,0:T(1,128)} %bitcast.55, bf16[2048,1024]{1,0:T(8,128)(2,1)} %refs_2_.21, f32[16,1]{1,0:T(8,128)} %get-tuple-element.112.refs_3_.refs_2_), custom_call_target="tpu_custom_call" | custom-call | flops 13799999488 | bytes 10000 | tf_op jit(solution)/shard_map/pallas_call | solution.py:116
  36.2 10.2 %shard_map.326 = (f32[1536,384]{1,0:T(8,128)}, f32[16,1408]{1,0:T(8,128)}, bf16[2048,384]{1,0:T(8,128)(2,1)}, f32[8,1280]{1,0:T(8,128)}) custom-call(s32[1]{0:T(128)} %bitcast.6.refs_0_, bf16[1536,2048]{1,0:T(8,128)(2,1)} %get-tuple-element.114.refs_1_.refs_0_, bf16[2080,64]{1,0:T(8,128)(2,1)} %copy-done.3, bf16[2080,64]{1,0:T(8,128)(2,1)} %copy.65.refs_3_, ...), custom_call_target="tpu_custom_call" | custom-call | flops 11500000256 | bytes 10000 | tf_op jit(solution)/shard_map/pallas_call | solution.py:116
  46.4 16.9 %shard_map.327 = (bf16[1536,1024]{1,0:T(8,128)(2,1)}, bf16[1536,256]{1,0:T(8,128)(2,1)}, f32[1536,128]{1,0:T(8,128)}, f32[1536,128]{1,0:T(8,128)}, f32[128,1024]...) custom-call(bf16[1536,1024]{1,0:T(8,128)(2,1)} %get-tuple-element.113.refs_0_.refs_7_.refs_9_, ...), custom_call_target="tpu_custom_call" | custom-call | flops 19549999104 | bytes 10000 | tf_op jit(solution)/shard_map/pallas_call | solution.py:116
  64.8 8.5 %shard_map.328.refs_4_.refs_2_ = bf16[1536,1024]{1,0:T(8,128)(2,1)} custom-call(bf16[1536,2048]{1,0:T(8,128)(2,1)} %get-tuple-element.114.refs_1_.refs_0_, bf16[2048,1024]{1,0:T(8,128)(2,1)} %refs_2_.17, f32[8,1024]{1,0:T(8,128)} %get-tuple-element.126.refs_2_.refs_3_), custom_call_target="tpu_custom_call" | custom-call | flops 6670000128 | bytes 10000 | tf_op jit(solution)/shard_map/pallas_call | solution.py:116
  76.3 6.2 %shard_map.330.refs_2_.refs_5_.refs_1_ = bf16[1536,1024]{1,0:T(8,128)(2,1)} custom-call(bf16[1536,2048]{1,0:T(8,128)(2,1)} %get-tuple-element.114.refs_1_.refs_0_, bf16[2048,1024]{1,0:T(8,128)(2,1)} %refs_2_.17, bf16[1536,1024]{1,0:T(8,128)(2,1)} %shard_map.328.refs_4_.refs_2_, ...), custom_call_target="tpu_custom_call", output_to_operand_aliasing={{}: (2, {})} | custom-call | flops 3335000064 | bytes 10000 | tf_op jit(solution)/shard_map/pallas_call | solution.py:116
  84.1 6.2 %shard_map.331.refs_5_.refs_2_ = bf16[1536,1024]{1,0:T(8,128)(2,1)} custom-call(bf16[1536,2048]{1,0:T(8,128)(2,1)} %refs_1_.12, bf16[1024,2048]{1,0:T(8,128)(2,1)} %refs_2_.16, bf16[1536,1024]{1,0:T(8,128)(2,1)} %shard_map.330.refs_2_.refs_5_.refs_1_), custom_call_target="tpu_custom_call" | custom-call | flops 3335000064 | bytes 10000 | tf_op jit(solution)/shard_map/pallas_call | solution.py:116
  96.8 8.8 %shard_map.333.refs_5_.refs_6_.refs_2_ = bf16[1536,1024]{1,0:T(8,128)(2,1)} custom-call(bf16[1536,2048]{1,0:T(8,128)(2,1)} %refs_1_.12, bf16[1024,2048]{1,0:T(8,128)(2,1)} %refs_2_.16, bf16[1536,1024]{1,0:T(8,128)(2,1)} %shard_map.331.refs_5_.refs_2_, f32[8,1024]{1,0:T(8,128)} %get-tuple-element.133.refs_3_.refs_5_), custom_call_target="tpu_custom_call", output_to_operand_aliasing={{}: (2, {})} | custom-call | flops 6670000128 | bytes 10000 | tf_op jit(solution)/shard_map/pallas_call | solution.py:116
  105.6 3.8 collective-permute-done.6.refs_1_
  112.2 17.9 %shard_map.335 = (bf16[1536,1024]{1,0:T(8,128)(2,1)}, bf16[1536,1024]{1,0:T(8,128)(2,1)}, f32[12,2,128]{2,1,0:T(2,128)}, bf16[12,128,1024]{2,1,0:T(8,128)(2,1)}) custom-call(bf16[1536,1024]{1,0:T(8,128)(2,1)} %get-tuple-element.122.refs_0_.refs_3_, bf16[1536,256]{1,0:T(8,128)(2,1)} %get-tuple-element.123.refs_1_.refs_4_, ...), custom_call_target="tpu_custom_call" | custom-call | flops 20700000256 | bytes 10000 | tf_op jit(solution)/shard_map/pallas_call | solution.py:116
  130.2 5.2 %shard_map.336.refs_4_ = bf16[1536,512]{1,0:T(8,128)(2,1)} custom-call(s32[1]{0:T(128)} %bitcast.14.refs_0_, bf16[1536,1024]{1,0:T(8,128)(2,1)} %get-tuple-element.141.refs_1_.refs_3_, bf16[1024,2048]{1,0:T(8,128)(2,1)} %refs_2_.16, f32[12,2,128]{2,1,0:T(2,128)} %get-tuple-element.140.refs_3_), custom_call_target="tpu_custom_call" | custom-call | flops 5750000128 | bytes 10000 | tf_op jit(solution)/shard_map/pallas_call | solution.py:116
  137.2 5.2 %shard_map.337.refs_4_ = bf16[1536,512]{1,0:T(8,128)(2,1)} custom-call(s32[1]{0:T(128)} %bitcast.13.refs_0_, bf16[1536,1024]{1,0:T(8,128)(2,1)} %get-tuple-element.141.refs_1_.refs_3_, bf16[1024,2048]{1,0:T(8,128)(2,1)} %refs_2_.16, f32[12,2,128]{2,1,0:T(2,128)} %copy-done.15, bf16[1536,512]{1,0:T(8,128)(2,1)} %shard_map.336.refs_4_), custom_call_target="tpu_custom_call" | custom-call | flops 5750000128 | bytes 10000 | tf_op jit(solution)/shard_map/pallas_call | solution.py:116
  144.2 10.0 %shard_map.338.refs_4_ = bf16[1024,1024]{1,0:T(8,128)(2,1)} custom-call(s32[4]{0:T(128)} %fusion.11.refs_0_, bf16[1536,2048]{1,0:T(8,128)(2,1)} %refs_1_.12, f32[1536,1]{1,0:T(8,128)} %copy.69.refs_2_, bf16[1536,1024]{1,0:T(8,128)(2,1)} %get-tuple-element.141.refs_1_.refs_3_, bf16[1536,512]{1,0:T(8,128)(2,1)} %shard_map.337.refs_4_), custom_call_target="tpu_custom_call" | custom-call | flops 9200000000 | bytes 10000 | tf_op jit(solution)/shard_map/pallas_call | solution.py:116
  155.9 5.5 %shard_map.339.refs_4_ = bf16[1536,512]{1,0:T(8,128)(2,1)} custom-call(s32[1]{0:T(128)} %bitcast.15.refs_0_, bf16[1536,1024]{1,0:T(8,128)(2,1)} %get-tuple-element.141.refs_1_.refs_3_, bf16[1024,2048]{1,0:T(8,128)(2,1)} %refs_2_.16, bf16[1536,512]{1,0:T(8,128)(2,1)} %copy-done.24, bf16[1024,1024]{1,0:T(8,128)(2,1)} %shard_map.338.refs_4_), custom_call_target="tpu_custom_call" | custom-call | flops 5750000128 | bytes 10000 | tf_op jit(solution)/shard_map/pallas_call | solution.py:116
  163.3 6.1 %shard_map.340.refs_4_ = f32[1536,512]{1,0:T(8,128)} custom-call(s32[1]{0:T(128)} %bitcast.12.refs_0_, bf16[1536,1024]{1,0:T(8,128)(2,1)} %get-tuple-element.141.refs_1_.refs_3_, bf16[1024,2048]{1,0:T(8,128)(2,1)} %refs_2_.16, bf16[1536,512]{1,0:T(8,128)(2,1)} %copy-done.25, bf16[1536,512]{1,0:T(8,128)(2,1)} %shard_map.339.refs_4_), custom_call_target="tpu_custom_call" | custom-call | flops 5750000128 | bytes 10000 | tf_op jit(solution)/shard_map/pallas_call | solution.py:116
  169.4 10.1 %shard_map.341.refs_11_.refs_1_.refs_3_.refs_5_.refs_7_ = bf16[1024,1024]{1,0:T(8,128)(2,1)} custom-call(s32[4]{0:T(128)} %fusion.10.refs_0_, bf16[1536,2048]{1,0:T(8,128)(2,1)} %refs_1_.12, f32[1536,1]{1,0:T(8,128)} %copy.69.refs_2_, bf16[1536,1024]{1,0:T(8,128)(2,1)} %get-tuple-element.141.refs_1_.refs_3_, f32[1536,512]{1,0:T(8,128)} %shard_map.340.refs_4_), custom_call_target="tpu_custom_call" | custom-call | flops 9200000000 | bytes 10000 | tf_op jit(solution)/shard_map/pallas_call | solution.py:116
  179.5 17.7 %shard_map.342 = (bf16[1536,1024]{1,0:T(8,128)(2,1)}, bf16[1536,1024]{1,0:T(8,128)(2,1)}, f32[12,8,128]{2,1,0:T(8,128)}, f32[128,1024]{1,0:T(8,128)}, bf16[128,1...) custom-call(bf16[1536,1024]{1,0:T(8,128)(2,1)} %get-tuple-element.142.refs_0_, ...), custom_call_target="tpu_custom_call" | custom-call | flops 19549999104 | bytes 10000 | tf_op jit(solution)/shard_map/pallas_call | solution.py:116
  198.9 8.1 %shard_map.343.refs_5_ = bf16[1024,1024]{1,0:T(8,128)(2,1)} custom-call(s32[4]{0:T(128)} %fusion.11.refs_0_, bf16[1536,2048]{1,0:T(8,128)(2,1)} %get-tuple-element.114.refs_1_.refs_0_, bf16[1536,1024]{1,0:T(8,128)(2,1)} %get-tuple-element.147.refs_2_.refs_1_, f32[8,1024]{1,0:T(8,128)} %get-tuple-element.148.refs_3_.refs_22_), custom_call_target="tpu_custom_call" | custom-call | flops 9200000000 | bytes 10000 | tf_op jit(solution)/shard_map/pallas_call | solution.py:116
  211.2 8.1 %shard_map.345.refs_6_.refs_1_.refs_3_.refs_5_.refs_7_ = bf16[1024,1024]{1,0:T(8,128)(2,1)} custom-call(s32[4]{0:T(128)} %fusion.10.refs_0_, bf16[1536,2048]{1,0:T(8,128)(2,1)} %get-tuple-element.114.refs_1_.refs_0_, bf16[1536,1024]{1,0:T(8,128)(2,1)} %get-tuple-element.147.refs_2_.refs_1_, f32[8,1024]{1,0:T(8,128)} %get-tuple-element.151.refs_3_), custom_call_target="tpu_custom_call" | custom-call | flops 9200000000 | bytes 10000 | tf_op jit(solution)/shard_map/pallas_call | solution.py:116
  225.6 16.5 %shard_map.347.refs_6_.refs_5_ = bf16[4,1536,512]{2,1,0:T(8,128)(2,1)} custom-call(s32[4]{0:T(128)} %pad_add_fusion.refs_0_, bf16[1536,1024]{1,0:T(8,128)(2,1)} %get-tuple-element.147.refs_2_.refs_1_, bf16[2048,1024]{1,0:T(8,128)(2,1)} %refs_2_.17, f32[8,1024]{1,0:T(8,128)} %get-tuple-element.155.refs_3_), custom_call_target="tpu_custom_call" | custom-call | flops 19549999104 | bytes 10000 | tf_op jit(solution)/shard_map/pallas_call | solution.py:116
  246.3 15.7 %shard_map.349 = (f32[256,1024]{1,0:T(8,128)}, bf16[256,1024]{1,0:T(8,128)(2,1)}, bf16[256,1024]{1,0:T(8,128)(2,1)}, bf16[256,1024]{1,0:T(8,128)(2,1)}) custom-call(s32[4]{0:T(128)} %pad_add_fusion.1.refs_0_, bf16[1024,1024]{1,0:T(8,128)(2,1)} %shard_map.341.refs_11_.refs_1_.refs_3_.refs_5_.refs_7_, bf16[1024,1024]{1,0:T(8,128)(2,1)} %copy-done.20, ...), custom_call_target="tpu_custom_call" | custom-call | flops 4600000000 | bytes 10000 | tf_op jit(solution)/shard_map/pallas_call | solution.py:116
  267.7 4.1 shard_map.350
  273.9 57.6 %shard_map.351 = (bf16[1536,1024]{1,0:T(8,128)(2,1)}, bf16[1536,384]{1,0:T(8,128)(2,1)}, f32[12,8,128]{2,1,0:T(8,128)}, f32[128,1024]{1,0:T(8,128)}, f32[8,1280]...) custom-call(bf16[1536,1024]{1,0:T(8,128)(2,1)} %get-tuple-element.12, ...), custom_call_target="tpu_custom_call", output_to_operand_aliasing={{2}: (24, {})} | custom-call | flops 73600000000 | bytes 10000 | tf_op jit(solution)/shard_map/pallas_call | solution.py:116
  347.7 9.9 %shard_map.354 = (bf16[1024,512]{1,0:T(8,128)(2,1)}, bf16[1024,512]{1,0:T(8,128)(2,1)}, bf16[2048,128]{1,0:T(8,128)(2,1)}, bf16[2048,128]{1,0:T(8,128)(2,1)}, bf16[2048,128]{1,0:T(8,128)(2,1)}) custom-call(s32[4]{0:T(128)} %fusion.11.refs_0_, bf16[1536,2048]{1,0:T(8,128)(2,1)} %get-tuple-element.114.refs_1_.refs_0_, ...), custom_call_target="tpu_custom_call" | custom-call | flops 9200000000 | bytes 10000 | tf_op jit(solution)/shard_map/pallas_call | solution.py:116
  357.6 10.0 %shard_map.355 = (bf16[1024,512]{1,0:T(8,128)(2,1)}, bf16[1024,512]{1,0:T(8,128)(2,1)}, bf16[2048,128]{1,0:T(8,128)(2,1)}, bf16[2048,128]{1,0:T(8,128)(2,1)}, bf16[2048,128]{1,0:T(8,128)(2,1)}) custom-call(s32[4]{0:T(128)} %fusion.10.refs_0_, ...), custom_call_target="tpu_custom_call", output_to_operand_aliasing={{2}: (5, {}), {3}: (6, {}), {4}: (7, {})} | custom-call | flops 9200000000 | bytes 10000 | tf_op jit(solution)/shard_map/pallas_call | solution.py:116
  367.6 6.6 %shard_map.356.refs_3_ = bf16[1536,512]{1,0:T(8,128)(2,1)} custom-call(s32[1]{0:T(128)} %bitcast.14.refs_0_, bf16[1536,1024]{1,0:T(8,128)(2,1)} %get-tuple-element.172.refs_2_.refs_3_.refs_1_, bf16[2048,1024]{1,0:T(8,128)(2,1)} %refs_2_.21, bf16[1536,384]{1,0:T(8,128)(2,1)} %get-tuple-element.173.refs_4_.refs_3_, ...), custom_call_target="tpu_custom_call" | custom-call | flops 7474999808 | bytes 10000 | tf_op jit(solution)/shard_map/pallas_call | solution.py:116
  376.7 5.8 %shard_map.357 = (f32[2048,64]{1,0:T(8,128)}, bf16[2048,64]{1,0:T(8,128)(2,1)}) custom-call(s32[1]{0:T(128)} %bitcast.6.refs_0_, bf16[2048,128]{1,0:T(8,128)(2,1)} %get-tuple-element.183.refs_1_, bf16[2048,128]{1,0:T(8,128)(2,1)} %copy-done.36, bf16[1536,512]{1,0:T(8,128)(2,1)} %shard_map.356.refs_3_), custom_call_target="tpu_custom_call" | custom-call | flops 3449999872 | bytes 10000 | tf_op jit(solution)/shard_map/pallas_call | solution.py:116
  391.1 6.5 %shard_map.360.refs_9_ = bf16[1536,512]{1,0:T(8,128)(2,1)} custom-call(s32[1]{0:T(128)} %bitcast.13.refs_0_, bf16[1536,1024]{1,0:T(8,128)(2,1)} %get-tuple-element.172.refs_2_.refs_3_.refs_1_, bf16[2048,1024]{1,0:T(8,128)(2,1)} %refs_2_.21, bf16[1536,384]{1,0:T(8,128)(2,1)} %get-tuple-element.173.refs_4_.refs_3_, ...), custom_call_target="tpu_custom_call" | custom-call | flops 7474999808 | bytes 10000 | tf_op jit(solution)/shard_map/pallas_call | solution.py:116
  405.2 5.6 %shard_map.362.refs_7_ = bf16[2048,128]{1,0:T(8,128)(2,1)} custom-call(f32[2048,64]{1,0:T(8,128)} %get-tuple-element.185.refs_4_.refs_0_, bf16[2048,64]{1,0:T(8,128)(2,1)} %collective-permute-done.30.refs_1_, bf16[2048,128]{1,0:T(8,128)(2,1)} %get-tuple-element.188.refs_2_, f32[256,512]{1,0:T(8,128)} %get-tuple-element.191.refs_3_.refs_0_), custom_call_target="tpu_custom_call" | custom-call | flops 3449999872 | bytes 10000 | tf_op jit(solution)/shard_map/pallas_call | solution.py:116
  414.7 6.9 %shard_map.363.refs_7_ = bf16[1536,512]{1,0:T(8,128)(2,1)} custom-call(s32[1]{0:T(128)} %bitcast.15.refs_0_, bf16[1536,1024]{1,0:T(8,128)(2,1)} %get-tuple-element.172.refs_2_.refs_3_.refs_1_, bf16[2048,1024]{1,0:T(8,128)(2,1)} %refs_2_.21, bf16[1536,384]{1,0:T(8,128)(2,1)} %get-tuple-element.173.refs_4_.refs_3_, ...), custom_call_target="tpu_custom_call" | custom-call | flops 7474999808 | bytes 10000 | tf_op jit(solution)/shard_map/pallas_call | solution.py:116
  424.6 7.4 %shard_map.364.refs_4_ = f32[1536,512]{1,0:T(8,128)} custom-call(s32[1]{0:T(128)} %bitcast.12.refs_0_, bf16[1536,1024]{1,0:T(8,128)(2,1)} %get-tuple-element.172.refs_2_.refs_3_.refs_1_, bf16[2048,1024]{1,0:T(8,128)(2,1)} %refs_2_.21, bf16[1536,384]{1,0:T(8,128)(2,1)} %get-tuple-element.173.refs_4_.refs_3_, bf16[2048,384]{1,0:T(8,128)(2,1)} %get-tuple-element.174.refs_4_, ...), custom_call_target="tpu_custom_call" | custom-call | flops 7474999808 | bytes 10000 | tf_op jit(solution)/shard_map/pallas_call | solution.py:116
  455.2 17.9 %collective-permute-done.50 = f32[8,64]{1,0:T(8,128)S(1)} collective-permute-done((f32[8,64]{1,0:T(8,128)S(1)}, f32[8,64]{1,0:T(8,128)S(1)}, u32[]{:S(2)}, u32[]{:S(2)}) %collective-permute-start.50) | collective-permute-done | bytes 2080 | tf_op jit(solution)/shard_map/ppermute | solution.py:725
  475.0 5.5 %fusion.6 = (f32[512]{0:T(512)S(1)}, f32[1536,512]{1,0:T(8,128)}, bf16[1536,512]{1,0:T(8,128)(2,1)}) fusion(f32[1536,512]{1,0:T(8,128)S(1)} %copy-done.2, bf16[1536,512]{1,0:T(8,128)(2,1)} %collective-permute-done.32, f32[1536]{0:T(1024)S(1)} %copy-done.10, bf16[1536,2048]{1,0:T(8,128)(2,1)} %refs_0_.3, s32[]{:T(128)S(6)} %select_n.32, f32[1536]{0:T(1024)S(1)} %bitcast.49, ...), kind=kLoop, calls=%fused_computation.9 | loop fusion | flops 15728128 | bytes 17324036 | tf_op jit(solution)/shard_map/reduce_sum | solution.py:1297
  (289 shorter events, 154.7 us)
Async XLA Ops:
  4.6 27.8 %collective-permute-start.2 = (bf16[2080,64]{0,1:T(8,128)(2,1)S(1)}, bf16[2080,64]{0,1:T(8,128)(2,1)S(1)}, u32[]{:S(2)}, u32[]{:S(2)}) collective-permute-start(bf16[2080,64]{0,1:T(8,128)(2,1)S(1)} %copy.62), channel_id=1, source_target_pairs={{0,3},{1,2},{2,1},{3,0},{4,7},{5,6},{6,5},{7,4},{8,11},{9,10},{10,... | collective-permute-start | bytes 798728 | tf_op jit(solution)/shard_map/ppermute | solution.py:725
  7.0 26.4 %collective-permute-start.1 = (bf16[2080,64]{0,1:T(8,128)(2,1)S(1)}, bf16[2080,64]{0,1:T(8,128)(2,1)S(1)}, u32[]{:S(2)}, u32[]{:S(2)}) collective-permute-start(bf16[2080,64]{0,1:T(8,128)(2,1)S(1)} %copy.62), channel_id=1, source_target_pairs={{0,2},{1,3},{2,0},{3,1},{4,6},{5,7},{6,4},{7,5},{8,10},{9,11},{10,... | collective-permute-start | bytes 798728 | tf_op jit(solution)/shard_map/ppermute | solution.py:725
  7.7 26.9 %collective-permute-start = (bf16[2080,64]{0,1:T(8,128)(2,1)S(1)}, bf16[2080,64]{0,1:T(8,128)(2,1)S(1)}, u32[]{:S(2)}, u32[]{:S(2)}) collective-permute-start(bf16[2080,64]{0,1:T(8,128)(2,1)S(1)} %copy.62), channel_id=1, source_target_pairs={{0,1},{1,0},{2,3},{3,2},{4,5},{5,4},{6,7},{7,6},{8,9},{9,8},{10,11... | collective-permute-start | bytes 798728 | tf_op jit(solution)/shard_map/ppermute | solution.py:725
  9.8 25.8 %collective-permute-start.3 = (bf16[16,2048]{1,0:T(8,128)(2,1)}, bf16[16,2048]{1,0:T(8,128)(2,1)S(1)}, u32[]{:S(2)}, u32[]{:S(2)}) collective-permute-start(bf16[16,2048]{1,0:T(8,128)(2,1)} %get-tuple-element.115), channel_id=1, source_target_pairs={{0,4},{4,8},{8,12},{12,16},{16,20},{20,24},{24,28},{1,5},{5,9},{9,... | collective-permute-start | bytes 196616 | tf_op jit(solution)/shard_map/ppermute | solution.py:739
  135.4 19.4 %collective-permute-start.10 = (bf16[1536,512]{1,0:T(8,128)(2,1)}, bf16[1536,512]{1,0:T(8,128)(2,1)S(1)}, u32[]{:S(2)}, u32[]{:S(2)}) collective-permute-start(bf16[1536,512]{1,0:T(8,128)(2,1)} %shard_map.336.refs_4_), channel_id=1, source_target_pairs={{0,1},{1,0},{2,3},{3,2},{4,5},{5,4},{6,7},{7,6},{8,9},{9,8},{10,11... | collective-permute-start | bytes 4718600 | tf_op jit(solution)/shard_map/ppermute | solution.py:725
  142.4 19.7 %collective-permute-start.9 = (bf16[1536,512]{1,0:T(8,128)(2,1)}, bf16[1536,512]{1,0:T(8,128)(2,1)S(1)}, u32[]{:S(2)}, u32[]{:S(2)}) collective-permute-start(bf16[1536,512]{1,0:T(8,128)(2,1)} %shard_map.337.refs_4_), channel_id=1, source_target_pairs={{0,1},{1,0},{2,3},{3,2},{4,5},{5,4},{6,7},{7,6},{8,9},{9,8},{10,11... | collective-permute-start | bytes 4718600 | tf_op jit(solution)/shard_map/ppermute | solution.py:725
  154.2 90.7 %collective-permute-start.16 = (bf16[1024,1024]{1,0:T(8,128)(2,1)}, bf16[1024,1024]{1,0:T(8,128)(2,1)S(1)}, u32[]{:S(2)}, u32[]{:S(2)}) collective-permute-start(bf16[1024,1024]{1,0:T(8,128)(2,1)} %shard_map.338.refs_4_), channel_id=1, source_target_pairs={{0,4},{4,0},{8,12},{12,8},{16,20},{20,16},{24,28},{28,24},{1,5},{5... | collective-permute-start | bytes 6291464 | tf_op jit(solution)/shard_map/ppermute | solution.py:725
  161.4 110.4 %collective-permute-start.11 = (bf16[1536,512]{1,0:T(8,128)(2,1)}, bf16[1536,512]{1,0:T(8,128)(2,1)S(1)}, u32[]{:S(2)}, u32[]{:S(2)}) collective-permute-start(bf16[1536,512]{1,0:T(8,128)(2,1)} %shard_map.339.refs_4_), channel_id=1, source_target_pairs={{0,2},{1,3},{2,0},{3,1},{4,6},{5,7},{6,4},{7,5},{8,10},{9,11},{10,... | collective-permute-start | bytes 4718600 | tf_op jit(solution)/shard_map/ppermute | solution.py:725
  207.0 59.4 %collective-permute-start.15 = (bf16[1024,1024]{1,0:T(8,128)(2,1)}, bf16[1024,1024]{1,0:T(8,128)(2,1)S(1)}, u32[]{:S(2)}, u32[]{:S(2)}) collective-permute-start(bf16[1024,1024]{1,0:T(8,128)(2,1)} %shard_map.343.refs_5_), channel_id=1, source_target_pairs={{0,4},{4,0},{8,12},{12,8},{16,20},{20,16},{24,28},{28,24},{1,5},{5... | collective-permute-start | bytes 6291464 | tf_op jit(solution)/shard_map/ppermute | solution.py:725
  222.4 19.8 %collective-permute-start.14 = (bf16[128,1024]{1,0:T(8,128)(2,1)}, bf16[128,1024]{1,0:T(8,128)(2,1)S(1)}, u32[]{:S(2)}, u32[]{:S(2)}) collective-permute-start(bf16[128,1024]{1,0:T(8,128)(2,1)} %get-tuple-element.153), channel_id=1, source_target_pairs={{0,16},{4,20},{8,24},{12,28},{16,0},{20,4},{24,8},{28,12},{1,17},{... | collective-permute-start | bytes 786440 | tf_op jit(solution)/shard_map/ppermute | solution.py:725
  262.0 73.5 %collective-permute-start.19 = (bf16[256,1024]{1,0:T(8,128)(2,1)}, bf16[256,1024]{1,0:T(8,128)(2,1)S(1)}, u32[]{:S(2)}, u32[]{:S(2)}) collective-permute-start(bf16[256,1024]{1,0:T(8,128)(2,1)} %get-tuple-element.168), channel_id=1, source_target_pairs={{0,8},{4,12},{8,0},{12,4},{16,24},{20,28},{24,16},{28,20},{1,9},{5... | collective-permute-start | bytes 1572872 | tf_op jit(solution)/shard_map/ppermute | solution.py:725
  262.0 74.2 %collective-permute-start.20 = (bf16[256,1024]{1,0:T(8,128)(2,1)}, bf16[256,1024]{1,0:T(8,128)(2,1)S(1)}, u32[]{:S(2)}, u32[]{:S(2)}) collective-permute-start(bf16[256,1024]{1,0:T(8,128)(2,1)} %get-tuple-element.169), channel_id=1, source_target_pairs={{0,16},{4,20},{8,24},{12,28},{16,0},{20,4},{24,8},{28,12},{1,17},{... | collective-permute-start | bytes 1572872 | tf_op jit(solution)/shard_map/ppermute | solution.py:725
  263.6 73.6 %collective-permute-start.21 = (bf16[256,1024]{1,0:T(8,128)(2,1)}, bf16[256,1024]{1,0:T(8,128)(2,1)S(1)}, u32[]{:S(2)}, u32[]{:S(2)}) collective-permute-start(bf16[256,1024]{1,0:T(8,128)(2,1)} %get-tuple-element.170), channel_id=1, source_target_pairs={{0,24},{4,28},{8,16},{12,20},{16,8},{20,12},{24,0},{28,4},{1,25},{... | collective-permute-start | bytes 1572872 | tf_op jit(solution)/shard_map/ppermute | solution.py:725
  335.5 47.1 %collective-permute-start.24 = (bf16[256,1024]{1,0:T(8,128)(2,1)S(1)}, bf16[256,1024]{1,0:T(8,128)(2,1)}, u32[]{:S(2)}, u32[]{:S(2)}) collective-permute-start(bf16[256,1024]{1,0:T(8,128)(2,1)S(1)} %copy-done.32), channel_id=1, source_target_pairs={{0,8},{4,12},{8,0},{12,4},{16,24},{20,28},{24,16},{28,20},{1,9},{5... | collective-permute-start | bytes 1572872 | tf_op jit(solution)/shard_map/ppermute | solution.py:725
  336.2 46.6 %collective-permute-start.25 = (bf16[256,1024]{1,0:T(8,128)(2,1)S(1)}, bf16[256,1024]{1,0:T(8,128)(2,1)}, u32[]{:S(2)}, u32[]{:S(2)}) collective-permute-start(bf16[256,1024]{1,0:T(8,128)(2,1)S(1)} %copy-done.31), channel_id=1, source_target_pairs={{0,16},{4,20},{8,24},{12,28},{16,0},{20,4},{24,8},{28,12},{1,17},{... | collective-permute-start | bytes 1572872 | tf_op jit(solution)/shard_map/ppermute | solution.py:725
  337.2 45.9 %collective-permute-start.26 = (bf16[256,1024]{1,0:T(8,128)(2,1)S(1)}, bf16[256,1024]{1,0:T(8,128)(2,1)}, u32[]{:S(2)}, u32[]{:S(2)}) collective-permute-start(bf16[256,1024]{1,0:T(8,128)(2,1)S(1)} %copy-done.30), channel_id=1, source_target_pairs={{0,24},{4,28},{8,16},{12,20},{16,8},{20,12},{24,0},{28,4},{1,25},{... | collective-permute-start | bytes 1572872 | tf_op jit(solution)/shard_map/ppermute | solution.py:725
  345.3 41.1 %collective-permute-start.23 = (f32[8,1280]{1,0:T(8,128)}, f32[8,1280]{1,0:T(8,128)S(1)}, u32[]{:S(2)}, u32[]{:S(2)}) collective-permute-start(f32[8,1280]{1,0:T(8,128)} %get-tuple-element.176.refs_5_.refs_2_), channel_id=1, source_target_pairs={{0,8},{4,12},{8,0},{12,4},{16,24},{20,28},{24,16},{28,20},{1,9},{5... | collective-permute-start | bytes 122888 | tf_op jit(solution)/shard_map/ppermute | solution.py:725
  374.3 26.4 %collective-permute-start.31 = (bf16[1024,512]{1,0:T(8,128)(2,1)S(1)}, bf16[1024,512]{1,0:T(8,128)(2,1)S(1)}, u32[]{:S(2)}, u32[]{:S(2)}) collective-permute-start(bf16[1024,512]{1,0:T(8,128)(2,1)S(1)} %copy-done.28), channel_id=1, source_target_pairs={{0,4},{4,0},{8,12},{12,8},{16,20},{20,16},{24,28},{28,24},{1,5},{5... | collective-permute-start | bytes 3145736 | tf_op jit(solution)/shard_map/ppermute | solution.py:725
  382.5 30.0 %collective-permute-start.29 = (bf16[1536,512]{1,0:T(8,128)(2,1)S(1)}, bf16[1536,512]{1,0:T(8,128)(2,1)S(1)}, u32[]{:S(2)}, u32[]{:S(2)}) collective-permute-start(bf16[1536,512]{1,0:T(8,128)(2,1)S(1)} %copy-done.21), channel_id=1, source_target_pairs={{0,1},{1,0},{2,3},{3,2},{4,5},{5,4},{6,7},{7,6},{8,9},{9,8},{10,11... | collective-permute-start | bytes 4718600 | tf_op jit(solution)/shard_map/ppermute | solution.py:725
  383.1 54.6 %collective-permute-start.38 = (bf16[1024,512]{1,0:T(8,128)(2,1)S(1)}, bf16[1024,512]{1,0:T(8,128)(2,1)S(1)}, u32[]{:S(2)}, u32[]{:S(2)}) collective-permute-start(bf16[1024,512]{1,0:T(8,128)(2,1)S(1)} %copy-done.26), channel_id=1, source_target_pairs={{0,4},{4,0},{8,12},{12,8},{16,20},{20,16},{24,28},{28,24},{1,5},{5... | collective-permute-start | bytes 3145736 | tf_op jit(solution)/shard_map/ppermute | solution.py:725
  389.1 42.9 %collective-permute-start.33 = (f32[12,128]{1,0:T(8,128)}, f32[12,128]{1,0:T(8,128)S(1)}, u32[]{:S(2)}, u32[]{:S(2)}) collective-permute-start(f32[12,128]{1,0:T(8,128)} %get-tuple-element.186.refs_6_.refs_0_), channel_id=1, source_target_pairs={{0,2},{1,3},{2,0},{3,1},{4,6},{5,7},{6,4},{7,5},{8,10},{9,11},{10,... | collective-permute-start | bytes 18440 | tf_op jit(solution)/shard_map/ppermute | solution.py:725
  389.7 15.3 %collective-permute-start.30 = (bf16[2048,64]{1,0:T(8,128)(2,1)}, bf16[2048,64]{1,0:T(8,128)(2,1)}, u32[]{:S(2)}, u32[]{:S(2)}) collective-permute-start(bf16[2048,64]{1,0:T(8,128)(2,1)} %get-tuple-element.187), channel_id=1, source_target_pairs={{0,2},{1,3},{2,0},{3,1},{4,6},{5,7},{6,4},{7,5},{8,10},{9,11},{10,... | collective-permute-start | bytes 786440 | tf_op jit(solution)/shard_map/ppermute | solution.py:725
  400.7 20.9 %collective-permute-start.28 = (bf16[1536,512]{1,0:T(8,128)(2,1)}, bf16[1536,512]{1,0:T(8,128)(2,1)S(1)}, u32[]{:S(2)}, u32[]{:S(2)}) collective-permute-start(bf16[1536,512]{1,0:T(8,128)(2,1)} %shard_map.360.refs_9_), channel_id=1, source_target_pairs={{0,1},{1,0},{2,3},{3,2},{4,5},{5,4},{6,7},{7,6},{8,9},{9,8},{10,11... | collective-permute-start | bytes 4718600 | tf_op jit(solution)/shard_map/ppermute | solution.py:725
  405.1 28.5 %collective-permute-start.34 = (f32[8,1280]{1,0:T(8,128)S(1)}, f32[8,1280]{1,0:T(8,128)S(1)}, u32[]{:S(2)}, u32[]{:S(2)}) collective-permute-start(f32[8,1280]{1,0:T(8,128)S(1)} %copy-done.58), channel_id=1, source_target_pairs={{0,16},{4,20},{8,24},{12,28},{16,0},{20,4},{24,8},{28,12},{1,17},{... | collective-permute-start | bytes 122888 | tf_op jit(solution)/shard_map/ppermute | solution.py:725
  412.6 35.1 %collective-permute-start.42 = (bf16[256,512]{1,0:T(8,128)(2,1)S(1)}, bf16[256,512]{1,0:T(8,128)(2,1)S(1)}, u32[]{:S(2)}, u32[]{:S(2)}) collective-permute-start(bf16[256,512]{1,0:T(8,128)(2,1)S(1)} %copy-done.43), channel_id=1, source_target_pairs={{0,8},{4,12},{8,0},{12,4},{16,24},{20,28},{24,16},{28,20},{1,9},{5... | collective-permute-start | bytes 786440 | tf_op jit(solution)/shard_map/ppermute | solution.py:725
  421.6 26.0 %collective-permute-start.43 = (bf16[256,512]{1,0:T(8,128)(2,1)S(1)}, bf16[256,512]{1,0:T(8,128)(2,1)S(1)}, u32[]{:S(2)}, u32[]{:S(2)}) collective-permute-start(bf16[256,512]{1,0:T(8,128)(2,1)S(1)} %copy-done.42), channel_id=1, source_target_pairs={{0,16},{4,20},{8,24},{12,28},{16,0},{20,4},{24,8},{28,12},{1,17},{... | collective-permute-start | bytes 786440 | tf_op jit(solution)/shard_map/ppermute | solution.py:725
  432.0 15.7 %collective-permute-start.44 = (bf16[256,512]{1,0:T(8,128)(2,1)S(1)}, bf16[256,512]{1,0:T(8,128)(2,1)S(1)}, u32[]{:S(2)}, u32[]{:S(2)}) collective-permute-start(bf16[256,512]{1,0:T(8,128)(2,1)S(1)} %copy-done.41), channel_id=1, source_target_pairs={{0,24},{4,28},{8,16},{12,20},{16,8},{20,12},{24,0},{28,4},{1,25},{... | collective-permute-start | bytes 786440 | tf_op jit(solution)/shard_map/ppermute | solution.py:725
  437.8 37.1 %collective-permute-start.32 = (bf16[1536,512]{1,0:T(8,128)(2,1)}, bf16[1536,512]{1,0:T(8,128)(2,1)}, u32[]{:S(2)}, u32[]{:S(2)}) collective-permute-start(bf16[1536,512]{1,0:T(8,128)(2,1)} %shard_map.363.refs_7_), channel_id=1, source_target_pairs={{0,2},{1,3},{2,0},{3,1},{4,6},{5,7},{6,4},{7,5},{8,10},{9,11},{10,... | collective-permute-start | bytes 4718600 | tf_op jit(solution)/shard_map/ppermute | solution.py:725
  446.6 26.6 %collective-permute-start.50 = (f32[8,64]{1,0:T(8,128)S(1)}, f32[8,64]{1,0:T(8,128)S(1)}, u32[]{:S(2)}, u32[]{:S(2)}) collective-permute-start(f32[8,64]{1,0:T(8,128)S(1)} %slice.85), channel_id=1, source_target_pairs={{0,2},{1,3},{2,0},{3,1},{4,6},{5,7},{6,4},{7,5},{8,10},{9,11},{10,... | collective-permute-start | bytes 6152 | tf_op jit(solution)/shard_map/ppermute | solution.py:725
  452.0 39.8 %collective-permute-start.46 = (bf16[256,128]{1,0:T(8,128)(2,1)}, bf16[256,128]{1,0:T(8,128)(2,1)}, u32[]{:S(2)}, u32[]{:S(2)}) collective-permute-start(bf16[256,128]{1,0:T(8,128)(2,1)} %get-tuple-element.204), channel_id=1, source_target_pairs={{0,8},{4,12},{8,0},{12,4},{16,24},{20,28},{24,16},{28,20},{1,9},{5... | collective-permute-start | bytes 196616 | tf_op jit(solution)/shard_map/ppermute | solution.py:725
  452.1 32.0 %collective-permute-start.39 = (bf16[256,512]{1,0:T(8,128)(2,1)}, bf16[256,512]{1,0:T(8,128)(2,1)S(1)}, u32[]{:S(2)}, u32[]{:S(2)}) collective-permute-start(bf16[256,512]{1,0:T(8,128)(2,1)} %get-tuple-element.197), channel_id=1, source_target_pairs={{0,8},{4,12},{8,0},{12,4},{16,24},{20,28},{24,16},{28,20},{1,9},{5... | collective-permute-start | bytes 786440 | tf_op jit(solution)/shard_map/ppermute | solution.py:725
  454.0 32.2 %collective-permute-start.40 = (bf16[256,512]{1,0:T(8,128)(2,1)}, bf16[256,512]{1,0:T(8,128)(2,1)S(1)}, u32[]{:S(2)}, u32[]{:S(2)}) collective-permute-start(bf16[256,512]{1,0:T(8,128)(2,1)} %get-tuple-element.198), channel_id=1, source_target_pairs={{0,16},{4,20},{8,24},{12,28},{16,0},{20,4},{24,8},{28,12},{1,17},{... | collective-permute-start | bytes 786440 | tf_op jit(solution)/shard_map/ppermute | solution.py:725
  (82 other events, 710.3 us)
